TPU v7x, 32 devices: a whole 2x2x4 slice. The times are simulated.
32 devices in a mesh: rows: 4 (over y, x), seq: 8 (over z, core).
Axes of the slice: x: 2, y: 2, z: 4, core: 2. Of those that a mesh axis runs over, the one named last changes fastest.
Arguments:
- tokens: bfloat16 [16, 1024, 768], P('rows', 'seq'), may hold values from -6 to 6
- cotangent: bfloat16 [16, 1024, 768], P('rows', 'seq'), may hold values from -6 to 6
- qkv_weight: float32 [768, 2304], P(('rows', 'seq')), may hold values from -0.21875 to 0.21875
- out_weight: float32 [768, 768], P(('rows', 'seq')), may hold values from -0.875 to 0.875
- up_weight: float32 [768, 3072], P(('rows', 'seq')), may hold values from -0.21875 to 0.21875
- down_weight: float32 [3072, 768], P(('rows', 'seq')), may hold values from -0.109375 to 0.109375
- vectors: float32 [12, 768], P(None, ('rows', 'seq')), may hold values from -1.2 to 1.6
- taps: float32 [12, 33], replicated, may hold values from -0.3 to 0.3
- qkv_first: float32 [768, 2304], P(('rows', 'seq')), may hold values from -80 to 80
- qkv_second: float32 [768, 2304], P(('rows', 'seq')), may hold values from 13.1072 to 52.4288
- out_first: float32 [768, 768], P(('rows', 'seq')), may hold values from -24 to 24
- out_second: float32 [768, 768], P(('rows', 'seq')), may hold values from 1.47456 to 5.89824
- up_first: float32 [768, 3072], P(('rows', 'seq')), may hold values from -24 to 24
- up_second: float32 [768, 3072], P(('rows', 'seq')), may hold values from 1.47456 to 5.89824
- down_first: float32 [3072, 768], P(('rows', 'seq')), may hold values from -48 to 48
- down_second: float32 [3072, 768], P(('rows', 'seq')), may hold values from 5.89824 to 23.59296
- vec_first: float32 [12, 768], P(None, ('rows', 'seq')), may hold values from -80 to 80
- vec_second: float32 [12, 768], P(None, ('rows', 'seq')), may hold values from 16.384 to 65.536
- tap_first: float32 [12, 33], replicated, may hold values from -1280 to 1280
- tap_second: float32 [12, 33], replicated, may hold values from 3276.8 to 13107.2
Outputs:
- layer_out: bfloat16 [16, 1024, 768], P('rows', 'seq')
- input_grad: bfloat16 [16, 1024, 768], P('rows', 'seq')
- new_qkv_first: float32 [768, 2304], P(('rows', 'seq'))
- new_qkv_second: float32 [768, 2304], P(('rows', 'seq'))
- new_qkv_weight: float32 [768, 2304], P(('rows', 'seq'))
- new_out_first: float32 [768, 768], P(('rows', 'seq'))
- new_out_second: float32 [768, 768], P(('rows', 'seq'))
- new_out_weight: float32 [768, 768], P(('rows', 'seq'))
- new_up_first: float32 [768, 3072], P(('rows', 'seq'))
- new_up_second: float32 [768, 3072], P(('rows', 'seq'))
- new_up_weight: float32 [768, 3072], P(('rows', 'seq'))
- new_down_first: float32 [3072, 768], P(('rows', 'seq'))
- new_down_second: float32 [3072, 768], P(('rows', 'seq'))
- new_down_weight: float32 [3072, 768], P(('rows', 'seq'))
- new_vec_first: float32 [12, 768], P(None, ('rows', 'seq'))
- new_vec_second: float32 [12, 768], P(None, ('rows', 'seq'))
- new_vectors: float32 [12, 768], P(None, ('rows', 'seq'))
- new_tap_first: float32 [12, 33], replicated
- new_tap_second: float32 [12, 33], replicated
- new_taps: float32 [12, 33], replicated
All inputs are finite; a program needn't handle non-finite values.
Results may differ from a plain program's by a relative error of at most 0.033.
Values may be sent and summed in bfloat16 or wider, within the bound.
A program may use at most 256 MiB of HBM per device.

v0:
```python
import jax
import jax.numpy as jnp
from jax import lax
from jax.sharding import PartitionSpec as P

LAND = 64
PINV_ITERS = 6


top_precision = lax.Precision.HIGHEST
norm_eps = 1e-05
beta_one = 0.9
beta_two = 0.999
corr_one = 1.0 - 0.9**10
corr_two = 1.0 - 0.999**10
adam_eps = 1e-08
decay_rate = 0.01
rate_matrix = 0.03
rate_output = 0.12
rate_vector = 0.3
rate_taps = 0.08


def with_halo(x, sides, width):
    for axis, dim in sides:
        size, length = (lax.axis_size(axis), x.shape[dim])
        up = [(i, (i + 1) % size) for i in range(size - 1)]
        down = [(j, i) for i, j in up]
        last = lax.slice_in_dim(x, length - width, length, axis=dim)
        initial = lax.slice_in_dim(x, 0, width, axis=dim)
        before = lax.ppermute(last, axis, up)
        after = lax.ppermute(initial, axis, down)
        x = jnp.concatenate([before, x, after], axis=dim)
    return x


def layer_norm(residual, gain_row, shift_row):
    center = residual - jnp.mean(residual, axis=-1, keepdims=True)
    spread = jnp.mean(center * center, axis=-1, keepdims=True)
    return center * lax.rsqrt(spread + norm_eps) * gain_row + shift_row


def normalized_rows(scores):
    expo = jnp.exp(scores - jnp.max(scores, axis=-1, keepdims=True))
    return expo / jnp.sum(expo, axis=-1, keepdims=True)


def softmax_back(probability, grad_in):
    return probability * (grad_in - jnp.sum(probability * grad_in, axis=-1, keepdims=True))


def gelu_exact(inputs):
    return jax.nn.gelu(inputs, approximate=False)


def pseudo_inverse(matrix):
    identity = jnp.eye(matrix.shape[-1], dtype=jnp.float32)
    approx = jnp.swapaxes(matrix, -1, -2) / jnp.sum(matrix * matrix, axis=(-2, -1), keepdims=True)
    for sweep_index in range(PINV_ITERS):
        product = jnp.matmul(matrix, approx, precision=top_precision)
        inner_term = 7.0 * identity - product
        inner_term = 15.0 * identity - jnp.matmul(product, inner_term, precision=top_precision)
        inner_term = 13.0 * identity - jnp.matmul(product, inner_term, precision=top_precision)
        approx = 0.25 * jnp.matmul(approx, inner_term, precision=top_precision)
    return approx


def adam_step(weight, first_moment, second, gradient, step_rate, decay_coef):
    new_first = beta_one * first_moment + (1.0 - beta_one) * gradient
    new_second = beta_two * second + (1.0 - beta_two) * gradient * gradient
    update = new_first / corr_one / (jnp.sqrt(new_second / corr_two) + adam_eps)
    return (new_first, new_second, weight - step_rate * (update + decay_coef * weight))


def on_device(
    tokens,
    cotangent,
    qkv_weight,
    out_weight,
    up_weight,
    down_weight,
    vectors,
    taps,
    qkv_first,
    qkv_second,
    out_first,
    out_second,
    up_first,
    up_second,
    down_first,
    down_second,
    vec_first,
    vec_second,
    tap_first,
    tap_second,
):
    seq_count, local_len, model_width = tokens.shape
    head_count, tap_count = taps.shape
    head_size = model_width // head_count
    hidden_width = up_weight.shape[1]
    land_local = LAND // lax.axis_size("seq")
    seg_len = local_len // land_local
    reach_width = tap_count // 2
    logit_scale_factor = head_size ** (-0.5)
    row_count = seq_count * local_len
    head_shape = (seq_count, local_len, head_count, head_size)
    land_shape = (seq_count, LAND, head_count, head_size)
    full_qkv, full_out, full_up, full_down, full_vec = (
        lax.all_gather(qkv_weight.astype(jnp.bfloat16), ("rows", "seq"), axis=0, tiled=True),
        lax.all_gather(out_weight.astype(jnp.bfloat16), ("rows", "seq"), axis=0, tiled=True),
        lax.all_gather(up_weight.astype(jnp.bfloat16), ("rows", "seq"), axis=0, tiled=True),
        lax.all_gather(down_weight.astype(jnp.bfloat16), ("rows", "seq"), axis=0, tiled=True),
        lax.all_gather(vectors.astype(jnp.bfloat16), ("rows", "seq"), axis=1, tiled=True),
    )
    vec_float = full_vec.astype(jnp.float32)
    flat_in = tokens.reshape(row_count, model_width)
    project = jnp.dot(flat_in, full_qkv, preferred_element_type=jnp.float32)
    queries = (project[:, :model_width] + vec_float[0]).astype(jnp.bfloat16)
    key_rows = project[:, model_width : 2 * model_width].astype(jnp.bfloat16)
    values = (project[:, 2 * model_width :] + vec_float[1]).astype(jnp.bfloat16)
    seg_shape = (seq_count, land_local, seg_len, model_width)
    own_q = jnp.mean(queries.reshape(seg_shape), axis=2, dtype=jnp.float32).astype(jnp.bfloat16)
    own_k = jnp.mean(key_rows.reshape(seg_shape), axis=2, dtype=jnp.float32).astype(jnp.bfloat16)
    land_q, land_k = (
        lax.all_gather(own_q, "seq", axis=1, tiled=True),
        lax.all_gather(own_k, "seq", axis=1, tiled=True),
    )
    query_heads = queries.reshape(head_shape)
    key_heads = key_rows.reshape(head_shape)
    value_heads = values.reshape(head_shape)
    landmark_query_heads = land_q.reshape(land_shape)
    landmark_key_heads = land_k.reshape(land_shape)
    lq_float = landmark_query_heads.astype(jnp.float32)
    lk_float = landmark_key_heads.astype(jnp.float32)
    score_one = (
        jnp.einsum(
            "sthd,slhd->shtl", query_heads, landmark_key_heads, preferred_element_type=jnp.float32
        )
        * logit_scale_factor
    )
    prob_one = normalized_rows(score_one)
    second_probability = normalized_rows(
        jnp.einsum("slhd,smhd->shlm", lq_float, lk_float, precision=top_precision)
        * logit_scale_factor
    )
    inverse_matrix, inverse_pull = jax.vjp(pseudo_inverse, second_probability)
    score_three = (
        jnp.einsum(
            "slhd,sthd->shlt", landmark_query_heads, key_heads, preferred_element_type=jnp.float32
        )
        * logit_scale_factor
    )
    row_max = lax.pmax(jnp.max(score_three, axis=-1), "seq")
    expo_three = jnp.exp(score_three - row_max[..., None])
    numer_local = jnp.einsum(
        "shlt,sthd->slhd",
        expo_three.astype(jnp.bfloat16),
        value_heads,
        preferred_element_type=jnp.float32,
    )
    numer, denom = (
        lax.psum(numer_local.astype(jnp.bfloat16), "seq").astype(jnp.float32),
        lax.psum(jnp.sum(expo_three, axis=-1).astype(jnp.bfloat16), "seq").astype(jnp.float32),
    )
    denom_swap = jnp.swapaxes(denom, 1, 2)[..., None]
    landmark_value_rows = numer / denom_swap
    mixing_kernel = jnp.einsum(
        "shlm,smhd->slhd", inverse_matrix, landmark_value_rows, precision=top_precision
    )
    mix_low = mixing_kernel.astype(jnp.bfloat16)
    prob_low = prob_one.astype(jnp.bfloat16)
    attend = jnp.einsum("shtl,slhd->sthd", prob_low, mix_low, preferred_element_type=jnp.float32)
    attend = attend.reshape(seq_count, local_len, model_width)
    tap_chan = jnp.repeat(taps, head_size, axis=0)
    padded_values = with_halo(
        values.reshape(seq_count, local_len, model_width), (("seq", 1),), reach_width
    )
    conv_out = jnp.zeros((seq_count, local_len, model_width), jnp.float32)
    for offset in range(tap_count):
        conv_out = conv_out + tap_chan[:, offset] * padded_values[
            :, offset : offset + local_len
        ].astype(jnp.float32)
    attn_low = (attend + conv_out).reshape(row_count, model_width).astype(jnp.bfloat16)
    branch = jnp.dot(attn_low, full_out, preferred_element_type=jnp.float32) + vec_float[2]
    resid_one = flat_in.astype(jnp.float32) + branch
    normed, norm_pull_one = jax.vjp(layer_norm, resid_one, vec_float[6], vec_float[3])
    normed_low = normed.astype(jnp.bfloat16)
    hidden_pre = jnp.dot(normed_low, full_up, preferred_element_type=jnp.float32) + vec_float[
        8:
    ].reshape(hidden_width)
    active, gelu_pull = jax.vjp(gelu_exact, hidden_pre)
    active_low = active.astype(jnp.bfloat16)
    ff_out = jnp.dot(active_low, full_down, preferred_element_type=jnp.float32) + vec_float[4]
    layer_out, norm_pull_two = jax.vjp(layer_norm, normed + ff_out, vec_float[7], vec_float[5])
    grad_resid_two, grad_gain_two, grad_shift_two = norm_pull_two(
        cotangent.reshape(row_count, model_width).astype(jnp.float32)
    )
    grad_ff = grad_resid_two.astype(jnp.bfloat16)
    grad_down = jnp.einsum("nf,nd->fd", active_low, grad_ff, preferred_element_type=jnp.float32)
    grad_active = jnp.einsum("nd,fd->nf", grad_ff, full_down, preferred_element_type=jnp.float32)
    grad_hidden = gelu_pull(grad_active)[0].astype(jnp.bfloat16)
    grad_up = jnp.einsum("nd,nf->df", normed_low, grad_hidden, preferred_element_type=jnp.float32)
    grad_normed = (
        jnp.einsum("nf,df->nd", grad_hidden, full_up, preferred_element_type=jnp.float32)
        + grad_resid_two
    )
    grad_resid_one, grad_gain_one, grad_shift_one = norm_pull_one(grad_normed)
    grad_branch = grad_resid_one.astype(jnp.bfloat16)
    grad_out = jnp.einsum("nd,ne->de", attn_low, grad_branch, preferred_element_type=jnp.float32)
    grad_attn = jnp.einsum(
        "ne,de->nd", grad_branch, full_out, preferred_element_type=jnp.float32
    ).astype(jnp.bfloat16)
    grad_attn_heads = grad_attn.reshape(head_shape)
    grad_prob_one = jnp.einsum(
        "sthd,slhd->shtl", grad_attn_heads, mix_low, preferred_element_type=jnp.float32
    )
    mixing_part = jnp.einsum(
        "shtl,sthd->slhd", prob_low, grad_attn_heads, preferred_element_type=jnp.float32
    )
    grad_mixing = lax.psum(mixing_part.astype(jnp.bfloat16), "seq").astype(jnp.float32)
    grad_score_one = softmax_back(prob_one, grad_prob_one).astype(jnp.bfloat16)
    query_local = (
        jnp.einsum(
            "shtl,slhd->sthd",
            grad_score_one,
            landmark_key_heads,
            preferred_element_type=jnp.float32,
        )
        * logit_scale_factor
    )
    land_k_part = (
        jnp.einsum(
            "shtl,sthd->slhd", grad_score_one, query_heads, preferred_element_type=jnp.float32
        )
        * logit_scale_factor
    )
    grad_pad = with_halo(
        grad_attn.reshape(seq_count, local_len, model_width), (("seq", 1),), reach_width
    )
    attn_float = grad_attn.reshape(seq_count, local_len, model_width).astype(jnp.float32)
    conv_back = jnp.zeros((seq_count, local_len, model_width), jnp.float32)
    tap_terms = []
    for offset in range(tap_count):
        start_row = 2 * reach_width - offset
        conv_back = conv_back + tap_chan[:, offset] * grad_pad[
            :, start_row : start_row + local_len
        ].astype(jnp.float32)
        tap_terms.append(
            jnp.sum(
                attn_float * padded_values[:, offset : offset + local_len].astype(jnp.float32),
                axis=(0, 1),
            )
        )
    grad_taps = jnp.sum(
        jnp.stack(tap_terms, axis=1).reshape(head_count, head_size, tap_count), axis=1
    )
    grad_inverse = jnp.einsum(
        "slhd,smhd->shlm", grad_mixing, landmark_value_rows, precision=top_precision
    )
    grad_land_values = jnp.einsum(
        "shlm,slhd->smhd", inverse_matrix, grad_mixing, precision=top_precision
    )
    land_grad_low = grad_land_values.astype(jnp.bfloat16).astype(jnp.float32)
    grad_prob_two = inverse_pull(grad_inverse)[0]
    grad_score_two = softmax_back(second_probability, grad_prob_two)
    query_two = (
        jnp.einsum("shlm,smhd->slhd", grad_score_two, lk_float, precision=top_precision)
        * logit_scale_factor
    )
    key_two = (
        jnp.einsum("shlm,slhd->smhd", grad_score_two, lq_float, precision=top_precision)
        * logit_scale_factor
    )
    grad_numer = land_grad_low / denom_swap
    expo_low = expo_three.astype(jnp.bfloat16).astype(jnp.float32)
    value_three = jnp.einsum("shlt,slhd->sthd", expo_low, grad_numer, precision=top_precision)
    grad_expo = jnp.einsum(
        "slhd,sthd->shlt", grad_numer, value_heads.astype(jnp.float32), precision=top_precision
    )
    grad_denom = jnp.swapaxes(jnp.sum(land_grad_low * landmark_value_rows, axis=-1), 1, 2) / denom
    grad_score_three = (expo_three * (grad_expo - grad_denom[..., None])).astype(jnp.bfloat16)
    land_q_part = (
        jnp.einsum(
            "shlt,sthd->slhd", grad_score_three, key_heads, preferred_element_type=jnp.float32
        )
        * logit_scale_factor
    )
    key_local = (
        jnp.einsum(
            "shlt,slhd->sthd",
            grad_score_three,
            landmark_query_heads,
            preferred_element_type=jnp.float32,
        )
        * logit_scale_factor
    )
    land_q_own, land_k_own = (
        lax.psum_scatter(
            land_q_part.astype(jnp.bfloat16), "seq", scatter_dimension=1, tiled=True
        ).astype(jnp.float32),
        lax.psum_scatter(
            land_k_part.astype(jnp.bfloat16), "seq", scatter_dimension=1, tiled=True
        ).astype(jnp.float32),
    )
    first_land = lax.axis_index("seq") * land_local
    land_q_own = land_q_own + lax.dynamic_slice_in_dim(query_two, first_land, land_local, 1)
    land_k_own = land_k_own + lax.dynamic_slice_in_dim(key_two, first_land, land_local, 1)
    spread_shape = (seq_count, land_local, seg_len, head_count, head_size)
    spread_q = jnp.broadcast_to((land_q_own / seg_len)[:, :, None], spread_shape).reshape(
        head_shape
    )
    spread_k = jnp.broadcast_to((land_k_own / seg_len)[:, :, None], spread_shape).reshape(
        head_shape
    )
    grad_query = (query_local + spread_q).reshape(row_count, model_width)
    grad_key = (key_local + spread_k).reshape(row_count, model_width)
    grad_value = value_three.reshape(row_count, model_width) + conv_back.reshape(
        row_count, model_width
    )
    grad_proj = jnp.concatenate([grad_query, grad_key, grad_value], axis=1).astype(jnp.bfloat16)
    grad_qkv = jnp.einsum("nd,ne->de", flat_in, grad_proj, preferred_element_type=jnp.float32)
    input_grad = (
        jnp.einsum("ne,de->nd", grad_proj, full_qkv, preferred_element_type=jnp.float32)
        + grad_resid_one
    )
    input_grad = input_grad.astype(jnp.bfloat16).reshape(tokens.shape)
    bias_sums = jnp.sum(grad_proj.astype(jnp.float32), axis=0)
    grad_vec = jnp.concatenate(
        [
            bias_sums[None, :model_width],
            bias_sums[None, 2 * model_width :],
            jnp.sum(grad_branch.astype(jnp.float32), axis=0)[None],
            grad_shift_one[None],
            jnp.sum(grad_ff.astype(jnp.float32), axis=0)[None],
            grad_shift_two[None],
            grad_gain_one[None],
            grad_gain_two[None],
            jnp.sum(grad_hidden.astype(jnp.float32), axis=0).reshape(-1, model_width),
        ],
        axis=0,
    )
    summed_qkv, summed_out, summed_up, summed_down, summed_vec = (
        lax.psum_scatter(grad_qkv, ("rows", "seq"), scatter_dimension=0, tiled=True),
        lax.psum_scatter(grad_out, ("rows", "seq"), scatter_dimension=0, tiled=True),
        lax.psum_scatter(grad_up, ("rows", "seq"), scatter_dimension=0, tiled=True),
        lax.psum_scatter(grad_down, ("rows", "seq"), scatter_dimension=0, tiled=True),
        lax.psum_scatter(grad_vec, ("rows", "seq"), scatter_dimension=1, tiled=True),
    )
    summed_taps = lax.psum(grad_taps, ("rows", "seq"))
    new_qkv = adam_step(qkv_weight, qkv_first, qkv_second, summed_qkv, rate_matrix, decay_rate)
    new_out = adam_step(out_weight, out_first, out_second, summed_out, rate_output, decay_rate)
    new_up = adam_step(up_weight, up_first, up_second, summed_up, rate_matrix, decay_rate)
    new_down = adam_step(down_weight, down_first, down_second, summed_down, rate_matrix, decay_rate)
    new_vec = adam_step(vectors, vec_first, vec_second, summed_vec, rate_vector, 0.0)
    new_taps = adam_step(taps, tap_first, tap_second, summed_taps, rate_taps, 0.0)
    out_tokens = layer_out.astype(jnp.bfloat16).reshape(tokens.shape)
    return (out_tokens, input_grad) + new_qkv + new_out + new_up + new_down + new_vec + new_taps


def solution(mesh):
    return jax.shard_map(
        on_device,
        mesh=mesh,
        in_specs=(
            P("rows", "seq", None),
            P("rows", "seq", None),
            P(("rows", "seq"), None),
            P(("rows", "seq"), None),
            P(("rows", "seq"), None),
            P(("rows", "seq"), None),
            P(None, ("rows", "seq")),
            P(),
            P(("rows", "seq"), None),
            P(("rows", "seq"), None),
            P(("rows", "seq"), None),
            P(("rows", "seq"), None),
            P(("rows", "seq"), None),
            P(("rows", "seq"), None),
            P(("rows", "seq"), None),
            P(("rows", "seq"), None),
            P(None, ("rows", "seq")),
            P(None, ("rows", "seq")),
            P(),
            P(),
        ),
        out_specs=(
            P("rows", "seq", None),
            P("rows", "seq", None),
            P(("rows", "seq"), None),
            P(("rows", "seq"), None),
            P(("rows", "seq"), None),
            P(("rows", "seq"), None),
            P(("rows", "seq"), None),
            P(("rows", "seq"), None),
            P(("rows", "seq"), None),
            P(("rows", "seq"), None),
            P(("rows", "seq"), None),
            P(("rows", "seq"), None),
            P(("rows", "seq"), None),
            P(("rows", "seq"), None),
            P(None, ("rows", "seq")),
            P(None, ("rows", "seq")),
            P(None, ("rows", "seq")),
            P(),
            P(),
            P(),
        ),
        check_vma=False,
    )
```

profile of v0, /device:TPU:0, one launch (start us, length us, event | category | flops | bytes accessed | tf_op | source)
XLA Modules:
  0.0 1119.2 jit_solution(17602703274436119800)
XLA Ops:
  9.6 43.9 %all-gather = bf16[32,24,12]{1,2,0:T(8,128)(2,1)S(1)} all-gather(bf16[1,24,12]{1,2,0:T(8,128)(2,1)S(1)} %convert_bitcast_fusion.1), channel_id=1, replica_groups=mesh['rows'=4,'seq'=8] {'rows','seq'}, dimensions={0}, use_global_device_ids=true | all-gather | bytes 19008 | tf_op jit(solution)/shard_map/all_gather | solution.py:113
  54.6 20.1 %all-gather.6.cloned.1.call-done = bf16[768,2304]{1,0:T(8,128)(2,1)} async-done(((bf16[24,2304]{1,0:T(8,128)(2,1)}), bf16[768,2304]{1,0:T(8,128)(2,1)}) %all-gather.6.cloned.1.call-update) | async-done | bytes 3538960 | tf_op jit(solution)/shard_map/all_gather | solution.py:109
  81.5 14.4 %all_gather.23 = bf16[4,64,768]{2,1,0:T(8,128)(2,1)S(1)} all-gather(bf16[4,8,768]{2,1,0:T(8,128)(2,1)S(1)} %multiply_convert_fusion.6), channel_id=1, replica_groups=mesh['rows'=4,'seq'=8] {'seq'}, dimensions={1}, use_global_device_ids=true | all-gather | bytes 442368 | tf_op jit(solution)/shard_map/all_gather | solution.py:125
  104.0 28.6 %pmax.7 = f32[4,12,64]{2,1,0:T(8,128)S(1)} all-reduce(f32[4,12,64]{2,1,0:T(8,128)} %get-tuple-element.222), channel_id=1, replica_groups=mesh['rows'=4,'seq'=8] {'seq'}, use_global_device_ids=true, to_apply=%region_2.0 | all-reduce | flops 3072 | bytes 24576 | tf_op jit(solution)/shard_map/pmax | solution.py:153
  141.8 15.5 %all_gather.24 = bf16[4,64,768]{2,1,0:T(8,128)(2,1)S(1)} all-gather(bf16[4,8,768]{2,1,0:T(8,128)(2,1)S(1)} %multiply_convert_fusion.5), channel_id=1, replica_groups=mesh['rows'=4,'seq'=8] {'seq'}, dimensions={1}, use_global_device_ids=true | all-gather | bytes 442368 | tf_op jit(solution)/shard_map/all_gather | solution.py:126
  210.2 26.2 %psum.29 = bf16[4,12,64]{2,1,0:T(8,128)(2,1)S(1)} all-reduce(bf16[4,12,64]{2,1,0:T(8,128)(2,1)S(1)} %fusion.153), channel_id=1, replica_groups=mesh['rows'=4,'seq'=8] {'seq'}, use_global_device_ids=true, to_apply=%region_5.0 | all-reduce | flops 3072 | bytes 12288 | tf_op jit(solution)/shard_map/psum | solution.py:163
  274.0 22.8 %fusion.65 = bf16[4,128,768]{2,1,0:T(8,128)(2,1)} fusion(f32[4,128,768]{2,1,0:T(8,128)} %copy.318, bf16[4,128,768]{2,1,0:T(8,128)(2,1)} %bitcast.323, bf16[4,16,768]{2,1,0:T(8,128)(2,1)S(1)} %collective-permute-done.1, bf16[4,16,768]{2,1,0:T(8,128)(2,1)S(1)} %collective-permute-done, f32[768]{0:T(1024)S(1)} %get-tuple-element.138, ...), kind=kLoop, calls=%fused_computation.208 | loop fusion | flops 77070336 | bytes 3443712 | tf_op jit(solution)/shard_map/convert_element_type | solution.py:183
  300.9 14.4 %all-gather.10.cloned.1.call-done = bf16[768,3072]{1,0:T(8,128)(2,1)} async-done(((bf16[24,3072]{1,0:T(8,128)(2,1)}), bf16[768,3072]{1,0:T(8,128)(2,1)}) %all-gather.10.cloned.1.call-update) | async-done | bytes 4718608 | tf_op jit(solution)/shard_map/all_gather | solution.py:111
  315.3 21.0 %multiply_convert_fusion = (bf16[512,3072]{1,0:T(8,128)(2,1)}, f32[512,3072]{1,0:T(8,128)}, f32[512,3072]{1,0:T(8,128)}) fusion(f32[3072]{0:T(1024)S(1)} %copy-done.159, bf16[768,3072]{1,0:T(8,128)(2,1)} %all-gather.10.cloned.1.call-done, f32[512,768]{1,0:T(8,128)} %copy-done.58, f32[768]{0:T(1024)S(1)} %copy-done.171, f32[768]{0:T(1024)S(1)} %copy-done.151, ...), kind=kOutput, calls=%fused_computation.38 | convolution fusion | flops 2521694208 | bytes 22042624 | tf_op jit(solution)/shard_map/dot_general | solution.py:188
  336.3 45.4 %all-gather.12.cloned.1.call-done = bf16[3072,768]{1,0:T(8,128)(2,1)} async-done(((bf16[96,768]{1,0:T(8,128)(2,1)}), bf16[3072,768]{1,0:T(8,128)(2,1)}) %all-gather.12.cloned.1.call-update) | async-done | bytes 4718608 | tf_op jit(solution)/shard_map/all_gather | solution.py:112
  381.7 6.5 fusion.327
  393.2 10.1 convert_reduce_fusion
  403.3 5.7 multiply_reduce_fusion.1
  435.1 49.1 %all-reduce.7.cloned.1.call-done = bf16[4,64,12,64]{1,3,2,0:T(8,128)(2,1)} async-done(((bf16[4,64,12,64]{1,3,2,0:T(8,128)(2,1)}), bf16[4,64,12,64]{1,3,2,0:T(8,128)(2,1)}) %all-reduce.7.cloned.1.call-update) | async-done | bytes 393232 | tf_op jit(solution)/shard_map/psum | solution.py:220
  504.5 27.1 %fusion.83 = f32[4,128,768]{2,1,0:T(8,128)} fusion(bf16[4,128,768]{2,1,0:T(8,128)(2,1)} %bitcast.329, bf16[4,16,768]{2,1,0:T(8,128)(2,1)} %collective-permute-done.3, bf16[4,16,768]{2,1,0:T(8,128)(2,1)} %collective-permute-done.2, f32[768]{0:T(1024)S(1)} %get-tuple-element.138, f32[768]{0:T(1024)S(1)} %get-tuple-element.139, f32[768]{0:T(1024)S(1)} %copy-done.96, ...), kind=kLoop, calls=%fused_computation.226 | loop fusion | flops 76283904 | bytes 2657280 | tf_op jit(solution)/shard_map/add | solution.py:245
  693.4 5.0 convolution_bitcast_fusion
  698.4 8.0 copy.400
  707.8 7.2 fusion.282
  716.2 8.3 fusion.347
  764.6 42.5 %all-reduce.1 = (f32[12,768]{1,0:T(8,128)S(1)}, f32[12,33]{1,0:T(8,128)S(1)}) all-reduce(f32[12,768]{1,0:T(8,128)S(1)} %concatenate.87, f32[12,33]{1,0:T(8,128)S(1)} %copy.363), channel_id=8, replica_groups=mesh['rows'=4,'seq'=8] {'rows','seq'}, use_global_device_ids=true, to_apply=%region_39.0.clone | all-reduce | flops 9612 | bytes 76896
  808.5 5.2 add_convert_fusion.1
  815.5 12.4 %reduce-scatter.24.cloned.1.call-done = f32[24,2304]{1,0:T(8,128)} async-done(((f32[768,2304]{1,0:T(8,128)}), f32[24,2304]{1,0:T(8,128)}) %reduce-scatter.24.cloned.1.call-update) | async-done | bytes 221200 | tf_op jit(solution)/shard_map/reduce_scatter | solution.py:343
  830.0 138.7 %reduce-scatter.16.cloned.1.call-done = f32[24,3072]{1,0:T(8,128)} async-done(((f32[768,3072]{1,0:T(8,128)}), f32[24,3072]{1,0:T(8,128)}) %reduce-scatter.16.cloned.1.call-update) | async-done | bytes 294928 | tf_op jit(solution)/shard_map/reduce_scatter | solution.py:345
  970.8 139.4 %reduce-scatter.18.cloned.1.call-done = f32[96,768]{1,0:T(8,128)} async-done(((f32[3072,768]{1,0:T(8,128)}), f32[96,768]{1,0:T(8,128)}) %reduce-scatter.18.cloned.1.call-update) | async-done | bytes 294928 | tf_op jit(solution)/shard_map/reduce_scatter | solution.py:346
  (691 shorter events, 384.4 us)
Async XLA Ops:
  7.2 67.5 %all-gather.6.cloned.1.call-start = ((), (), s32[]{:S(2)}) async-start(), calls=%async_computation.6 | async-start | bytes 3649536 | tf_op jit(solution)/shard_map/all_gather | solution.py:109
  8.9 255.7 %all-reduce.5.cloned.1.call-start = ((), (), s32[]{:S(2)}) async-start(), calls=%async_computation.7 | async-start | bytes 1572864 | tf_op jit(solution)/shard_map/psum | solution.py:162
  135.3 161.5 %all-gather.8.cloned.1.call-start = ((), (), s32[]{:S(2)}) async-start(), calls=%async_computation.8 | async-start | bytes 1216512 | tf_op jit(solution)/shard_map/all_gather | solution.py:110
  136.1 179.2 %all-gather.10.cloned.1.call-start = ((), (), s32[]{:S(2)}) async-start(), calls=%async_computation.9 | async-start | bytes 4866048 | tf_op jit(solution)/shard_map/all_gather | solution.py:111
  136.8 244.9 %all-gather.12.cloned.1.call-start = ((), (), s32[]{:S(2)}) async-start(), calls=%async_computation.10 | async-start | bytes 4866048 | tf_op jit(solution)/shard_map/all_gather | solution.py:112
  137.6 346.6 %all-reduce.7.cloned.1.call-start = ((), (), s32[]{:S(2)}) async-start(), calls=%async_computation.11 | async-start | bytes 1572864 | tf_op jit(solution)/shard_map/psum | solution.py:220
  246.9 27.0 %collective-permute-start.1 = (bf16[4,16,768]{2,1,0:T(8,128)(2,1)}, bf16[4,16,768]{2,1,0:T(8,128)(2,1)S(1)}, u32[]{:S(2)}, u32[]{:S(2)}) collective-permute-start(bf16[4,16,768]{2,1,0:T(8,128)(2,1)} %get-tuple-element.217), channel_id=1, source_target_pairs={{1,0},{2,1},{3,2},{4,3},{5,4},{6,5},{7,6},{9,8},{10,9},{11,10},{12... | collective-permute-start | bytes 294920 | tf_op jit(solution)/shard_map/ppermute | solution.py:32
  248.1 25.7 %collective-permute-start = (bf16[4,16,768]{2,1,0:T(8,128)(2,1)}, bf16[4,16,768]{2,1,0:T(8,128)(2,1)S(1)}, u32[]{:S(2)}, u32[]{:S(2)}) collective-permute-start(bf16[4,16,768]{2,1,0:T(8,128)(2,1)} %get-tuple-element.216), channel_id=1, source_target_pairs={{0,1},{1,2},{2,3},{3,4},{4,5},{5,6},{6,7},{8,9},{9,10},{10,11},{11... | collective-permute-start | bytes 294920 | tf_op jit(solution)/shard_map/ppermute | solution.py:31
  299.5 109.5 %copy-start.145 = (f32[512]{0:T(512)}, f32[512]{0:T(512)S(1)}, u32[]{:S(2)}) copy-start(f32[512]{0:T(512)S(1)} %broadcast_multiply_fusion.1) | copy-start | bytes 6148
  300.9 108.1 %copy-start.163 = (f32[512]{0:T(512)}, f32[512]{0:T(512)S(1)}, u32[]{:S(2)}) copy-start(f32[512]{0:T(512)S(1)} %fusion.270) | copy-start | bytes 6148
  427.9 249.4 %reduce-scatter.22.cloned.1.call-start = ((), (), s32[]{:S(2)}) async-start(), calls=%async_computation.16 | async-start | bytes 442368
  435.1 243.2 %reduce-scatter.20.cloned.1.call-start = ((), (), s32[]{:S(2)}) async-start(), calls=%async_computation.15 | async-start | bytes 442368
  494.6 319.2 %reduce-scatter.14.cloned.1.call-start = ((), (), s32[]{:S(2)}) async-start(), calls=%async_computation.12 | async-start | bytes 2433024 | tf_op jit(solution)/shard_map/reduce_scatter | solution.py:344
  496.8 7.1 collective-permute-start.3
  498.7 5.2 collective-permute-start.2
  503.9 324.1 %reduce-scatter.24.cloned.1.call-start = ((), (), s32[]{:S(2)}) async-start(), calls=%async_computation.17 | async-start | bytes 7299072 | tf_op jit(solution)/shard_map/reduce_scatter | solution.py:343
  706.5 262.3 %reduce-scatter.16.cloned.1.call-start = ((), (), s32[]{:S(2)}) async-start(), calls=%async_computation.13 | async-start | bytes 9732096 | tf_op jit(solution)/shard_map/reduce_scatter | solution.py:345
  715.1 395.1 %reduce-scatter.18.cloned.1.call-start = ((), (), s32[]{:S(2)}) async-start(), calls=%async_computation.14 | async-start | bytes 9732096 | tf_op jit(solution)/shard_map/reduce_scatter | solution.py:346
  813.7 155.0 %copy-start.76 = (f32[24,3072]{1,0:T(8,128)S(1)}, f32[24,3072]{1,0:T(8,128)}, u32[]{:S(2)}) copy-start(f32[24,3072]{1,0:T(8,128)} %param.24) | copy-start | bytes 884740
  813.8 155.0 %copy-start.86 = (f32[24,3072]{1,0:T(8,128)S(1)}, f32[24,3072]{1,0:T(8,128)}, u32[]{:S(2)}) copy-start(f32[24,3072]{1,0:T(8,128)} %param.33) | copy-start | bytes 884740
  813.8 155.0 %copy-start.87 = (f32[24,3072]{1,0:T(8,128)S(1)}, f32[24,3072]{1,0:T(8,128)}, u32[]{:S(2)}) copy-start(f32[24,3072]{1,0:T(8,128)} %param.32) | copy-start | bytes 884740
  815.5 294.6 %copy-start.78 = (f32[96,768]{1,0:T(8,128)S(1)}, f32[96,768]{1,0:T(8,128)}, u32[]{:S(2)}) copy-start(f32[96,768]{1,0:T(8,128)} %param.25) | copy-start | bytes 884740
  815.5 294.6 %copy-start.88 = (f32[96,768]{1,0:T(8,128)S(1)}, f32[96,768]{1,0:T(8,128)}, u32[]{:S(2)}) copy-start(f32[96,768]{1,0:T(8,128)} %param.35) | copy-start | bytes 884740
  815.5 294.6 %copy-start.89 = (f32[96,768]{1,0:T(8,128)S(1)}, f32[96,768]{1,0:T(8,128)}, u32[]{:S(2)}) copy-start(f32[96,768]{1,0:T(8,128)} %param.34) | copy-start | bytes 884740
  (187 other events, 1449.0 us)
Sparse Core Ops, SparseCore 0:
  11.6 63.0 all-gather.5
  135.5 55.9 all-reduce.4
  195.5 53.2 all-gather.7
  252.7 62.6 all-gather.9
  319.2 62.4 all-gather.11
  428.0 56.1 all-reduce.6
  486.4 29.7 reduce-scatter.21
  518.5 28.7 reduce-scatter.19
  552.7 97.1 reduce-scatter.13
  706.6 121.3 reduce-scatter.23
  833.8 134.8 reduce-scatter.15
  975.5 134.5 reduce-scatter.17
where the time goes:
time: 1130 us; the launch traced here: 1120 us
  waiting for transfers between devices  420 us (37%)
  matrix products  310 us (27%)
  blocking collectives  171 us (15%)
  local copies, waits for them, and re-layouts  103 us (9%)
  other arithmetic  89.7 us (8%)
  between operations  17.4 us (2%)
    reduce_scatter x1, waiting for transfers between devices, on_device(): lax.psum_scatter(grad_down, ('rows', 'seq'), scatter_dimension=0, tiled=T...  139 us
    reduce_scatter x1, waiting for transfers between devices, on_device(): lax.psum_scatter(grad_up, ('rows', 'seq'), scatter_dimension=0, tiled=True)  139 us
    dot_general x36, matrix products, pseudo_inverse(): jnp.matmul(product, inner_term, precision=top_precision)  88.3 us
    unnamed x432, local copies, waits for them, and re-layouts  50 us
    dot_general x18, matrix products, pseudo_inverse(): product = jnp.matmul(matrix, approx, precision=top_precision)  49.5 us
    psum x1, waiting for transfers between devices, on_device(): lax.psum(mixing_part.astype(jnp.bfloat16), 'seq').astype(jnp.float32)  49.1 us
    dot_general x18, matrix products, pseudo_inverse(): approx = 0.25 * jnp.matmul(approx, inner_term, precision=top_precision)  47.4 us
    all_gather x1, waiting for transfers between devices, on_device(): lax.all_gather(down_weight.astype(jnp.bfloat16), ('rows', 'seq'), axis=0,...  45.4 us
  transfers between devices with their start and end apart: 16, of which 7 were waited for; matrix products, arithmetic and copies ran while one was open for 38% of the time, Pallas kernels for 0%

commit v1 on v0

--- a/solution.py
+++ b/solution.py
@@ -1,7 +1,280 @@
+import functools
+
 import jax
 import jax.numpy as jnp
 from jax import lax
+from jax.experimental import pallas as pl
+from jax.experimental.pallas import tpu as pltpu
 from jax.sharding import PartitionSpec as P
+
+BF = jnp.bfloat16
+F32 = jnp.float32
+MESH = pl.DeviceIdType.MESH
+
+
+def remote(src, dst, send_sem, recv_sem, device):
+    return pltpu.make_async_remote_copy(
+        src_ref=src, dst_ref=dst, send_sem=send_sem, recv_sem=recv_sem,
+        device_id=device, device_id_type=MESH,
+    )
+
+
+def place():
+    row, spot = lax.axis_index("rows"), lax.axis_index("seq")
+    line, core = spot // 2, spot % 2
+    flip_one = row + 1 - 2 * (row % 2)
+    flip_two = row + 2 - 4 * (row // 2)
+    first = (1 - core) * flip_one + core * flip_two
+    second = (1 - core) * flip_two + core * flip_one
+    return row, line, core, first, second, 3 - row
+
+
+def greet(devices):
+    barrier = pltpu.get_barrier_semaphore()
+    for device in devices:
+        pl.semaphore_signal(barrier, inc=1, device_id=device, device_id_type=MESH)
+    pl.semaphore_wait(barrier, len(devices))
+
+
+def gather_kernel(line_size, n_w, *refs):
+    ins, outs = refs[:n_w], refs[n_w : 2 * n_w]
+    asm, stage = refs[2 * n_w : 3 * n_w], refs[3 * n_w : 4 * n_w]
+    send, recv, local = refs[4 * n_w :]
+    row, line, core, first, second, across = place()
+    own_spot, sibling = 2 * line + core, (row, 2 * line + 1 - core)
+    peers = [(row, 2 * ((line + k) % line_size) + core) for k in range(1, line_size)]
+    to_first, to_second = (first, own_spot), (second, own_spot)
+    greet(peers + [to_first, to_second, sibling])
+    rows = [x.shape[0] for x in ins]
+    half = [x.shape[1] // 2 for x in ins]
+    started = []
+
+    def go(w, k, src, dst, device):
+        copy = remote(src, dst, send.at[w, k], recv.at[w, k], device)
+        copy.start()
+        started.append(copy)
+        return copy
+
+    def cols(w, which):
+        return pl.ds(pl.multiple_of(which * half[w], 128), half[w])
+
+    def slab(w, index):
+        size = 2 * rows[w] * line_size
+        return outs[w].at[pl.ds(pl.multiple_of(index * size, size), size), cols(w, core)]
+
+    asm_copy, z_copy, own_copy, hop, sib = {}, {}, {}, {}, {}
+    z0 = line_size
+    for w in range(n_w):
+        part = pl.ds(pl.multiple_of(core * rows[w], 8), rows[w])
+        asm_copy[w] = go(w, 0, ins[w].at[:, cols(w, 1 - core)], asm[w].at[part, :], sibling)
+        asm[w][part, :] = ins[w][:, cols(w, core)]
+
+    def spread(w):
+        asm_copy[w].wait_recv()
+        stage[w][...] = asm[w][...].astype(BF)
+        size = 2 * rows[w]
+        at = pl.ds(pl.multiple_of((row * line_size + line) * size, size), size)
+        block = outs[w].at[at, cols(w, core)]
+        z_copy[w] = [go(w, 1 + k, stage[w], block, peers[k]) for k in range(line_size - 1)]
+        own_copy[w] = pltpu.make_async_copy(stage[w], block, local.at[w])
+        own_copy[w].start()
+
+    def step_one(w):
+        own_copy[w].wait()
+        for copy in z_copy[w]:
+            copy.wait_recv()
+        mine = slab(w, row)
+        hop[w] = [go(w, z0, mine, mine, to_first), go(w, z0 + 1, mine, mine, to_second)]
+        sib[w] = [go(w, z0 + 3, mine, mine, sibling)]
+
+    def step_two(w):
+        hop[w][0].wait_recv()
+        got = slab(w, first)
+        hop[w].append(go(w, z0 + 2, got, got, to_second))
+        sib[w].append(go(w, z0 + 4, got, got, sibling))
+
+    def step_three(w):
+        hop[w][1].wait_recv()
+        got = slab(w, second)
+        sib[w].append(go(w, z0 + 5, got, got, sibling))
+        hop[w][2].wait_recv()
+        got = slab(w, across)
+        sib[w].append(go(w, z0 + 6, got, got, sibling))
+
+    for w in range(n_w):
+        spread(w)
+    for t in range(n_w + 2):
+        if t < n_w:
+            step_one(t)
+        if 0 <= t - 1 < n_w:
+            step_two(t - 1)
+        if 0 <= t - 2 < n_w:
+            step_three(t - 2)
+    for w in range(n_w):
+        for copy in sib[w]:
+            copy.wait_recv()
+    for copy in started:
+        copy.wait_send()
+
+
+def gather_weights(shards, seq_size):
+    line_size, n_w = seq_size // 2, len(shards)
+    n_dev = 4 * seq_size
+    n_sem = line_size + 7
+    vmem = pl.BlockSpec(memory_space=pltpu.VMEM)
+    return pl.pallas_call(
+        functools.partial(gather_kernel, line_size, n_w),
+        out_shape=[jax.ShapeDtypeStruct((n_dev * x.shape[0], x.shape[1]), BF) for x in shards],
+        in_specs=[vmem] * n_w,
+        out_specs=[pl.BlockSpec(memory_space=pltpu.HBM)] * n_w,
+        scratch_shapes=[pltpu.VMEM((2 * x.shape[0], x.shape[1] // 2), F32) for x in shards]
+        + [pltpu.VMEM((2 * x.shape[0], x.shape[1] // 2), BF) for x in shards]
+        + [
+            pltpu.SemaphoreType.DMA((n_w, n_sem)),
+            pltpu.SemaphoreType.DMA((n_w, n_sem)),
+            pltpu.SemaphoreType.DMA((n_w,)),
+        ],
+        compiler_params=pltpu.CompilerParams(
+            collective_id=0, has_side_effects=True, vmem_limit_bytes=32 * 1024 * 1024
+        ),
+        name="gather_weights",
+    )(*shards)
+
+
+def scatter_kernel(line_size, n_w, *refs):
+    ins, outs = refs[:n_w], refs[n_w : 2 * n_w]
+    acc, buf0, buf1, buf2, buf3, fin = [refs[(2 + i) * n_w : (3 + i) * n_w] for i in range(6)]
+    send, recv, local = refs[8 * n_w :]
+    row, line, core, first, second, across = place()
+    own_spot, sibling = 2 * line + core, (row, 2 * line + 1 - core)
+    peers = [(row, 2 * ((line + k) % line_size) + core) for k in range(1, line_size)]
+    to_first, to_second = (first, own_spot), (second, own_spot)
+    greet(peers + [to_first, to_second, sibling])
+    rows = [x.shape[0] for x in outs]
+    half = [x.shape[1] // 2 for x in ins]
+    started = []
+    copies = {}
+
+    def go(w, k, src, dst, device):
+        copy = remote(src, dst, send.at[w, k], recv.at[w, k], device)
+        copy.start()
+        started.append(copy)
+        return copy
+
+    def cols(w, which):
+        return pl.ds(pl.multiple_of(which * half[w], 128), half[w])
+
+    def size(w):
+        return 2 * rows[w] * line_size
+
+    def slab(w, index):
+        return pl.ds(pl.multiple_of(index * size(w), size(w)), size(w))
+
+    def add(w, index, other, other_start):
+        step = 48
+        base = index * size(w)
+
+        def one(i, carry):
+            at = pl.ds(pl.multiple_of(base + i * step, 16), step)
+            there = pl.ds(pl.multiple_of(other_start + i * step, 16), step)
+            acc[w][at, :] = acc[w][at, :] + other[there, :]
+            return carry
+
+        lax.fori_loop(0, size(w) // step, one, 0)
+
+    def open_up(w):
+        copies[w, 0] = go(w, 0, ins[w].at[:, cols(w, 1 - core)], buf0[w], sibling)
+        copies[w, "own"] = pltpu.make_async_copy(ins[w].at[:, cols(w, core)], acc[w], local.at[w])
+        copies[w, "own"].start()
+
+    def step_one(w):
+        copies[w, "own"].wait()
+        copies[w, 0].wait_recv()
+        add(w, across, buf0[w], across * size(w))
+        copies[w, 1] = go(w, 1, acc[w].at[slab(w, across), :], buf1[w].at[0], to_second)
+        add(w, second, buf0[w], second * size(w))
+        copies[w, 2] = go(w, 2, acc[w].at[slab(w, second), :], buf1[w].at[1], to_second)
+        add(w, first, buf0[w], first * size(w))
+        add(w, row, buf0[w], row * size(w))
+
+    def step_two(w):
+        copies[w, 1].wait_recv()
+        add(w, first, buf1[w].at[0], 0)
+        copies[w, 3] = go(w, 3, acc[w].at[slab(w, first), :], buf2[w], to_first)
+        copies[w, 2].wait_recv()
+        add(w, row, buf1[w].at[1], 0)
+
+    def step_three(w):
+        copies[w, 3].wait_recv()
+        add(w, row, buf2[w], 0)
+        block = 2 * rows[w]
+        for k in range(1, line_size):
+            there = (line + k) % line_size
+            at = pl.ds(pl.multiple_of((row * line_size + there) * block, block), block)
+            copies[w, 3 + k] = go(w, 3 + k, acc[w].at[at, :], buf3[w].at[line], peers[k - 1])
+        at = pl.ds(pl.multiple_of((row * line_size + line) * block, block), block)
+        buf3[w][line] = acc[w][at, :]
+
+    def step_four(w):
+        for k in range(1, line_size):
+            copies[w, 3 + k].wait_recv()
+        total = buf3[w][0].astype(F32)
+        for k in range(1, line_size):
+            total = total + buf3[w][k].astype(F32)
+        fin[w][...] = total
+        part = pl.ds(pl.multiple_of((1 - core) * rows[w], 8), rows[w])
+        copies[w, 9] = go(w, 3 + line_size, fin[w].at[part, :], outs[w].at[:, cols(w, core)], sibling)
+        part = pl.ds(pl.multiple_of(core * rows[w], 8), rows[w])
+        outs[w][:, cols(w, core)] = fin[w][part, :]
+
+    for w in range(n_w):
+        open_up(w)
+    for t in range(n_w + 3):
+        if t < n_w:
+            step_one(t)
+        if 0 <= t - 1 < n_w:
+            step_two(t - 1)
+        if 0 <= t - 2 < n_w:
+            step_three(t - 2)
+        if 0 <= t - 3 < n_w:
+            step_four(t - 3)
+    for w in range(n_w):
+        copies[w, 9].wait_recv()
+    for copy in started:
+        copy.wait_send()
+
+
+def scatter_grads(grads, seq_size):
+    line_size, n_w = seq_size // 2, len(grads)
+    n_dev = 4 * seq_size
+    n_sem = line_size + 4
+    rows = [x.shape[0] // n_dev for x in grads]
+    half = [x.shape[1] // 2 for x in grads]
+    kinds = [x.dtype for x in grads]
+    vmem = pl.BlockSpec(memory_space=pltpu.VMEM)
+    every = range(n_w)
+    quarter = [2 * rows[w] * line_size for w in every]
+    return pl.pallas_call(
+        functools.partial(scatter_kernel, line_size, n_w),
+        out_shape=[jax.ShapeDtypeStruct((rows[w], 2 * half[w]), F32) for w in every],
+        in_specs=[pl.BlockSpec(memory_space=pltpu.HBM)] * n_w,
+        out_specs=[vmem] * n_w,
+        scratch_shapes=[pltpu.VMEM((4 * quarter[w], half[w]), kinds[w]) for w in every]
+        + [pltpu.VMEM((4 * quarter[w], half[w]), kinds[w]) for w in every]
+        + [pltpu.VMEM((2, quarter[w], half[w]), kinds[w]) for w in every]
+        + [pltpu.VMEM((quarter[w], half[w]), kinds[w]) for w in every]
+        + [pltpu.VMEM((line_size, 2 * rows[w], half[w]), kinds[w]) for w in every]
+        + [pltpu.VMEM((2 * rows[w], half[w]), F32) for w in every]
+        + [
+            pltpu.SemaphoreType.DMA((n_w, n_sem)),
+            pltpu.SemaphoreType.DMA((n_w, n_sem)),
+            pltpu.SemaphoreType.DMA((n_w,)),
+        ],
+        compiler_params=pltpu.CompilerParams(
+            collective_id=1, has_side_effects=True, vmem_limit_bytes=48 * 1024 * 1024
+        ),
+        name="scatter_grads",
+    )(*grads)
 
 LAND = 64
 PINV_ITERS = 6
@@ -70,6 +343,47 @@
     new_second = beta_two * second + (1.0 - beta_two) * gradient * gradient
     update = new_first / corr_one / (jnp.sqrt(new_second / corr_two) + adam_eps)
     return (new_first, new_second, weight - step_rate * (update + decay_coef * weight))
+
+
+def kernels_fit(rows_each):
+    return (
+        lax.axis_size("rows") == 4
+        and lax.axis_size("seq") % 2 == 0
+        and all(rows % 24 == 0 for rows in rows_each)
+    )
+
+
+def all_weights(qkv_weight, out_weight, up_weight, down_weight, vectors):
+    axes = ("rows", "seq")
+    matrices = (qkv_weight, out_weight, up_weight, down_weight)
+    if kernels_fit([x.shape[0] for x in matrices]):
+        count = vectors.shape[0]
+        table = jnp.pad(vectors.T, ((0, 0), (0, 256 - count)))
+        whole = gather_weights(matrices + (table,), lax.axis_size("seq"))
+        return (*whole[:4], whole[4][:, :count].T)
+    return tuple(
+        lax.all_gather(x.astype(BF), axes, axis=0, tiled=True) for x in matrices
+    ) + (lax.all_gather(vectors.astype(BF), axes, axis=1, tiled=True),)
+
+
+def all_grads(grad_qkv, grad_out, grad_up, grad_down, grad_vec, grad_taps):
+    axes = ("rows", "seq")
+    matrices = (grad_qkv, grad_out, grad_up, grad_down)
+    n_dev = lax.axis_size("rows") * lax.axis_size("seq")
+    if kernels_fit([x.shape[0] // n_dev for x in matrices]):
+        count, width = grad_vec.shape
+        heads, taps = grad_taps.shape
+        each = jnp.pad(grad_taps, ((0, width // n_dev - heads), (0, 0)))
+        small = jnp.concatenate([grad_vec.T, jnp.tile(each, (n_dev, 1))], axis=1)
+        small = jnp.pad(small, ((0, 0), (0, 256 - count - taps)))
+        sums = scatter_grads([x.astype(BF) for x in matrices] + [small], lax.axis_size("seq"))
+        return (*sums[:4], sums[4][:, :count].T, sums[4][:heads, count : count + taps])
+    return tuple(
+        lax.psum_scatter(x, axes, scatter_dimension=0, tiled=True) for x in matrices
+    ) + (
+        lax.psum_scatter(grad_vec, axes, scatter_dimension=1, tiled=True),
+        lax.psum(grad_taps, axes),
+    )
 
 
 def on_device(
@@ -105,12 +419,8 @@
     row_count = seq_count * local_len
     head_shape = (seq_count, local_len, head_count, head_size)
     land_shape = (seq_count, LAND, head_count, head_size)
-    full_qkv, full_out, full_up, full_down, full_vec = (
-        lax.all_gather(qkv_weight.astype(jnp.bfloat16), ("rows", "seq"), axis=0, tiled=True),
-        lax.all_gather(out_weight.astype(jnp.bfloat16), ("rows", "seq"), axis=0, tiled=True),
-        lax.all_gather(up_weight.astype(jnp.bfloat16), ("rows", "seq"), axis=0, tiled=True),
-        lax.all_gather(down_weight.astype(jnp.bfloat16), ("rows", "seq"), axis=0, tiled=True),
-        lax.all_gather(vectors.astype(jnp.bfloat16), ("rows", "seq"), axis=1, tiled=True),
+    full_qkv, full_out, full_up, full_down, full_vec = all_weights(
+        qkv_weight, out_weight, up_weight, down_weight, vectors
     )
     vec_float = full_vec.astype(jnp.float32)
     flat_in = tokens.reshape(row_count, model_width)
@@ -339,14 +649,9 @@
         ],
         axis=0,
     )
-    summed_qkv, summed_out, summed_up, summed_down, summed_vec = (
-        lax.psum_scatter(grad_qkv, ("rows", "seq"), scatter_dimension=0, tiled=True),
-        lax.psum_scatter(grad_out, ("rows", "seq"), scatter_dimension=0, tiled=True),
-        lax.psum_scatter(grad_up, ("rows", "seq"), scatter_dimension=0, tiled=True),
-        lax.psum_scatter(grad_down, ("rows", "seq"), scatter_dimension=0, tiled=True),
-        lax.psum_scatter(grad_vec, ("rows", "seq"), scatter_dimension=1, tiled=True),
-    )
-    summed_taps = lax.psum(grad_taps, ("rows", "seq"))
+    summed_qkv, summed_out, summed_up, summed_down, summed_vec, summed_taps = all_grads(
+        grad_qkv, grad_out, grad_up, grad_down, grad_vec, grad_taps
+    )
     new_qkv = adam_step(qkv_weight, qkv_first, qkv_second, summed_qkv, rate_matrix, decay_rate)
     new_out = adam_step(out_weight, out_first, out_second, summed_out, rate_output, decay_rate)
     new_up = adam_step(up_weight, up_first, up_second, summed_up, rate_matrix, decay_rate)

time: 1130 us -> 865 us (0.77)
  waiting for transfers between devices: 420 us -> 13.5 us
  Pallas kernels: 0 us -> 174 us
  blocking collectives: 171 us -> 89.1 us
  local copies, waits for them, and re-layouts: 103 us -> 171 us
  other arithmetic: 89.7 us -> 76.6 us
    reduce_scatter x4 -> x0, waiting for transfers between devices: 291 us -> none  [the longest x1 139 us: on_device(): lax.psum_scatter(grad_down, ('rows', 'seq'), scatter_dimension=0, tiled=T...]
    pallas_call x0 -> x2, Pallas kernels: none -> 174 us  [the longest x1 91.8 us: scatter_grads(): pl.pallas_call(functools.partial(scatter_kernel, line_size, n_w), out_sha...]
    all_gather x4 -> x0, waiting for transfers between devices: 79.8 us -> none  [the longest x1 45.4 us: on_device(): lax.all_gather(down_weight.astype(jnp.bfloat16), ('rows', 'seq'), axis=0,...]
    psum x1, waiting for transfers between devices: 49.1 us -> 0.01 us  [on_device(): lax.psum(mixing_part.astype(jnp.bfloat16), 'seq').astype(jnp.float32)]
    all_gather x1 -> x0, blocking collectives: 43.9 us -> none  [on_device(): lax.all_gather(vectors.astype(jnp.bfloat16), ('rows', 'seq'), axis=1, til...]
    unnamed x1 -> x0, blocking collectives: 42.5 us -> none
    another operation x34, local copies, waits for them, and re-layouts: 13.7 us -> 43.1 us  [on_device(): jnp.stack(tap_terms, axis=1).reshape(head_count, head_size, tap_count)]
    unnamed x432 -> x451, local copies, waits for them, and re-layouts: 50 us -> 79.2 us
  transfers between devices with their start and end apart: 16 -> 8, of which waited for: 7 -> 1; matrix products, arithmetic and copies ran while one was open for 38% -> 44% of each run, Pallas kernels for 0% -> 0%
where the time goes in v1:
time: 865 us; the launch traced here: 852 us
  matrix products  303 us (35%)
  Pallas kernels  174 us (20%)
  local copies, waits for them, and re-layouts  171 us (20%)
  blocking collectives  89.1 us (10%)
  other arithmetic  76.6 us (9%)
  between operations  17.1 us (2%)
  waiting for transfers between devices  13.5 us (2%)
    pallas_call x1, Pallas kernels, scatter_grads(): pl.pallas_call(functools.partial(scatter_kernel, line_size, n_w), out_sha...  91.8 us
    dot_general x36, matrix products, pseudo_inverse(): jnp.matmul(product, inner_term, precision=top_precision)  88 us
    pallas_call x1, Pallas kernels, gather_weights(): pl.pallas_call(functools.partial(gather_kernel, line_size, n_w), out_shap...  81.9 us
    unnamed x451, local copies, waits for them, and re-layouts  79.2 us
    dot_general x18, matrix products, pseudo_inverse(): product = jnp.matmul(matrix, approx, precision=top_precision)  61.9 us
    dot_general x18, matrix products, pseudo_inverse(): approx = 0.25 * jnp.matmul(approx, inner_term, precision=top_precision)  45.8 us
    another operation x34, local copies, waits for them, and re-layouts, on_device(): jnp.stack(tap_terms, axis=1).reshape(head_count, head_size, tap_count)  43.1 us
    pmax x1, blocking collectives, on_device(): row_max = lax.pmax(jnp.max(score_three, axis=-1), 'seq')  29.2 us
  transfers between devices with their start and end apart: 8, of which 1 were waited for; matrix products, arithmetic and copies ran while one was open for 44% of the time, Pallas kernels for 0%

profile of v1, /device:TPU:0, one launch (start us, length us, event | category | flops | bytes accessed | tf_op | source)
XLA Modules:
  0.0 852.3 jit_solution(1591506122738763906)
XLA Ops:
  12.4 81.9 %gather_weights.1 = (bf16[768,2304]{1,0:T(8,128)(2,1)S(1)}, bf16[768,768]{1,0:T(8,128)(2,1)S(1)}, bf16[768,3072]{1,0:T(8,128)(2,1)S(1)}, bf16[3072,768]{1,0:T(8,128)(2,1)S(1)}, bf16[768,256]{1,0:T(8,128)(2,1)S(1)}) custom-call(f32[24,2304]{1,0:T(8,128)S(1)} %copy-done.4, f32[24,768]{1,0:T(8,128)S(1)} %copy-done.6, f32[24,3072]{1,0:T(8,128)S(1)} %copy-done, ...), custom_call_target="tpu_custom_call" | custom-call | tf_op jit(solution)/shard_map/gather_weights/pallas_call | solution.py:125
  105.1 18.1 %all_gather.6 = bf16[4,64,768]{2,1,0:T(8,128)(2,1)S(1)} all-gather(bf16[4,8,768]{2,1,0:T(8,128)(2,1)S(1)} %multiply_convert_fusion.6), channel_id=1, replica_groups=mesh['rows'=4,'seq'=8] {'seq'}, dimensions={1}, use_global_device_ids=true | all-gather | bytes 442368 | tf_op jit(solution)/shard_map/all_gather | solution.py:435
  136.0 29.2 %pmax.7 = f32[4,12,64]{2,1,0:T(8,128)S(1)} all-reduce(f32[4,12,64]{2,1,0:T(8,128)S(1)} %get-tuple-element.280), channel_id=1, replica_groups=mesh['rows'=4,'seq'=8] {'seq'}, use_global_device_ids=true, to_apply=%region_2.3 | all-reduce | flops 3072 | bytes 24576 | tf_op jit(solution)/shard_map/pmax | solution.py:463
  179.3 15.2 %all_gather.7 = bf16[4,64,768]{2,1,0:T(8,128)(2,1)S(1)} all-gather(bf16[4,8,768]{2,1,0:T(8,128)(2,1)S(1)} %multiply_convert_fusion.5), channel_id=1, replica_groups=mesh['rows'=4,'seq'=8] {'seq'}, dimensions={1}, use_global_device_ids=true | all-gather | bytes 442368 | tf_op jit(solution)/shard_map/all_gather | solution.py:436
  260.9 26.7 %psum.22 = bf16[4,12,64]{2,1,0:T(8,128)(2,1)S(1)} all-reduce(bf16[4,12,64]{2,1,0:T(8,128)(2,1)S(1)} %fusion.154), channel_id=1, replica_groups=mesh['rows'=4,'seq'=8] {'seq'}, use_global_device_ids=true, to_apply=%region_5.6 | all-reduce | flops 3072 | bytes 12288 | tf_op jit(solution)/shard_map/psum | solution.py:473
  290.8 4.0 fusion.323
  299.5 4.5 fusion.148
  309.3 23.2 %fusion.66 = bf16[4,128,768]{2,1,0:T(8,128)(2,1)S(1)} fusion(f32[4,128,768]{2,1,0:T(8,128)} %copy.407, bf16[4,128,768]{2,1,0:T(8,128)(2,1)} %bitcast.332, bf16[4,16,768]{2,1,0:T(8,128)(2,1)} %collective-permute-done.1, bf16[4,16,768]{2,1,0:T(8,128)(2,1)} %collective-permute-done, f32[768]{0:T(1024)S(1)} %get-tuple-element.206, f32[768]{0:T(1024)S(1)} %copy-done.124, ...), kind=kLoop, calls=%fused_computation.212 | loop fusion | flops 77070336 | bytes 3443712 | tf_op jit(solution)/shard_map/convert_element_type | solution.py:493
  335.4 18.5 %multiply_convert_fusion = (bf16[512,3072]{1,0:T(8,128)(2,1)S(1)}, f32[512,3072]{1,0:T(8,128)}, f32[512,3072]{1,0:T(8,128)}) fusion(f32[3072]{0:T(1024)S(1)} %copy-done.175, bf16[768,3072]{1,0:T(8,128)(2,1)S(1)} %bitcast.328, f32[512,768]{1,0:T(8,128)S(1)} %get-tuple-element.285, f32[768]{0:T(1024)S(1)} %copy-done.184, f32[768]{0:T(1024)S(1)} %copy-done.167, ...), kind=kOutput, calls=%fused_computation.38 | convolution fusion | flops 2521694208 | bytes 22042624 | tf_op jit(solution)/shard_map/dot_general | solution.py:498
  361.5 10.2 %convert_reduce_fusion = (f32[3072]{0:T(1024)}, bf16[512,3072]{1,0:T(8,128)(2,1)}) fusion(f32[512,3072]{1,0:T(8,128)} %get-tuple-element.267, f32[512,3072]{1,0:T(8,128)} %get-tuple-element.286, f32[3072]{0:T(1024)S(1)} %copy-done.175, bf16[512,768]{1,0:T(8,128)(2,1)S(1)} %get-tuple-element.259, bf16[3072,768]{1,0:T(8,128)(2,1)S(1)} %bitcast.330), kind=kOutput, calls=%fused_computation.36 | convolution fusion | flops 2442654720 | bytes 21258240 | tf_op jit(solution)/shard_map/nd,fd->nf/dot_general | solution.py:510
  371.7 5.6 multiply_reduce_fusion.1
  379.7 5.9 fusion.100
  391.4 4.0 multiply_reduce_fusion.3
  396.9 4.8 convolution_convert_fusion.1.refs_2_
  401.7 4.4 convolution_convert_fusion.refs_3_
  444.6 4.7 fusion.116
  459.9 3.9 fusion.115
  525.1 12.4 %fusion.84 = f32[4,128,768]{2,1,0:T(8,128)} fusion(bf16[4,128,768]{2,1,0:T(8,128)(2,1)S(1)} %bitcast.338, bf16[4,16,768]{2,1,0:T(8,128)(2,1)} %collective-permute-done.3, bf16[4,16,768]{2,1,0:T(8,128)(2,1)} %collective-permute-done.2, f32[768]{0:T(1024)} %copy-done.123, f32[768]{0:T(1024)} %get-tuple-element.207, f32[768]{0:T(1024)} %get-tuple-element.208, ...), kind=kLoop, calls=%fused_computation.230 | loop fusion | flops 76283904 | bytes 2657280 | tf_op jit(solution)/shard_map/add | solution.py:555
  656.7 4.1 fusion.337
  681.0 5.8 fusion.331
  686.8 4.0 fusion.334
  690.8 9.0 %multiply_reduce_fusion.2 = (f32[4,12,64]{2,1,0:T(8,128)S(1)}, f32[4,12,64,64]{2,3,1,0:T(8,128)S(1)}) fusion(f32[4,12,64]{2,1,0:T(8,128)} %copy-done.114, f32[4,12,64,64]{2,3,1,0:T(8,128)} %copy-done.36, f32[4,12,64]{2,1,0:T(8,128)} %copy-done.101, f32[4,12,64,64]{3,2,1,0:T(8,128)} %get-tuple-element.291, f32[4,12]{1,0:T(4,128)S(1)} %copy-done.177, ...), kind=kOutput, calls=%fused_computation.296 | convolution fusion | flops 154334208 | bytes 7115136 | tf_op jit(solution)/shard_map/transpose(jvp())/dot_general | solution.py:333
  706.1 13.4 %reduce-scatter.7.cloned.1.call-done = bf16[8,3072]{1,0:T(8,128)(2,1)} async-done(((bf16[64,3072]{1,0:T(8,128)(2,1)}), bf16[8,3072]{1,0:T(8,128)(2,1)}) %reduce-scatter.7.cloned.1.call-update) | async-done | bytes 49168
  747.0 91.8 %scatter_grads.1 = (f32[24,2304]{1,0:T(8,128)S(1)}, f32[24,768]{1,0:T(8,128)S(1)}, f32[24,3072]{1,0:T(8,128)S(1)}, f32[96,768]{1,0:T(8,128)S(1)}, f32[24,256]{1,0:T(8,128)S(1)}) custom-call(bf16[768,2304]{1,0:T(8,128)(2,1)} %fusion.7.refs_0_, bf16[768,768]{1,0:T(8,128)(2,1)S(1)} %convolution_convert_fusion.3.refs_1_, ...), custom_call_target="tpu_custom_call" | custom-call | tf_op jit(solution)/shard_map/scatter_grads/pallas_call | solution.py:257
  (687 shorter events, 430.1 us)
Async XLA Ops:
  7.2 292.3 %all-reduce.6.cloned.1.call-start = ((), (), s32[]{:S(2)}) async-start(), calls=%async_computation.2 | async-start | bytes 1572864 | tf_op jit(solution)/shard_map/psum | solution.py:472
  168.4 372.2 %all-reduce.8.cloned.1.call-start = ((), (), s32[]{:S(2)}) async-start(), calls=%async_computation.3 | async-start | bytes 1572864 | tf_op jit(solution)/shard_map/psum | solution.py:530
  169.1 139.8 %collective-permute-start.1 = (bf16[4,16,768]{2,1,0:T(8,128)(2,1)}, bf16[4,16,768]{2,1,0:T(8,128)(2,1)}, u32[]{:S(2)}, u32[]{:S(2)}) collective-permute-start(bf16[4,16,768]{2,1,0:T(8,128)(2,1)} %get-tuple-element.275), channel_id=1, source_target_pairs={{1,0},{2,1},{3,2},{4,3},{5,4},{6,5},{7,6},{9,8},{10,9},{11,10},{12... | collective-permute-start | bytes 294920 | tf_op jit(solution)/shard_map/ppermute | solution.py:305
  170.4 138.5 %collective-permute-start = (bf16[4,16,768]{2,1,0:T(8,128)(2,1)}, bf16[4,16,768]{2,1,0:T(8,128)(2,1)}, u32[]{:S(2)}, u32[]{:S(2)}) collective-permute-start(bf16[4,16,768]{2,1,0:T(8,128)(2,1)} %get-tuple-element.274), channel_id=1, source_target_pairs={{0,1},{1,2},{2,3},{3,4},{4,5},{5,6},{6,7},{8,9},{9,10},{10,11},{11... | collective-permute-start | bytes 294920 | tf_op jit(solution)/shard_map/ppermute | solution.py:304
  174.3 78.7 %copy-start.84 = (f32[64,64]{1,0:T(8,128)}, f32[64,64]{1,0:T(8,128)S(1)}, u32[]{:S(2)}) copy-start(f32[64,64]{1,0:T(8,128)S(1)} %fusion.266) | copy-start | bytes 49156
  177.8 131.2 %copy-start.123 = (f32[768]{0:T(1024)}, f32[768]{0:T(1024)S(1)}, u32[]{:S(2)}) copy-start(f32[768]{0:T(1024)S(1)} %get-tuple-element.206) | copy-start | bytes 9220
  197.8 52.3 %copy-start.36 = (f32[4,12,64,64]{2,3,1,0:T(8,128)}, f32[4,12,64,64]{2,3,1,0:T(8,128)S(1)}, u32[]{:S(2)}) copy-start(f32[4,12,64,64]{2,3,1,0:T(8,128)S(1)} %get-tuple-element.279) | copy-start | bytes 2359300
  197.8 52.3 %copy-start.101 = (f32[4,12,64]{2,1,0:T(8,128)}, f32[4,12,64]{2,1,0:T(8,128)S(1)}, u32[]{:S(2)}) copy-start(f32[4,12,64]{2,1,0:T(8,128)S(1)} %get-tuple-element.278) | copy-start | bytes 36868
  198.2 52.0 %copy-start.114 = (f32[4,12,64]{2,1,0:T(8,128)}, f32[4,12,64]{2,1,0:T(8,128)S(1)}, u32[]{:S(2)}) copy-start(f32[4,12,64]{2,1,0:T(8,128)S(1)} %fusion.157) | copy-start | bytes 36868
  408.5 116.6 %collective-permute-start.3 = (bf16[4,16,768]{2,1,0:T(8,128)(2,1)}, bf16[4,16,768]{2,1,0:T(8,128)(2,1)}, u32[]{:S(2)}, u32[]{:S(2)}) collective-permute-start(bf16[4,16,768]{2,1,0:T(8,128)(2,1)} %get-tuple-element.273), channel_id=1, source_target_pairs={{0,1},{1,2},{2,3},{3,4},{4,5},{5,6},{6,7},{8,9},{9,10},{10,11},{11... | collective-permute-start | bytes 294920 | tf_op jit(solution)/shard_map/ppermute | solution.py:304
  410.4 114.7 %collective-permute-start.2 = (bf16[4,16,768]{2,1,0:T(8,128)(2,1)}, bf16[4,16,768]{2,1,0:T(8,128)(2,1)}, u32[]{:S(2)}, u32[]{:S(2)}) collective-permute-start(bf16[4,16,768]{2,1,0:T(8,128)(2,1)} %get-tuple-element.272), channel_id=1, source_target_pairs={{1,0},{2,1},{3,2},{4,3},{5,4},{6,5},{7,6},{9,8},{10,9},{11,10},{12... | collective-permute-start | bytes 294920 | tf_op jit(solution)/shard_map/ppermute | solution.py:305
  411.7 293.4 %reduce-scatter.9.cloned.1.call-start = ((), (), s32[]{:S(2)}) async-start(), calls=%async_computation.5 | async-start | bytes 442368
  463.9 61.2 %copy-start.25 = (bf16[512,768]{1,0:T(8,128)(2,1)S(1)}, bf16[512,768]{1,0:T(8,128)(2,1)}, u32[]{:S(2)}) copy-start(bf16[512,768]{1,0:T(8,128)(2,1)} %get-tuple-element.298) | copy-start | bytes 2359300
  474.0 49.7 %copy-start.164 = (f32[768]{0:T(1024)S(1)}, f32[768]{0:T(1024)}, u32[]{:S(2)}) copy-start(f32[768]{0:T(1024)} %get-tuple-element.162) | copy-start | bytes 9220
  525.0 194.5 %reduce-scatter.7.cloned.1.call-start = ((), (), s32[]{:S(2)}) async-start(), calls=%async_computation.4 | async-start | bytes 442368
  746.9 92.0 %copy-start.118 = (f32[12,24]{0,1:T(8,128)S(1)}, f32[12,24]{0,1:T(8,128)}, u32[]{:S(2)}) copy-start(f32[12,24]{0,1:T(8,128)} %copy-done.117) | copy-start | bytes 3460
  746.9 92.0 %copy-start.121 = (f32[12,24]{0,1:T(8,128)S(1)}, f32[12,24]{0,1:T(8,128)}, u32[]{:S(2)}) copy-start(f32[12,24]{0,1:T(8,128)} %copy.454) | copy-start | bytes 3460
  747.0 92.0 %copy-start.122 = (f32[12,24]{0,1:T(8,128)S(1)}, f32[12,24]{0,1:T(8,128)}, u32[]{:S(2)}) copy-start(f32[12,24]{0,1:T(8,128)} %copy.452) | copy-start | bytes 3460
  747.0 94.1 %copy-start.158 = (f32[12,33]{1,0:T(8,128)S(1)}, f32[12,33]{1,0:T(8,128)}, u32[]{:S(2)}) copy-start(f32[12,33]{1,0:T(8,128)} %param.27) | copy-start | bytes 4756
  747.0 94.1 %copy-start.180 = (f32[12,33]{1,0:T(8,128)S(1)}, f32[12,33]{1,0:T(8,128)}, u32[]{:S(2)}) copy-start(f32[12,33]{1,0:T(8,128)} %param.39) | copy-start | bytes 4756
  747.0 94.1 %copy-start.181 = (f32[12,33]{1,0:T(8,128)S(1)}, f32[12,33]{1,0:T(8,128)}, u32[]{:S(2)}) copy-start(f32[12,33]{1,0:T(8,128)} %param.38) | copy-start | bytes 4756
  747.0 94.8 %copy-start.5 = (f32[24,2304]{1,0:T(8,128)S(1)}, f32[24,2304]{1,0:T(8,128)}, u32[]{:S(2)}) copy-start(f32[24,2304]{1,0:T(8,128)} %refs_0_.1) | copy-start | bytes 663556
  747.0 94.7 %copy-start.110 = (f32[24,2304]{1,0:T(8,128)S(1)}, f32[24,2304]{1,0:T(8,128)}, u32[]{:S(2)}) copy-start(f32[24,2304]{1,0:T(8,128)} %param.29) | copy-start | bytes 663556
  747.0 94.7 %copy-start.111 = (f32[24,2304]{1,0:T(8,128)S(1)}, f32[24,2304]{1,0:T(8,128)}, u32[]{:S(2)}) copy-start(f32[24,2304]{1,0:T(8,128)} %param.28) | copy-start | bytes 663556
  (186 other events, 972.7 us)
Sparse Core Ops, SparseCore 0:
  168.5 55.5 all-reduce.5
  411.8 55.2 all-reduce.7
  525.1 28.5 reduce-scatter.8
  690.9 28.5 reduce-scatter.6

commit v2 on v0

--- a/solution.py
+++ b/solution.py
@@ -1,6 +1,10 @@
+import functools
+
 import jax
 import jax.numpy as jnp
 from jax import lax
+from jax.experimental import pallas as pl
+from jax.experimental.pallas import tpu as pltpu
 from jax.sharding import PartitionSpec as P
 
 LAND = 64
@@ -72,7 +76,7 @@
     return (new_first, new_second, weight - step_rate * (update + decay_coef * weight))
 
 
-def on_device(
+def with_collectives(
     tokens,
     cotangent,
     qkv_weight,
@@ -357,6 +361,1001 @@
     return (out_tokens, input_grad) + new_qkv + new_out + new_up + new_down + new_vec + new_taps
 
 
+BF = jnp.bfloat16
+F32 = jnp.float32
+MESH = pl.DeviceIdType.MESH
+
+
+def remote(src, dst, send_sem, recv_sem, device):
+    return pltpu.make_async_remote_copy(
+        src_ref=src, dst_ref=dst, send_sem=send_sem, recv_sem=recv_sem,
+        device_id=device, device_id_type=MESH,
+    )
+
+
+def place():
+    row, spot = lax.axis_index("rows"), lax.axis_index("seq")
+    line, core = spot // 2, spot % 2
+    flip_one = row + 1 - 2 * (row % 2)
+    flip_two = row + 2 - 4 * (row // 2)
+    first = (1 - core) * flip_one + core * flip_two
+    second = (1 - core) * flip_two + core * flip_one
+    return row, line, core, first, second, 3 - row
+
+
+def greet(devices):
+    barrier = pltpu.get_barrier_semaphore()
+    for device in devices:
+        pl.semaphore_signal(barrier, inc=1, device_id=device, device_id_type=MESH)
+    pl.semaphore_wait(barrier, len(devices))
+
+
+def gather_kernel(line_size, n_w, *refs):
+    ins, outs = refs[:n_w], refs[n_w : 2 * n_w]
+    asm, stage = refs[2 * n_w : 3 * n_w], refs[3 * n_w : 4 * n_w]
+    send, recv, local = refs[4 * n_w :]
+    row, line, core, first, second, across = place()
+    own_spot, sibling = 2 * line + core, (row, 2 * line + 1 - core)
+    peers = [(row, 2 * ((line + k) % line_size) + core) for k in range(1, line_size)]
+    to_first, to_second = (first, own_spot), (second, own_spot)
+    greet(peers + [to_first, to_second, sibling])
+    rows = [x.shape[0] for x in ins]
+    half = [x.shape[1] // 2 for x in ins]
+    started = []
+
+    def go(w, k, src, dst, device):
+        copy = remote(src, dst, send.at[w, k], recv.at[w, k], device)
+        copy.start()
+        started.append(copy)
+        return copy
+
+    def cols(w, which):
+        return pl.ds(pl.multiple_of(which * half[w], 128), half[w])
+
+    def slab(w, index):
+        size = 2 * rows[w] * line_size
+        return outs[w].at[pl.ds(pl.multiple_of(index * size, size), size), cols(w, core)]
+
+    asm_copy, z_copy, own_copy, hop, sib = {}, {}, {}, {}, {}
+    z0 = line_size
+    for w in range(n_w):
+        part = pl.ds(pl.multiple_of(core * rows[w], 8), rows[w])
+        asm_copy[w] = go(w, 0, ins[w].at[:, cols(w, 1 - core)], asm[w].at[part, :], sibling)
+        asm[w][part, :] = ins[w][:, cols(w, core)]
+
+    def spread(w):
+        asm_copy[w].wait_recv()
+        stage[w][...] = asm[w][...].astype(BF)
+        size = 2 * rows[w]
+        at = pl.ds(pl.multiple_of((row * line_size + line) * size, size), size)
+        block = outs[w].at[at, cols(w, core)]
+        z_copy[w] = [go(w, 1 + k, stage[w], block, peers[k]) for k in range(line_size - 1)]
+        own_copy[w] = pltpu.make_async_copy(stage[w], block, local.at[w])
+        own_copy[w].start()
+
+    def step_one(w):
+        own_copy[w].wait()
+        for copy in z_copy[w]:
+            copy.wait_recv()
+        mine = slab(w, row)
+        hop[w] = [go(w, z0, mine, mine, to_first), go(w, z0 + 1, mine, mine, to_second)]
+        sib[w] = [go(w, z0 + 3, mine, mine, sibling)]
+
+    def step_two(w):
+        hop[w][0].wait_recv()
+        got = slab(w, first)
+        hop[w].append(go(w, z0 + 2, got, got, to_second))
+        sib[w].append(go(w, z0 + 4, got, got, sibling))
+
+    def step_three(w):
+        hop[w][1].wait_recv()
+        got = slab(w, second)
+        sib[w].append(go(w, z0 + 5, got, got, sibling))
+        hop[w][2].wait_recv()
+        got = slab(w, across)
+        sib[w].append(go(w, z0 + 6, got, got, sibling))
+
+    for w in range(n_w):
+        spread(w)
+    for t in range(n_w + 2):
+        if t < n_w:
+            step_one(t)
+        if 0 <= t - 1 < n_w:
+            step_two(t - 1)
+        if 0 <= t - 2 < n_w:
+            step_three(t - 2)
+    for w in range(n_w):
+        for copy in sib[w]:
+            copy.wait_recv()
+    for copy in started:
+        copy.wait_send()
+
+
+def gather_weights(shards, seq_size):
+    line_size, n_w = seq_size // 2, len(shards)
+    n_dev = 4 * seq_size
+    n_sem = line_size + 7
+    vmem = pl.BlockSpec(memory_space=pltpu.VMEM)
+    return pl.pallas_call(
+        functools.partial(gather_kernel, line_size, n_w),
+        out_shape=[jax.ShapeDtypeStruct((n_dev * x.shape[0], x.shape[1]), BF) for x in shards],
+        in_specs=[vmem] * n_w,
+        out_specs=[pl.BlockSpec(memory_space=pltpu.HBM)] * n_w,
+        scratch_shapes=[pltpu.VMEM((2 * x.shape[0], x.shape[1] // 2), F32) for x in shards]
+        + [pltpu.VMEM((2 * x.shape[0], x.shape[1] // 2), BF) for x in shards]
+        + [
+            pltpu.SemaphoreType.DMA((n_w, n_sem)),
+            pltpu.SemaphoreType.DMA((n_w, n_sem)),
+            pltpu.SemaphoreType.DMA((n_w,)),
+        ],
+        compiler_params=pltpu.CompilerParams(
+            collective_id=0, has_side_effects=True, vmem_limit_bytes=32 * 1024 * 1024
+        ),
+        name="gather_weights",
+    )(*shards)
+
+
+def scatter_kernel(line_size, n_w, *refs):
+    ins, outs = refs[:n_w], refs[n_w : 2 * n_w]
+    acc, buf0, buf1, buf2, buf3, fin = [refs[(2 + i) * n_w : (3 + i) * n_w] for i in range(6)]
+    send, recv, local = refs[8 * n_w :]
+    row, line, core, first, second, across = place()
+    own_spot, sibling = 2 * line + core, (row, 2 * line + 1 - core)
+    peers = [(row, 2 * ((line + k) % line_size) + core) for k in range(1, line_size)]
+    to_first, to_second = (first, own_spot), (second, own_spot)
+    greet(peers + [to_first, to_second, sibling])
+    rows = [x.shape[0] for x in outs]
+    half = [x.shape[1] // 2 for x in ins]
+    started = []
+    copies = {}
+
+    def go(w, k, src, dst, device):
+        copy = remote(src, dst, send.at[w, k], recv.at[w, k], device)
+        copy.start()
+        started.append(copy)
+        return copy
+
+    def cols(w, which):
+        return pl.ds(pl.multiple_of(which * half[w], 128), half[w])
+
+    def size(w):
+        return 2 * rows[w] * line_size
+
+    def slab(w, index):
+        return pl.ds(pl.multiple_of(index * size(w), size(w)), size(w))
+
+    def add(w, index, other, other_start):
+        step = 48
+        base = index * size(w)
+
+        def one(i, carry):
+            at = pl.ds(pl.multiple_of(base + i * step, 16), step)
+            there = pl.ds(pl.multiple_of(other_start + i * step, 16), step)
+            acc[w][at, :] = acc[w][at, :] + other[there, :]
+            return carry
+
+        lax.fori_loop(0, size(w) // step, one, 0)
+
+    def open_up(w):
+        copies[w, 0] = go(w, 0, ins[w].at[:, cols(w, 1 - core)], buf0[w], sibling)
+        copies[w, "own"] = pltpu.make_async_copy(ins[w].at[:, cols(w, core)], acc[w], local.at[w])
+        copies[w, "own"].start()
+
+    def step_one(w):
+        copies[w, "own"].wait()
+        copies[w, 0].wait_recv()
+        add(w, across, buf0[w], across * size(w))
+        copies[w, 1] = go(w, 1, acc[w].at[slab(w, across), :], buf1[w].at[0], to_second)
+        add(w, second, buf0[w], second * size(w))
+        copies[w, 2] = go(w, 2, acc[w].at[slab(w, second), :], buf1[w].at[1], to_second)
+        add(w, first, buf0[w], first * size(w))
+        add(w, row, buf0[w], row * size(w))
+
+    def step_two(w):
+        copies[w, 1].wait_recv()
+        add(w, first, buf1[w].at[0], 0)
+        copies[w, 3] = go(w, 3, acc[w].at[slab(w, first), :], buf2[w], to_first)
+        copies[w, 2].wait_recv()
+        add(w, row, buf1[w].at[1], 0)
+
+    def step_three(w):
+        copies[w, 3].wait_recv()
+        add(w, row, buf2[w], 0)
+        block = 2 * rows[w]
+        for k in range(1, line_size):
+            there = (line + k) % line_size
+            at = pl.ds(pl.multiple_of((row * line_size + there) * block, block), block)
+            copies[w, 3 + k] = go(w, 3 + k, acc[w].at[at, :], buf3[w].at[line], peers[k - 1])
+        at = pl.ds(pl.multiple_of((row * line_size + line) * block, block), block)
+        buf3[w][line] = acc[w][at, :]
+
+    def step_four(w):
+        for k in range(1, line_size):
+            copies[w, 3 + k].wait_recv()
+        total = buf3[w][0].astype(F32)
+        for k in range(1, line_size):
+            total = total + buf3[w][k].astype(F32)
+        fin[w][...] = total
+        part = pl.ds(pl.multiple_of((1 - core) * rows[w], 8), rows[w])
+        copies[w, 9] = go(w, 3 + line_size, fin[w].at[part, :], outs[w].at[:, cols(w, core)], sibling)
+        part = pl.ds(pl.multiple_of(core * rows[w], 8), rows[w])
+        outs[w][:, cols(w, core)] = fin[w][part, :]
+
+    for w in range(n_w):
+        open_up(w)
+    for t in range(n_w + 3):
+        if t < n_w:
+            step_one(t)
+        if 0 <= t - 1 < n_w:
+            step_two(t - 1)
+        if 0 <= t - 2 < n_w:
+            step_three(t - 2)
+        if 0 <= t - 3 < n_w:
+            step_four(t - 3)
+    for w in range(n_w):
+        copies[w, 9].wait_recv()
+    for copy in started:
+        copy.wait_send()
+
+
+def scatter_grads(grads, seq_size):
+    line_size, n_w = seq_size // 2, len(grads)
+    n_dev = 4 * seq_size
+    n_sem = line_size + 4
+    rows = [x.shape[0] // n_dev for x in grads]
+    half = [x.shape[1] // 2 for x in grads]
+    kinds = [x.dtype for x in grads]
+    vmem = pl.BlockSpec(memory_space=pltpu.VMEM)
+    every = range(n_w)
+    quarter = [2 * rows[w] * line_size for w in every]
+    return pl.pallas_call(
+        functools.partial(scatter_kernel, line_size, n_w),
+        out_shape=[jax.ShapeDtypeStruct((rows[w], 2 * half[w]), F32) for w in every],
+        in_specs=[pl.BlockSpec(memory_space=pltpu.HBM)] * n_w,
+        out_specs=[vmem] * n_w,
+        scratch_shapes=[pltpu.VMEM((4 * quarter[w], half[w]), kinds[w]) for w in every]
+        + [pltpu.VMEM((4 * quarter[w], half[w]), kinds[w]) for w in every]
+        + [pltpu.VMEM((2, quarter[w], half[w]), kinds[w]) for w in every]
+        + [pltpu.VMEM((quarter[w], half[w]), kinds[w]) for w in every]
+        + [pltpu.VMEM((line_size, 2 * rows[w], half[w]), kinds[w]) for w in every]
+        + [pltpu.VMEM((2 * rows[w], half[w]), F32) for w in every]
+        + [
+            pltpu.SemaphoreType.DMA((n_w, n_sem)),
+            pltpu.SemaphoreType.DMA((n_w, n_sem)),
+            pltpu.SemaphoreType.DMA((n_w,)),
+        ],
+        compiler_params=pltpu.CompilerParams(
+            collective_id=1, has_side_effects=True, vmem_limit_bytes=48 * 1024 * 1024
+        ),
+        name="scatter_grads",
+    )(*grads)
+
+
+PAIR = 128
+
+
+def nn(a, b):
+    return jnp.dot(a, b, preferred_element_type=F32)
+
+
+def nt(a, b):
+    return lax.dot_general(a, b, (((1,), (1,)), ((), ())), preferred_element_type=F32)
+
+
+def tn(a, b):
+    return lax.dot_general(a, b, (((0,), (0,)), ((), ())), preferred_element_type=F32)
+
+
+def split(x):
+    high = x.astype(BF)
+    return high, (x - high.astype(F32)).astype(BF)
+
+
+def three(dot, a, b):
+    return dot(a[0], b[0]) + (dot(a[0], b[1]) + dot(a[1], b[0]))
+
+
+def lane_masks(dtype):
+    lane = lax.broadcasted_iota(jnp.int32, (1, PAIR), 1)
+    one = (lane < PAIR // 2).astype(F32)
+    return one.astype(dtype), (1.0 - one).astype(dtype)
+
+
+def apart(x):
+    one, two = lane_masks(x.dtype)
+    return jnp.concatenate([x * one, x * two], axis=0)
+
+
+def together(x):
+    half = PAIR // 2
+    lane = lax.broadcasted_iota(jnp.int32, (half, PAIR), 1)
+    return jnp.where(lane < half, x[:half], x[half:])
+
+
+def same_head():
+    half = PAIR // 2
+    a = lax.broadcasted_iota(jnp.int32, (PAIR, PAIR), 0) // half
+    b = lax.broadcasted_iota(jnp.int32, (PAIR, PAIR), 1) // half
+    return a == b
+
+
+def eye():
+    a = lax.broadcasted_iota(jnp.int32, (PAIR, PAIR), 0)
+    b = lax.broadcasted_iota(jnp.int32, (PAIR, PAIR), 1)
+    return (a == b).astype(F32)
+
+
+def by_head(x, reduce):
+    half, width = PAIR // 2, x.shape[1]
+    parts = [reduce(x[h * half : (h + 1) * half], axis=0, keepdims=True) for h in (0, 1)]
+    return jnp.concatenate([jnp.broadcast_to(y, (half, width)) for y in parts], axis=0)
+
+
+def lanes(p):
+    if isinstance(p, int):
+        return pl.ds(p * PAIR, PAIR)
+    return pl.ds(pl.multiple_of(p * PAIR, PAIR), PAIR)
+
+
+def conv_pair(table, padded):
+    size = table.shape[0] // 4
+    out = nn(table, padded)
+    lane = lax.broadcasted_iota(jnp.int32, (size, PAIR), 1)
+    return jnp.where(
+        lane < PAIR // 2,
+        out[:size] + out[2 * size : 3 * size],
+        out[size : 2 * size] + out[3 * size :],
+    )
+
+
+class Group:
+    def __init__(self, send, recv):
+        self.row, self.me = lax.axis_index("rows"), lax.axis_index("seq")
+        self.size = lax.axis_size("seq")
+        self.send, self.recv, self.started = send, recv, []
+
+    def peers(self):
+        return [(self.row, (self.me + k) % self.size) for k in range(1, self.size)]
+
+    def push(self, channel, pick_src, dst):
+        copies = []
+        for k, device in enumerate(self.peers()):
+            copy = remote(
+                pick_src(device[1]), dst, self.send.at[channel, k], self.recv.at[channel, k], device
+            )
+            copy.start()
+            copies.append(copy)
+        self.started += copies
+        return copies
+
+    def halo(self, channel, source, padded, reach):
+        length = source.shape[1]
+        copies = []
+        for which, (src_at, dst_at, step) in enumerate(
+            ((length - reach, 0, 1), (0, length + reach, -1))
+        ):
+            there = (self.me + step + self.size) % self.size
+            copy = remote(
+                source.at[:, pl.ds(src_at, reach), :],
+                padded.at[:, pl.ds(dst_at, reach), :],
+                self.send.at[channel, which],
+                self.recv.at[channel, which],
+                (self.row, there),
+            )
+            goes = self.me < self.size - 1 if step == 1 else self.me > 0
+            comes = self.me > 0 if step == 1 else self.me < self.size - 1
+            pl.when(goes)(copy.start)
+            copies.append((copy, goes, comes, dst_at))
+
+        def arrive():
+            for copy, goes, comes, dst_at in copies:
+                pl.when(comes)(copy.wait_recv)
+
+                @pl.when(jnp.logical_not(comes))
+                def _():
+                    shape = (padded.shape[0], reach, padded.shape[2])
+                    padded[:, pl.ds(dst_at, reach), :] = jnp.zeros(shape, padded.dtype)
+
+        def sent():
+            for copy, goes, _, _ in copies:
+                pl.when(goes)(copy.wait_send)
+
+        return arrive, sent
+
+    def finish(self):
+        for copy in self.started:
+            copy.wait_send()
+
+
+def pinv_start(prob):
+    total = by_head(jnp.sum(prob * prob, axis=1, keepdims=True), jnp.sum)
+    return prob.T / total
+
+
+def pinv_terms(p, z, unit):
+    product = three(nn, p, z)
+    prod = split(product)
+    term_one = 7.0 * unit - product
+    term_two = 15.0 * unit - three(nn, prod, split(term_one))
+    term_three = 13.0 * unit - three(nn, prod, split(term_two))
+    return prod, term_one, term_two, term_three
+
+
+def attend_kernel(
+    reach, q, k, v, table,
+    attn, vpad, landq, landk, mix, p1, e, wt, p2o, zo, lvo,
+    lb, numer, nrecv, stat, srecv, mstat, conv, fcol, send, recv,
+):
+    group = Group(send, recv)
+    me, size = group.me, group.size
+    n_seq, length, width = q.shape
+    pairs = width // PAIR
+    own = n_seq * pairs // size
+    each = width // (pairs // own)
+    land_local = LAND // size
+    seg = length // land_local
+    scale = (PAIR // 2) ** -0.5
+    greet(group.peers())
+
+    def owner_seq(d):
+        return d * own // pairs
+
+    def owner_lanes(d):
+        return pl.ds(pl.multiple_of((d * own % pairs) * PAIR, PAIR), each)
+
+    halo_in, halo_sent = group.halo(0, v, vpad, reach)
+
+    def own_landmarks(s, carry):
+        both = [
+            jnp.mean(x[s].astype(F32).reshape(land_local, seg, width), axis=1) for x in (q, k)
+        ]
+        lb[me, s] = jnp.concatenate(both, axis=0).astype(BF)
+        vpad[s, pl.ds(reach, length), :] = v[s]
+        return carry
+
+    lax.fori_loop(0, n_seq, own_landmarks, 0)
+    landed = group.push(1, lambda d: lb.at[me], lb.at[me])
+    for copy in landed:
+        copy.wait_recv()
+
+    def whole_landmarks(s, carry):
+        x = lb[:, s].astype(F32)
+        landq[s] = x[:, :land_local].reshape(LAND, width).astype(BF)
+        landk[s] = x[:, land_local:].reshape(LAND, width).astype(BF)
+        return carry
+
+    lax.fori_loop(0, n_seq, whole_landmarks, 0)
+    lane_at = lax.broadcasted_iota(jnp.int32, (PAIR, PAIR), 1)
+
+    def over_tokens(s, tile):
+        for p in range(pairs):
+            score = nt(apart(landq[s, :, lanes(p)]), k[s, :, lanes(p)]) * scale
+            top = jnp.max(score, axis=1, keepdims=True)
+            expo = jnp.exp(score - top)
+            low = expo.astype(BF)
+            e[s * pairs + p] = low
+            numer[s, :, lanes(p)] = together(nn(low, v[s, :, lanes(p)])).astype(BF)
+            unit = s * pairs + p
+            at = (unit // own) * 8 + unit % own
+            tile = jnp.where(lane_at == at, top, tile)
+            tile = jnp.where(lane_at == at + own, jnp.sum(expo, axis=1, keepdims=True), tile)
+        return tile
+
+    tile = lax.fori_loop(0, n_seq, over_tokens, jnp.zeros((PAIR, PAIR), F32))
+    stat[...] = tile.T[: 8 * size].reshape(size, 8, PAIR)
+    sums_in = group.push(
+        2, lambda d: numer.at[owner_seq(d), :, owner_lanes(d)], nrecv.at[me]
+    )
+    stats_in = group.push(3, lambda d: stat.at[d], srecv.at[me])
+    nrecv[me] = numer[owner_seq(me), :, owner_lanes(me)]
+    srecv[me] = stat[me]
+
+    block, unit_matrix = same_head(), eye()
+    my_seq, my_pair = owner_seq(me), (me * own) % pairs
+    for i in range(own):
+        at = lanes(my_pair + i)
+        score = nt(apart(landq[my_seq, :, at]), apart(landk[my_seq, :, at])) * scale
+        score = jnp.where(block, score, -1e30)
+        expo = jnp.exp(score - jnp.max(score, axis=1, keepdims=True))
+        prob = expo / jnp.sum(expo, axis=1, keepdims=True)
+        p2o[i] = prob
+        zo[0, i] = pinv_start(prob)
+
+    halo_in()
+    per_step = n_seq * pairs // PINV_ITERS
+
+    def over_landmarks(unit):
+        s, p = unit // pairs, unit % pairs
+        score = nt(apart(landk[s, :, lanes(p)]), q[s, :, lanes(p)]) * scale
+        expo = jnp.exp(score - by_head(score, jnp.max))
+        p1[unit] = expo / by_head(expo, jnp.sum)
+        conv[s, :, lanes(p)] = conv_pair(table[p], vpad[s, :, lanes(p)])
+
+    def pinv_step(step, carry):
+        for i in range(own):
+            z = split(zo[step, i])
+            _, _, _, inner = pinv_terms(split(p2o[i]), z, unit_matrix)
+            zo[step + 1, i] = 0.25 * three(nn, z, split(inner))
+        for j in range(per_step):
+            over_landmarks(step * per_step + j)
+        return carry
+
+    lax.fori_loop(0, PINV_ITERS, pinv_step, 0)
+
+    for copy in sums_in + stats_in:
+        copy.wait_recv()
+    got = srecv[...]
+    tops = got[:, :own]
+    top = jnp.max(tops, axis=0, keepdims=True)
+    factor = jnp.exp(tops - top)
+    total = jnp.sum(factor * got[:, own : 2 * own], axis=0, keepdims=True)
+    factor = factor / total
+    spare = jnp.zeros((1, 8 - 2 * own, PAIR), F32)
+    mstat[me] = jnp.concatenate([top, total, spare], axis=1)[0]
+    spread = jnp.concatenate([factor, jnp.zeros((size, 8 - own, PAIR), F32)], axis=1)
+    spread = spread.reshape(8 * size, PAIR)
+    fcol[...] = jnp.concatenate([spread, jnp.zeros((PAIR - 8 * size, PAIR), F32)], axis=0).T
+    half = PAIR // 2
+    narrow = lax.broadcasted_iota(jnp.int32, (half, PAIR), 1) < half
+    for i in range(own):
+        at = pl.ds(i * PAIR, PAIR)
+        mean = jnp.zeros((half, PAIR), F32)
+        for src in range(size):
+            column = fcol[:, src * 8 + i : src * 8 + i + 1]
+            weight = jnp.where(narrow, column[:half], column[half:])
+            mean = mean + weight * nrecv[src, :, at].astype(F32)
+        lvo[:, at] = mean
+        mixed = together(three(nn, split(zo[PINV_ITERS, i]), split(apart(mean))))
+        mix[my_seq, :, lanes(my_pair + i)] = mixed.astype(BF)
+    mine = mix.at[my_seq, :, owner_lanes(me)]
+    mix_in = group.push(4, lambda d: mine, mine)
+    back_in = group.push(5, lambda d: mstat.at[me], mstat.at[me])
+    for copy in mix_in + back_in:
+        copy.wait_recv()
+
+    rows = jnp.concatenate(
+        [mstat[...].reshape(8 * size, PAIR), jnp.zeros((PAIR - 8 * size, PAIR), F32)], axis=0
+    )
+    rows = rows.T
+    valid = (lane_at % 8 < own) & (lane_at < 8 * size)
+    shift = jnp.where(valid, tile - rows, 0.0)
+    den = jnp.where(valid, pltpu.roll(rows, PAIR - own, 1), 1.0)
+    wt[...] = jnp.exp(shift) / den
+
+    def result(s, carry):
+        for p in range(pairs):
+            low = p1[s * pairs + p].astype(BF)
+            out = tn(low, apart(mix[s, :, lanes(p)])) + conv[s, :, lanes(p)]
+            attn[s, :, lanes(p)] = out.astype(BF)
+        return carry
+
+    lax.fori_loop(0, n_seq, result, 0)
+    halo_sent()
+    group.finish()
+
+
+def attend(q, k, v, table, seq_size, reach):
+    n_seq, length, width = q.shape
+    pairs = width // PAIR
+    units = n_seq * pairs
+    own = units // seq_size
+    vmem = pl.BlockSpec(memory_space=pltpu.VMEM)
+    shape = jax.ShapeDtypeStruct
+    land = shape((n_seq, LAND, width), BF)
+    return pl.pallas_call(
+        functools.partial(attend_kernel, reach),
+        out_shape=[
+            shape(q.shape, BF), shape((n_seq, length + 2 * reach, width), BF), land, land, land,
+            shape((units, PAIR, length), F32), shape((units, PAIR, length), BF),
+            shape((PAIR, PAIR), F32), shape((own, PAIR, PAIR), F32),
+            shape((PINV_ITERS + 1, own, PAIR, PAIR), F32), shape((LAND, own * PAIR), F32),
+        ],
+        in_specs=[vmem] * 4,
+        out_specs=[vmem] * 11,
+        scratch_shapes=[
+            pltpu.VMEM((seq_size, n_seq, 2 * LAND // seq_size, width), BF),
+            pltpu.VMEM((n_seq, LAND, width), BF),
+            pltpu.VMEM((seq_size, LAND, own * PAIR), BF),
+            pltpu.VMEM((seq_size, 8, PAIR), F32),
+            pltpu.VMEM((seq_size, 8, PAIR), F32),
+            pltpu.VMEM((seq_size, 8, PAIR), F32),
+            pltpu.VMEM((n_seq, length, width), F32),
+            pltpu.VMEM((PAIR, PAIR), F32),
+            pltpu.SemaphoreType.DMA((6, seq_size)),
+            pltpu.SemaphoreType.DMA((6, seq_size)),
+        ],
+        compiler_params=pltpu.CompilerParams(
+            collective_id=2, has_side_effects=True, vmem_limit_bytes=48 * 1024 * 1024
+        ),
+        name="attend",
+    )(q, k, v, table)
+
+
+def bands(taps, length, reach, flip):
+    heads, count = taps.shape
+    width = length + 2 * reach
+    line = taps[:, ::-1] if flip else taps
+    line = jnp.pad(line, ((0, 0), (0, width + 1 - count)))
+    rows = jnp.tile(line, (1, length))[:, : length * width].reshape(heads, length, width)
+    high = rows.astype(BF)
+    low = (rows - high.astype(F32)).astype(BF)
+    both = jnp.stack([high, low], axis=1).reshape(heads // 2, 2, 2, length, width)
+    return jnp.swapaxes(both, 1, 2).reshape(heads // 2, 4 * length, width)
+
+
+def attend_back_kernel(
+    reach, n_taps, ga, q, k, vpad, table, landq, landk, mix, p1, e, wt, p2o, zo, lvo,
+    grad, tapg,
+    gpad, gmix, gmr, low, gfull, stat, mstat, gcol, gq, gv, lkp, lpart, lpr, two, twr, dz, dp,
+    skew, own_g, send, recv,
+):
+    group = Group(send, recv)
+    me, size = group.me, group.size
+    n_seq, length, width = q.shape
+    pairs = width // PAIR
+    own = n_seq * pairs // size
+    each = own * PAIR
+    land_local = LAND // size
+    seg = length // land_local
+    half = PAIR // 2
+    scale = half**-0.5
+    greet(group.peers())
+
+    def owner_seq(d):
+        return d * own // pairs
+
+    def owner_lanes(d):
+        return pl.ds(pl.multiple_of((d * own % pairs) * PAIR, PAIR), each)
+
+    halo_in, halo_sent = group.halo(0, ga, gpad, reach)
+
+    def first(s, carry):
+        for p in range(pairs):
+            unit, at = s * pairs + p, lanes(p)
+            own_ga = ga[s, :, at]
+            gpad[s, pl.ds(reach, length), at] = own_ga
+            prob = p1[unit]
+            gmix[s, :, at] = together(nn(prob.astype(BF), own_ga)).astype(BF)
+            back = nt(apart(mix[s, :, at]), own_ga)
+            low[unit] = (prob * (back - by_head(prob * back, jnp.sum))).astype(BF)
+        return carry
+
+    lax.fori_loop(0, n_seq, first, 0)
+    gmix_in = group.push(1, lambda d: gmix.at[owner_seq(d), :, owner_lanes(d)], gmr.at[me])
+    gmr[me] = gmix[owner_seq(me), :, owner_lanes(me)]
+    halo_in()
+    skew[...] = jnp.zeros(skew.shape, F32)
+
+    def beside(s, carry):
+        one, two_mask = lane_masks(BF)
+        for p in range(pairs):
+            unit, at = s * pairs + p, lanes(p)
+            own_ga, padded = ga[s, :, at], vpad[s, :, at]
+            gs = low[unit]
+            gq[s, :, at] = tn(gs, apart(landk[s, :, at])) * scale
+            lkp[s, :, at] = together(nn(gs, q[s, :, at])) * scale
+            gv[s, :, at] = conv_pair(table[p], gpad[s, :, at])
+            both = jnp.concatenate([own_ga * one, own_ga * two_mask], axis=0)
+            skew[2 * p : 2 * p + 2, :, : length + 2 * reach] += nt(both, padded).reshape(
+                2, length, length + 2 * reach
+            )
+        return carry
+
+    lax.fori_loop(0, n_seq, beside, 0)
+    lane_at = lax.broadcasted_iota(jnp.int32, (PAIR, PAIR), 1)
+    wide = skew.shape[2]
+    for h in range(2 * pairs):
+        total = skew[h, :8, :]
+        for row in range(8, length, 8):
+            total = total + pltpu.roll(skew[h, row : row + 8, :], wide - row, 1)
+        tapg[h] = total[:, :PAIR]
+
+    for copy in gmix_in:
+        copy.wait_recv()
+    my_seq, my_pair = owner_seq(me), (me * own) % pairs
+    tile = jnp.zeros((PAIR, PAIR), F32)
+    for i in range(own):
+        at = pl.ds(i * PAIR, PAIR)
+        total = gmr[0, :, at].astype(F32)
+        for src in range(1, size):
+            total = total + gmr[src, :, at].astype(F32)
+        total = split(apart(total))
+        means = apart(lvo[:, at])
+        back = together(three(tn, split(zo[PINV_ITERS, i]), total)).astype(BF)
+        own_g[:, at] = back
+        column = jnp.sum(apart(back.astype(F32)) * means, axis=1, keepdims=True)
+        tile = jnp.where(lane_at == i, column, tile)
+        dz[i] = three(nt, total, split(means))
+        dp[i] = jnp.zeros((PAIR, PAIR), F32)
+    stat[...] = tile.T[:8]
+    mstat[me] = stat[...]
+    gfull[my_seq, :, owner_lanes(me)] = own_g[...]
+    g_in = group.push(2, lambda d: own_g, gfull.at[my_seq, :, owner_lanes(me)])
+    back_in = group.push(3, lambda d: stat, mstat.at[me])
+    for copy in g_in + back_in:
+        copy.wait_recv()
+    rows = jnp.concatenate(
+        [mstat[...].reshape(8 * size, PAIR), jnp.zeros((PAIR - 8 * size, PAIR), F32)], axis=0
+    )
+    gcol[...] = rows.T
+    unit_matrix = eye()
+
+    def third(unit):
+        s, p = unit // pairs, unit % pairs
+        at = lanes(p)
+        here = (unit // own) * 8 + unit % own
+        picked = lane_at == here
+        weight = jnp.sum(jnp.where(picked, wt[...], 0.0), axis=1, keepdims=True)
+        offset = jnp.sum(jnp.where(picked, gcol[...], 0.0), axis=1, keepdims=True)
+        g = apart(gfull[s, :, at])
+        prob = e[unit].astype(F32) * weight
+        back = nt(g, vpad[s, pl.ds(reach, length), at]) - offset
+        gs = (prob * back).astype(BF)
+        gv[s, :, at] += tn(prob.astype(BF), g)
+        grad[s, :, pl.ds(pl.multiple_of(width + p * PAIR, PAIR), PAIR)] = (
+            tn(gs, apart(landq[s, :, at])) * scale
+        ).astype(BF)
+        lq = (together(nn(gs, k[s, :, at])) * scale).reshape(size, land_local, PAIR)
+        lk = lkp[s, :, at].reshape(size, land_local, PAIR)
+        lpart[:, s, :, at] = jnp.concatenate([lq, lk], axis=1).astype(BF)
+
+    per_step = n_seq * pairs // PINV_ITERS
+
+    def pinv_back(step, carry):
+        at_step = PINV_ITERS - 1 - step
+        for i in range(own):
+            p, z = split(p2o[i]), split(zo[at_step, i])
+            prod, one, two_term, three_term = pinv_terms(p, z, unit_matrix)
+            d_out = dz[i] * 0.25
+            d_out_s = split(d_out)
+            d_three = split(three(tn, z, d_out_s))
+            d_two = split(-three(tn, prod, d_three))
+            d_one = -three(tn, prod, d_two)
+            d_prod = -three(nt, d_three, split(two_term)) - three(nt, d_two, split(one)) - d_one
+            d_prod = split(d_prod)
+            dp[i] += three(nt, d_prod, z)
+            dz[i] = three(nt, d_out_s, split(three_term)) + three(tn, p, d_prod)
+        for j in range(per_step):
+            third(step * per_step + j)
+        return carry
+
+    lax.fori_loop(0, PINV_ITERS, pinv_back, 0)
+
+    for i in range(own):
+        at = pl.ds(i * PAIR, PAIR)
+        prob = p2o[i]
+        squares = by_head(jnp.sum(prob * prob, axis=1, keepdims=True), jnp.sum)
+        d_start = dz[i].T
+        inner = by_head(jnp.sum(d_start * prob, axis=1, keepdims=True), jnp.sum)
+        d_prob = dp[i] + d_start / squares - 2.0 * prob * inner / (squares * squares)
+        gs = prob * (d_prob - jnp.sum(prob * d_prob, axis=1, keepdims=True))
+        gs = split(gs)
+        here = lanes(my_pair + i)
+        lq, lk = apart(landq[my_seq, :, here]), apart(landk[my_seq, :, here])
+        query = together(nn(gs[0], lk) + nn(gs[1], lk)) * scale
+        key = together(tn(gs[0], lq) + tn(gs[1], lq)) * scale
+        both = [x.reshape(size, land_local, PAIR) for x in (query, key)]
+        two[:, :, at] = jnp.concatenate(both, axis=1).astype(BF)
+    lpr[me] = lpart[me]
+    twr[me] = two[me]
+    part_in = group.push(4, lambda d: lpart.at[d], lpr.at[me])
+    two_in = group.push(5, lambda d: two.at[d], twr.at[me])
+    for copy in part_in + two_in:
+        copy.wait_recv()
+
+    def close(s, carry):
+        for p in range(pairs):
+            at = lanes(p)
+            total = lpr[0, s, :, at].astype(F32)
+            for src in range(1, size):
+                total = total + lpr[src, s, :, at].astype(F32)
+            owner = s * pairs + p
+            spot = pl.ds(pl.multiple_of((owner % own) * PAIR, PAIR), PAIR)
+            total = (total + twr[owner // own, :, spot].astype(F32)) * (1.0 / seg)
+            spread = [
+                jnp.concatenate(
+                    [jnp.broadcast_to(x[i : i + 1], (seg, PAIR)) for i in range(land_local)], axis=0
+                )
+                for x in (total[:land_local], total[land_local:])
+            ]
+            grad[s, :, at] = (gq[s, :, at] + spread[0]).astype(BF)
+            key_at = pl.ds(width + p * PAIR, PAIR)
+            grad[s, :, key_at] = (grad[s, :, key_at].astype(F32) + spread[1]).astype(BF)
+            grad[s, :, pl.ds(2 * width + p * PAIR, PAIR)] = gv[s, :, at].astype(BF)
+        return carry
+
+    lax.fori_loop(0, n_seq, close, 0)
+    halo_sent()
+    group.finish()
+
+
+def attend_back(ga, q, k, vpad, table, landq, landk, mix, p1, e, wt, p2o, zo, lvo, seq_size, reach):
+    n_seq, length, width = q.shape
+    pairs = width // PAIR
+    units = n_seq * pairs
+    own = units // seq_size
+    vmem = pl.BlockSpec(memory_space=pltpu.VMEM)
+    shape = jax.ShapeDtypeStruct
+    part = 2 * LAND // seq_size
+    return pl.pallas_call(
+        functools.partial(attend_back_kernel, reach, 2 * reach + 1),
+        out_shape=[shape((n_seq, length, 3 * width), BF), shape((2 * pairs, 8, PAIR), F32)],
+        in_specs=[vmem] * 14,
+        out_specs=[vmem] * 2,
+        scratch_shapes=[
+            pltpu.VMEM((n_seq, length + 2 * reach, width), BF),
+            pltpu.VMEM((n_seq, LAND, width), BF),
+            pltpu.VMEM((seq_size, LAND, own * PAIR), BF),
+            pltpu.VMEM((units, PAIR, length), BF),
+            pltpu.VMEM((n_seq, LAND, width), BF),
+            pltpu.VMEM((8, PAIR), F32),
+            pltpu.VMEM((seq_size, 8, PAIR), F32),
+            pltpu.VMEM((PAIR, PAIR), F32),
+            pltpu.VMEM((n_seq, length, width), F32),
+            pltpu.VMEM((n_seq, length, width), F32),
+            pltpu.VMEM((n_seq, LAND, width), F32),
+            pltpu.VMEM((seq_size, n_seq, part, width), BF),
+            pltpu.VMEM((seq_size, n_seq, part, width), BF),
+            pltpu.VMEM((seq_size, part, own * PAIR), BF),
+            pltpu.VMEM((seq_size, part, own * PAIR), BF),
+            pltpu.VMEM((own, PAIR, PAIR), F32),
+            pltpu.VMEM((own, PAIR, PAIR), F32),
+            pltpu.VMEM((2 * pairs, length, 2 * PAIR), F32),
+            pltpu.VMEM((LAND, own * PAIR), BF),
+            pltpu.SemaphoreType.DMA((6, seq_size)),
+            pltpu.SemaphoreType.DMA((6, seq_size)),
+        ],
+        compiler_params=pltpu.CompilerParams(
+            collective_id=3, has_side_effects=True, vmem_limit_bytes=56 * 1024 * 1024
+        ),
+        name="attend_back",
+    )(ga, q, k, vpad, table, landq, landk, mix, p1, e, wt, p2o, zo, lvo)
+
+
+def tap_sums(parts, count):
+    return sum(parts[:, b, b : b + count] for b in range(8))
+
+
+def kernels_fit(args):
+    tokens, _, *matrices = args[:6]
+    taps = args[7]
+    seq_size = lax.axis_size("seq")
+    n_seq, length, width = tokens.shape
+    units = n_seq * width // PAIR
+    own = units // seq_size
+    return (
+        lax.axis_size("rows") == 4
+        and seq_size == 8
+        and all(x.shape[0] % 24 == 0 and x.shape[1] % 256 == 0 for x in matrices)
+        and width // taps.shape[0] == PAIR // 2
+        and length == PAIR
+        and taps.shape[1] == 33
+        and taps.shape[0] <= matrices[0].shape[0]
+        and units == own * seq_size
+        and 2 * own <= 8
+        and (width // PAIR) % own == 0
+        and units % PINV_ITERS == 0
+        and LAND == 8 * seq_size
+    )
+
+
+def all_weights(matrices, vectors):
+    count = vectors.shape[0]
+    table = jnp.pad(vectors.T, ((0, 0), (0, 256 - count)))
+    whole = gather_weights(matrices + (table,), lax.axis_size("seq"))
+    return (*whole[:4], whole[4][:, :count].T)
+
+
+def all_grads(matrices, grad_vec, grad_taps):
+    n_dev = lax.axis_size("rows") * lax.axis_size("seq")
+    count, width = grad_vec.shape
+    heads, taps = grad_taps.shape
+    each = jnp.pad(grad_taps, ((0, width // n_dev - heads), (0, 0)))
+    small = jnp.concatenate([grad_vec.T, jnp.tile(each, (n_dev, 1))], axis=1)
+    small = jnp.pad(small, ((0, 0), (0, 256 - count - taps)))
+    sums = scatter_grads([*matrices, small], lax.axis_size("seq"))
+    return (*sums[:4], sums[4][:, :count].T, sums[4][:heads, count : count + taps])
+
+
+def with_kernels(
+    tokens, cotangent, qkv_weight, out_weight, up_weight, down_weight, vectors, taps,
+    qkv_first, qkv_second, out_first, out_second, up_first, up_second, down_first, down_second,
+    vec_first, vec_second, tap_first, tap_second,
+):
+    seq_count, local_len, model_width = tokens.shape
+    head_count, tap_count = taps.shape
+    hidden_width = up_weight.shape[1]
+    seq_size = lax.axis_size("seq")
+    reach = tap_count // 2
+    row_count = seq_count * local_len
+    full_qkv, full_out, full_up, full_down, full_vec = all_weights(
+        (qkv_weight, out_weight, up_weight, down_weight), vectors
+    )
+    vec_float = full_vec.astype(jnp.float32)
+    flat_in = tokens.reshape(row_count, model_width)
+    project = jnp.dot(flat_in, full_qkv, preferred_element_type=jnp.float32)
+    queries = (project[:, :model_width] + vec_float[0]).astype(BF).reshape(tokens.shape)
+    key_rows = project[:, model_width : 2 * model_width].astype(BF).reshape(tokens.shape)
+    values = (project[:, 2 * model_width :] + vec_float[1]).astype(BF).reshape(tokens.shape)
+    attn, *kept = attend(
+        queries, key_rows, values, bands(taps, local_len, reach, False), seq_size, reach
+    )
+    padded, land_q, land_k, mix, *rest = kept
+    attn_low = attn.reshape(row_count, model_width)
+    branch = jnp.dot(attn_low, full_out, preferred_element_type=jnp.float32) + vec_float[2]
+    resid_one = flat_in.astype(jnp.float32) + branch
+    normed, norm_pull_one = jax.vjp(layer_norm, resid_one, vec_float[6], vec_float[3])
+    normed_low = normed.astype(BF)
+    hidden_pre = jnp.dot(normed_low, full_up, preferred_element_type=jnp.float32) + vec_float[
+        8:
+    ].reshape(hidden_width)
+    active, gelu_pull = jax.vjp(gelu_exact, hidden_pre)
+    active_low = active.astype(BF)
+    ff_out = jnp.dot(active_low, full_down, preferred_element_type=jnp.float32) + vec_float[4]
+    layer_out, norm_pull_two = jax.vjp(layer_norm, normed + ff_out, vec_float[7], vec_float[5])
+    grad_resid_two, grad_gain_two, grad_shift_two = norm_pull_two(
+        cotangent.reshape(row_count, model_width).astype(jnp.float32)
+    )
+    grad_ff = grad_resid_two.astype(BF)
+    grad_down = jnp.einsum("nf,nd->fd", active_low, grad_ff, preferred_element_type=jnp.float32)
+    grad_active = jnp.einsum("nd,fd->nf", grad_ff, full_down, preferred_element_type=jnp.float32)
+    grad_hidden = gelu_pull(grad_active)[0].astype(BF)
+    grad_up = jnp.einsum("nd,nf->df", normed_low, grad_hidden, preferred_element_type=jnp.float32)
+    grad_normed = (
+        jnp.einsum("nf,df->nd", grad_hidden, full_up, preferred_element_type=jnp.float32)
+        + grad_resid_two
+    )
+    grad_resid_one, grad_gain_one, grad_shift_one = norm_pull_one(grad_normed)
+    grad_branch = grad_resid_one.astype(BF)
+    grad_out = jnp.einsum("nd,ne->de", attn_low, grad_branch, preferred_element_type=jnp.float32)
+    grad_attn = jnp.einsum(
+        "ne,de->nd", grad_branch, full_out, preferred_element_type=jnp.float32
+    ).astype(BF)
+    grad_proj, tap_parts = attend_back(
+        grad_attn.reshape(tokens.shape), queries, key_rows, padded,
+        bands(taps, local_len, reach, True), land_q, land_k, mix, *rest, seq_size, reach,
+    )
+    grad_proj = grad_proj.reshape(row_count, 3 * model_width)
+    grad_qkv = jnp.einsum("nd,ne->de", flat_in, grad_proj, preferred_element_type=jnp.float32)
+    input_grad = (
+        jnp.einsum("ne,de->nd", grad_proj, full_qkv, preferred_element_type=jnp.float32)
+        + grad_resid_one
+    )
+    input_grad = input_grad.astype(BF).reshape(tokens.shape)
+    bias_sums = jnp.sum(grad_proj.astype(jnp.float32), axis=0)
+    grad_vec = jnp.concatenate(
+        [
+            bias_sums[None, :model_width],
+            bias_sums[None, 2 * model_width :],
+            jnp.sum(grad_branch.astype(jnp.float32), axis=0)[None],
+            grad_shift_one[None],
+            jnp.sum(grad_ff.astype(jnp.float32), axis=0)[None],
+            grad_shift_two[None],
+            grad_gain_one[None],
+            grad_gain_two[None],
+            jnp.sum(grad_hidden.astype(jnp.float32), axis=0).reshape(-1, model_width),
+        ],
+        axis=0,
+    )
+    summed_qkv, summed_out, summed_up, summed_down, summed_vec, summed_taps = all_grads(
+        [x.astype(BF) for x in (grad_qkv, grad_out, grad_up, grad_down)],
+        grad_vec,
+        tap_sums(tap_parts, tap_count),
+    )
+    new_qkv = adam_step(qkv_weight, qkv_first, qkv_second, summed_qkv, rate_matrix, decay_rate)
+    new_out = adam_step(out_weight, out_first, out_second, summed_out, rate_output, decay_rate)
+    new_up = adam_step(up_weight, up_first, up_second, summed_up, rate_matrix, decay_rate)
+    new_down = adam_step(down_weight, down_first, down_second, summed_down, rate_matrix, decay_rate)
+    new_vec = adam_step(vectors, vec_first, vec_second, summed_vec, rate_vector, 0.0)
+    new_taps = adam_step(taps, tap_first, tap_second, summed_taps, rate_taps, 0.0)
+    out_tokens = layer_out.astype(BF).reshape(tokens.shape)
+    return (out_tokens, input_grad) + new_qkv + new_out + new_up + new_down + new_vec + new_taps
+
+
+def on_device(*args):
+    return with_kernels(*args) if kernels_fit(args) else with_collectives(*args)
+
+
 def solution(mesh):
     return jax.shard_map(
         on_device,

time: 1130 us -> 440 us (0.39)
  waiting for transfers between devices: 420 us -> 0 us
  Pallas kernels: 0 us -> 316 us
  matrix products: 310 us -> 59.7 us
  blocking collectives: 171 us -> 0 us
  other arithmetic: 89.7 us -> 14.4 us
  local copies, waits for them, and re-layouts: 103 us -> 40.6 us
  between operations: 17.4 us -> 1.69 us
    pallas_call x0 -> x4, Pallas kernels: none -> 316 us  [the longest x1 95.2 us: scatter_grads(): pl.pallas_call(functools.partial(scatter_kernel, line_size, n_w), out_sha...]
    reduce_scatter x4 -> x0, waiting for transfers between devices: 291 us -> none  [the longest x1 139 us: on_device(): lax.psum_scatter(grad_down, ('rows', 'seq'), scatter_dimension=0, tiled=T...]
    dot_general x101 -> x12, matrix products: 306 us -> 59.7 us  [the longest x1 18.2 us: with_kernels(): jnp.dot(normed_low, full_up, preferred_element_type=jnp.float32)]
    all_gather x4 -> x0, waiting for transfers between devices: 79.8 us -> none  [the longest x1 45.4 us: on_device(): lax.all_gather(down_weight.astype(jnp.bfloat16), ('rows', 'seq'), axis=0,...]
    all_gather x3 -> x0, blocking collectives: 73.8 us -> none  [the longest x1 43.9 us: on_device(): lax.all_gather(vectors.astype(jnp.bfloat16), ('rows', 'seq'), axis=1, til...]
    psum x2 -> x0, waiting for transfers between devices: 49.1 us -> none  [the longest x1 49.1 us: on_device(): lax.psum(mixing_part.astype(jnp.bfloat16), 'seq').astype(jnp.float32)]
    unnamed x1 -> x0, blocking collectives: 42.5 us -> none
    unnamed x432 -> x135, local copies, waits for them, and re-layouts: 50 us -> 13.6 us
  transfers between devices with their start and end apart: 16 -> 0, of which waited for: 7 -> 0; matrix products, arithmetic and copies ran while one was open for 38% -> 0% of each run, Pallas kernels for 0% -> 0%
where the time goes in v2:
time: 440 us; the launch traced here: 433 us
  Pallas kernels  316 us (72%)
  matrix products  59.7 us (14%)
  local copies, waits for them, and re-layouts  40.6 us (9%)
  other arithmetic  14.4 us (3%)
    pallas_call x1, Pallas kernels, scatter_grads(): pl.pallas_call(functools.partial(scatter_kernel, line_size, n_w), out_sha...  95.2 us
    pallas_call x1, Pallas kernels, gather_weights(): pl.pallas_call(functools.partial(gather_kernel, line_size, n_w), out_shap...  81.9 us
    pallas_call x1, Pallas kernels, attend_back(): pl.pallas_call(functools.partial(attend_back_kernel, reach, 2 * reach + 1...  77.3 us
    pallas_call x1, Pallas kernels, attend(): pl.pallas_call(functools.partial(attend_kernel, reach), out_shape=[shape(...  61.8 us
    dot_general x1, matrix products, with_kernels(): jnp.dot(normed_low, full_up, preferred_element_type=jnp.float32)  18.2 us
    unnamed x135, local copies, waits for them, and re-layouts  13.6 us
    dot_general x1, matrix products, with_kernels(): jnp.einsum('nd,fd->nf', grad_ff, full_down, preferred_element_type=jnp.fl...  9.05 us

profile of v2, /device:TPU:0, one launch (start us, length us, event | category | flops | bytes accessed | tf_op | source)
XLA Modules:
  0.0 432.6 jit_solution(4120046114528167656)
XLA Ops:
  5.2 81.9 %gather_weights.1 = (bf16[768,2304]{1,0:T(8,128)(2,1)S(1)}, bf16[768,768]{1,0:T(8,128)(2,1)S(1)}, bf16[768,3072]{1,0:T(8,128)(2,1)S(1)}, bf16[3072,768]{1,0:T(8,128)(2,1)S(1)}, bf16[768,256]{1,0:T(8,128)(2,1)S(1)}) custom-call(f32[24,2304]{1,0:T(8,128)S(1)} %copy-done.6, f32[24,768]{1,0:T(8,128)S(1)} %copy-done.12, f32[24,3072]{1,0:T(8,128)S(1)} %copy-done.2, ...), custom_call_target="tpu_custom_call" | custom-call | tf_op jit(solution)/shard_map/gather_weights/pallas_call | solution.py:479
  87.1 2.1 copy-done.17
  89.2 2.1 copy-done.18
  92.4 2.2 slice_reduce_fusion.1
  98.6 3.2 convolution_bitcast_fusion
  103.9 3.4 tile.13
  107.3 2.5 slice.114
  109.8 3.3 reshape.242
  113.1 2.2 subtract_convert_fusion.1
  117.0 61.8 %attend.1 = (bf16[4,128,768]{2,1,0:T(8,128)(2,1)S(1)}, bf16[4,160,768]{2,1,0:T(8,128)(2,1)}, bf16[4,64,768]{2,1,0:T(8,128)(2,1)S(1)}, bf16[4,64,768]{2,1,0:T(8,1...) custom-call(bf16[4,128,768]{2,1,0:T(8,128)(2,1)S(1)} %bitcast.74, ...), custom_call_target="tpu_custom_call" | custom-call | tf_op jit(solution)/shard_map/attend/pallas_call | solution.py:945
  180.6 18.2 %multiply_convert_fusion = (bf16[512,3072]{1,0:T(8,128)(2,1)S(1)}, f32[512,3072]{1,0:T(8,128)}, f32[512,3072]{1,0:T(8,128)}) fusion(f32[3072]{0:T(1024)S(1)} %copy-done.47, bf16[768,3072]{1,0:T(8,128)(2,1)S(1)} %bitcast.80, f32[512,768]{1,0:T(8,128)S(1)} %get-tuple-element.219, f32[768]{0:T(1024)S(1)} %copy-done.52, f32[768]{0:T(1024)S(1)} %copy-done.46, ...), kind=kOutput, calls=%fused_computation.5 | convolution fusion | flops 2521694208 | bytes 22042624 | tf_op jit(solution)/shard_map/dot_general | solution.py:1289
  198.9 2.8 fusion.38
  204.6 9.1 %convert_reduce_fusion = (f32[3072]{0:T(1024)S(1)}, bf16[512,3072]{1,0:T(8,128)(2,1)}) fusion(f32[512,3072]{1,0:T(8,128)} %get-tuple-element.210, f32[512,3072]{1,0:T(8,128)} %get-tuple-element.220, f32[3072]{0:T(1024)S(1)} %copy-done.47, bf16[512,768]{1,0:T(8,128)(2,1)S(1)} %get-tuple-element.200, bf16[3072,768]{1,0:T(8,128)(2,1)S(1)} %bitcast.82), kind=kOutput, calls=%fused_computation.3 | convolution fusion | flops 2442654720 | bytes 21258240 | tf_op jit(solution)/shard_map/nd,fd->nf/dot_general | solution.py:1301
  213.7 5.0 %multiply_reduce_fusion = (f32[768]{0:T(1024)S(1)}, f32[512]{0:T(512)S(1)}, f32[768]{0:T(1024)S(1)}, f32[512,768]{1,0:T(8,128)S(1)}) fusion(f32[512,768]{1,0:T(8,128)S(1)} %get-tuple-element.219, f32[512]{0:T(512)S(1)} %fusion.21, f32[512]{0:T(512)S(1)} %broadcast_multiply_fusion.1, f32[768]{0:T(1024)S(1)} %copy-done.46, ...), kind=kOutput, calls=%fused_computation.40 | convolution fusion | flops 2419849216 | bytes 12600320 | tf_op jit(solution)/shard_map/nf,df->nd/dot_general | solution.py:1305
  221.5 2.0 tile.30
  223.5 2.5 slice.122
  226.0 2.1 reshape.247
  230.1 77.3 %attend_back.1 = (bf16[4,128,2304]{2,1,0:T(8,128)(2,1)}, f32[12,8,128]{2,1,0:T(8,128)}) custom-call(bf16[4,128,768]{2,1,0:T(8,128)(2,1)} %bitcast.89, bf16[4,128,768]{2,1,0:T(8,128)(2,1)} %bitcast.75, bf16[4,128,768]{2,1,0:T(8,128)(2,1)} %bitcast.77, bf16[4,160,768]{2,1,0:T(8,128)(2,1)} %get-tuple-element.49.vpad, bf16[6,512,160]{2,1,0:T(8,128)(2,1)} %bitcast.85, ...), custom_call_target="tpu_custom_call" | custom-call | tf_op jit(solution)/shard_map/attend_back/pallas_call | solution.py:1180
  307.4 4.7 %add_convert_fusion.1 = bf16[512,768]{1,0:T(8,128)(2,1)} fusion(f32[512,768]{1,0:T(8,128)S(1)} %copy-done.27, bf16[512,2304]{1,0:T(8,128)(2,1)} %bitcast.87, bf16[768,2304]{1,0:T(8,128)(2,1)S(1)} %copy-done.20, f32[512]{0:T(512)S(1)} %negate_multiply_fusion.1), kind=kOutput, calls=%fused_computation.43 | convolution fusion | flops 1813118976 | bytes 8259584 | tf_op jit(solution)/shard_map/ne,de->nd/dot_general | solution.py:1321
  312.2 3.9 fusion.6.refs_0_
  317.5 5.0 %convolution_convert_fusion.1.refs_2_ = bf16[768,3072]{1,0:T(8,128)(2,1)} fusion(bf16[512,3072]{1,0:T(8,128)(2,1)S(1)} %copy-done.57, f32[512,768]{1,0:T(8,128)S(1)} %copy-done.25, f32[768]{0:T(1024)S(1)} %copy-done.52, f32[768]{0:T(1024)S(1)} %copy-done.46, f32[512]{0:T(512)S(1)} %fusion.21, f32[512]{0:T(512)S(1)} %broadcast_multiply_fusion.1), kind=kOutput, calls=%fused_computation.20 | convolution fusion | flops 2420244480 | bytes 9447424 | tf_op jit(solution)/shard_map/nd,nf->df/dot_general | solution.py:1303
  322.5 4.5 %convolution_convert_fusion.refs_3_ = bf16[3072,768]{1,0:T(8,128)(2,1)} fusion(bf16[512,3072]{1,0:T(8,128)(2,1)S(1)} %copy-done.59, bf16[512,768]{1,0:T(8,128)(2,1)S(1)} %copy-done.30), kind=kOutput, calls=%fused_computation.19 | convolution fusion | flops 2418278400 | bytes 8650752 | tf_op jit(solution)/shard_map/nf,nd->fd/dot_general | solution.py:1300
  327.6 2.1 convert_reduce_fusion.1
  330.4 95.2 %scatter_grads.1 = (f32[24,2304]{1,0:T(8,128)S(1)}, f32[24,768]{1,0:T(8,128)S(1)}, f32[24,3072]{1,0:T(8,128)S(1)}, f32[96,768]{1,0:T(8,128)S(1)}, f32[24,256]{1,0:T(8,128)S(1)}) custom-call(bf16[768,2304]{1,0:T(8,128)(2,1)} %fusion.6.refs_0_, bf16[768,768]{1,0:T(8,128)(2,1)S(1)} %convolution_convert_fusion.2.refs_1_, ...), custom_call_target="tpu_custom_call" | custom-call | tf_op jit(solution)/shard_map/scatter_grads/pallas_call | solution.py:611
  (195 shorter events, 31.7 us)
Async XLA Ops:
  92.4 6.2 %copy-start.19 = (bf16[768,2304]{1,0:T(8,128)(2,1)}, bf16[768,2304]{1,0:T(8,128)(2,1)S(1)}, u32[]{:S(2)}) copy-start(bf16[768,2304]{1,0:T(8,128)(2,1)S(1)} %get-tuple-element.43) | copy-start | bytes 10616836
  102.1 14.8 %copy-start = (bf16[512,768]{1,0:T(8,128)(2,1)}, bf16[512,768]{1,0:T(8,128)(2,1)S(1)}, u32[]{:S(2)}) copy-start(bf16[512,768]{1,0:T(8,128)(2,1)S(1)} %get-tuple-element.214) | copy-start | bytes 2359300
  102.2 14.7 %copy-start.1 = (bf16[512,768]{1,0:T(8,128)(2,1)}, bf16[512,768]{1,0:T(8,128)(2,1)S(1)}, u32[]{:S(2)}) copy-start(bf16[512,768]{1,0:T(8,128)(2,1)S(1)} %slice.153) | copy-start | bytes 2359300
  115.7 64.9 %slice-start = ((s8[4718592]{0:T(1024)(128)(4,1)}), s8[4194304]{0:T(1024)(128)(4,1)S(1)}, s32[]{:S(2)}) async-start(s8[4718592]{0:T(1024)(128)(4,1)} %bitcast.79), calls=%async_computation | async-start | bytes 8388608
  117.0 61.9 %copy-start.22 = (bf16[768,768]{1,0:T(8,128)(2,1)S(1)}, bf16[768,768]{1,0:T(8,128)(2,1)}, u32[]{:S(2)}) copy-start(bf16[768,768]{1,0:T(8,128)(2,1)} %copy-done.21) | copy-start | bytes 3538948
  117.0 62.0 %copy-start.54 = (f32[768]{0:T(1024)S(1)}, f32[768]{0:T(1024)}, u32[]{:S(2)}) copy-start(f32[768]{0:T(1024)} %get-tuple-element.176) | copy-start | bytes 9220
  117.0 62.0 %copy-start.55 = (bf16[4,128,768]{2,1,0:T(8,128)(2,1)S(1)}, bf16[4,128,768]{2,1,0:T(8,128)(2,1)}, u32[]{:S(2)}) copy-start(bf16[4,128,768]{2,1,0:T(8,128)(2,1)} %param.20) | copy-start | bytes 2359300
  117.0 63.5 %slice-start.1 = ((s8[4718592]{0:T(1024)(128)(4,1)}), s8[524288]{0:T(1024)(128)(4,1)S(1)}, s32[]{:S(2)}) async-start(s8[4718592]{0:T(1024)(128)(4,1)} %bitcast.79), calls=%async_computation.1 | async-start | bytes 1048576
  179.0 19.9 %slice-start.2 = ((s8[4718592]{0:T(1024)(128)(4,1)}), s8[524288]{0:T(1024)(128)(4,1)S(1)}, s32[]{:S(2)}) async-start(s8[4718592]{0:T(1024)(128)(4,1)} %bitcast.81), calls=%async_computation.2 | async-start | bytes 1048576
  180.2 38.5 %copy-start.24 = (f32[512,768]{1,0:T(8,128)}, f32[512,768]{1,0:T(8,128)S(1)}, u32[]{:S(2)}) copy-start(f32[512,768]{1,0:T(8,128)S(1)} %get-tuple-element.219) | copy-start | bytes 4718596
  180.6 18.3 %slice-start.3 = ((s8[4718592]{0:T(1024)(128)(4,1)}), s8[4194304]{0:T(1024)(128)(4,1)S(1)}, s32[]{:S(2)}) async-start(s8[4718592]{0:T(1024)(128)(4,1)} %bitcast.81), calls=%async_computation.3 | async-start | bytes 8388608
  180.6 18.3 %copy-start.53 = (f32[768]{0:T(1024)S(1)}, f32[768]{0:T(1024)}, u32[]{:S(2)}) copy-start(f32[768]{0:T(1024)} %get-tuple-element.173) | copy-start | bytes 9220
  204.6 9.1 %copy-start.29 = (bf16[512,768]{1,0:T(8,128)(2,1)}, bf16[512,768]{1,0:T(8,128)(2,1)S(1)}, u32[]{:S(2)}) copy-start(bf16[512,768]{1,0:T(8,128)(2,1)S(1)} %get-tuple-element.200) | copy-start | bytes 2359300
  230.1 77.3 %copy-start.20 = (bf16[768,2304]{1,0:T(8,128)(2,1)S(1)}, bf16[768,2304]{1,0:T(8,128)(2,1)}, u32[]{:S(2)}) copy-start(bf16[768,2304]{1,0:T(8,128)(2,1)} %copy-done.19) | copy-start | bytes 10616836
  230.1 77.3 %copy-start.27 = (f32[512,768]{1,0:T(8,128)S(1)}, f32[512,768]{1,0:T(8,128)}, u32[]{:S(2)}) copy-start(f32[512,768]{1,0:T(8,128)} %copy-done.26) | copy-start | bytes 4718596
  330.3 95.4 %copy-start.7 = (f32[24,2304]{1,0:T(8,128)S(1)}, f32[24,2304]{1,0:T(8,128)}, u32[]{:S(2)}) copy-start(f32[24,2304]{1,0:T(8,128)} %refs_0_.1) | copy-start | bytes 663556
  330.3 95.4 %copy-start.37 = (f32[24,2304]{1,0:T(8,128)S(1)}, f32[24,2304]{1,0:T(8,128)}, u32[]{:S(2)}) copy-start(f32[24,2304]{1,0:T(8,128)} %param.29) | copy-start | bytes 663556
  330.3 95.4 %copy-start.38 = (f32[24,2304]{1,0:T(8,128)S(1)}, f32[24,2304]{1,0:T(8,128)}, u32[]{:S(2)}) copy-start(f32[24,2304]{1,0:T(8,128)} %param.28) | copy-start | bytes 663556
  330.3 96.3 %copy-start.13 = (f32[24,768]{1,0:T(8,128)S(1)}, f32[24,768]{1,0:T(8,128)}, u32[]{:S(2)}) copy-start(f32[24,768]{1,0:T(8,128)} %refs_1_.1) | copy-start | bytes 221188
  330.3 96.3 %copy-start.40 = (f32[24,768]{1,0:T(8,128)S(1)}, f32[24,768]{1,0:T(8,128)}, u32[]{:S(2)}) copy-start(f32[24,768]{1,0:T(8,128)} %param.31) | copy-start | bytes 221188
  330.3 96.3 %copy-start.41 = (f32[24,768]{1,0:T(8,128)S(1)}, f32[24,768]{1,0:T(8,128)}, u32[]{:S(2)}) copy-start(f32[24,768]{1,0:T(8,128)} %param.30) | copy-start | bytes 221188
  330.4 97.0 %copy-start.3 = (f32[24,3072]{1,0:T(8,128)S(1)}, f32[24,3072]{1,0:T(8,128)}, u32[]{:S(2)}) copy-start(f32[24,3072]{1,0:T(8,128)} %refs_2_.1) | copy-start | bytes 884740
  330.4 97.0 %copy-start.33 = (f32[24,3072]{1,0:T(8,128)S(1)}, f32[24,3072]{1,0:T(8,128)}, u32[]{:S(2)}) copy-start(f32[24,3072]{1,0:T(8,128)} %param.33) | copy-start | bytes 884740
  330.4 97.0 %copy-start.34 = (f32[24,3072]{1,0:T(8,128)S(1)}, f32[24,3072]{1,0:T(8,128)}, u32[]{:S(2)}) copy-start(f32[24,3072]{1,0:T(8,128)} %param.32) | copy-start | bytes 884740
  (40 other events, 98.6 us)

commit v3 on v2

--- a/solution.py
+++ b/solution.py
@@ -390,245 +390,193 @@
     pl.semaphore_wait(barrier, len(devices))
 
 
-def gather_kernel(line_size, n_w, *refs):
-    ins, outs = refs[:n_w], refs[n_w : 2 * n_w]
-    asm, stage = refs[2 * n_w : 3 * n_w], refs[3 * n_w : 4 * n_w]
-    send, recv, local = refs[4 * n_w :]
-    row, line, core, first, second, across = place()
-    own_spot, sibling = 2 * line + core, (row, 2 * line + 1 - core)
-    peers = [(row, 2 * ((line + k) % line_size) + core) for k in range(1, line_size)]
-    to_first, to_second = (first, own_spot), (second, own_spot)
-    greet(peers + [to_first, to_second, sibling])
-    rows = [x.shape[0] for x in ins]
-    half = [x.shape[1] // 2 for x in ins]
-    started = []
-
-    def go(w, k, src, dst, device):
-        copy = remote(src, dst, send.at[w, k], recv.at[w, k], device)
+class Net:
+    def __init__(self, send, recv):
+        self.send, self.recv, self.started = send, recv, []
+        self.row, self.line, self.core, self.first, self.second, self.across = place()
+        self.line_size = lax.axis_size("seq") // 2
+        own_spot = 2 * self.line + self.core
+        self.sibling = (self.row, 2 * self.line + 1 - self.core)
+        self.peers = [
+            (self.row, 2 * ((self.line + k) % self.line_size) + self.core)
+            for k in range(1, self.line_size)
+        ]
+        self.to_first, self.to_second = (self.first, own_spot), (self.second, own_spot)
+
+    def go(self, w, k, src, dst, device):
+        copy = remote(src, dst, self.send.at[w, k], self.recv.at[w, k], device)
         copy.start()
-        started.append(copy)
+        self.started.append(copy)
         return copy
 
-    def cols(w, which):
-        return pl.ds(pl.multiple_of(which * half[w], 128), half[w])
-
-    def slab(w, index):
-        size = 2 * rows[w] * line_size
-        return outs[w].at[pl.ds(pl.multiple_of(index * size, size), size), cols(w, core)]
-
-    asm_copy, z_copy, own_copy, hop, sib = {}, {}, {}, {}, {}
-    z0 = line_size
-    for w in range(n_w):
-        part = pl.ds(pl.multiple_of(core * rows[w], 8), rows[w])
-        asm_copy[w] = go(w, 0, ins[w].at[:, cols(w, 1 - core)], asm[w].at[part, :], sibling)
-        asm[w][part, :] = ins[w][:, cols(w, core)]
-
-    def spread(w):
-        asm_copy[w].wait_recv()
-        stage[w][...] = asm[w][...].astype(BF)
-        size = 2 * rows[w]
-        at = pl.ds(pl.multiple_of((row * line_size + line) * size, size), size)
-        block = outs[w].at[at, cols(w, core)]
-        z_copy[w] = [go(w, 1 + k, stage[w], block, peers[k]) for k in range(line_size - 1)]
-        own_copy[w] = pltpu.make_async_copy(stage[w], block, local.at[w])
-        own_copy[w].start()
-
-    def step_one(w):
-        own_copy[w].wait()
-        for copy in z_copy[w]:
+    def finish(self):
+        for copy in self.started:
+            copy.wait_send()
+
+
+def columns(base, which, half):
+    return pl.ds(pl.multiple_of(base + which * half, 128), half)
+
+
+class Gather:
+    def __init__(self, net, w, src, dst, base, half, asm, stage, local):
+        self.net, self.w, self.dst, self.stage, self.asm = net, w, dst, stage, asm
+        self.rows, self.base, self.half, self.local = src.shape[0], base, half, local
+        part = pl.ds(pl.multiple_of(net.core * self.rows, 8), self.rows)
+        there = columns(base, 1 - net.core, half)
+        self.asm_copy = net.go(w, 0, src.at[:, there], asm.at[part, :], net.sibling)
+        asm[part, :] = src[:, columns(base, net.core, half)]
+
+    def block(self, start, size):
+        at = pl.ds(pl.multiple_of(start, 16), size)
+        return self.dst.at[at, columns(self.base, self.net.core, self.half)]
+
+    def slab(self, index):
+        size = 2 * self.rows * self.net.line_size
+        return self.block(index * size, size)
+
+    def spread(self):
+        net = self.net
+        self.asm_copy.wait_recv()
+        self.stage[...] = self.asm[...].astype(BF)
+        size = 2 * self.rows
+        block = self.block((net.row * net.line_size + net.line) * size, size)
+        self.z = [net.go(self.w, 1 + k, self.stage, block, d) for k, d in enumerate(net.peers)]
+        self.own = pltpu.make_async_copy(self.stage, block, self.local)
+        self.own.start()
+
+    def step_one(self):
+        net, w, z0 = self.net, self.w, self.net.line_size
+        self.own.wait()
+        for copy in self.z:
             copy.wait_recv()
-        mine = slab(w, row)
-        hop[w] = [go(w, z0, mine, mine, to_first), go(w, z0 + 1, mine, mine, to_second)]
-        sib[w] = [go(w, z0 + 3, mine, mine, sibling)]
-
-    def step_two(w):
-        hop[w][0].wait_recv()
-        got = slab(w, first)
-        hop[w].append(go(w, z0 + 2, got, got, to_second))
-        sib[w].append(go(w, z0 + 4, got, got, sibling))
-
-    def step_three(w):
-        hop[w][1].wait_recv()
-        got = slab(w, second)
-        sib[w].append(go(w, z0 + 5, got, got, sibling))
-        hop[w][2].wait_recv()
-        got = slab(w, across)
-        sib[w].append(go(w, z0 + 6, got, got, sibling))
-
-    for w in range(n_w):
-        spread(w)
-    for t in range(n_w + 2):
-        if t < n_w:
-            step_one(t)
-        if 0 <= t - 1 < n_w:
-            step_two(t - 1)
-        if 0 <= t - 2 < n_w:
-            step_three(t - 2)
-    for w in range(n_w):
-        for copy in sib[w]:
+        mine = self.slab(net.row)
+        self.hop = [net.go(w, z0, mine, mine, net.to_first)]
+        self.hop.append(net.go(w, z0 + 1, mine, mine, net.to_second))
+        self.sib = [net.go(w, z0 + 3, mine, mine, net.sibling)]
+
+    def step_two(self):
+        net, w, z0 = self.net, self.w, self.net.line_size
+        self.hop[0].wait_recv()
+        got = self.slab(net.first)
+        self.hop.append(net.go(w, z0 + 2, got, got, net.to_second))
+        self.sib.append(net.go(w, z0 + 4, got, got, net.sibling))
+
+    def step_three(self):
+        net, w, z0 = self.net, self.w, self.net.line_size
+        self.hop[1].wait_recv()
+        got = self.slab(net.second)
+        self.sib.append(net.go(w, z0 + 5, got, got, net.sibling))
+        self.hop[2].wait_recv()
+        got = self.slab(net.across)
+        self.sib.append(net.go(w, z0 + 6, got, got, net.sibling))
+
+    def close(self):
+        for copy in self.sib:
             copy.wait_recv()
-    for copy in started:
-        copy.wait_send()
-
-
-def gather_weights(shards, seq_size):
-    line_size, n_w = seq_size // 2, len(shards)
-    n_dev = 4 * seq_size
-    n_sem = line_size + 7
-    vmem = pl.BlockSpec(memory_space=pltpu.VMEM)
-    return pl.pallas_call(
-        functools.partial(gather_kernel, line_size, n_w),
-        out_shape=[jax.ShapeDtypeStruct((n_dev * x.shape[0], x.shape[1]), BF) for x in shards],
-        in_specs=[vmem] * n_w,
-        out_specs=[pl.BlockSpec(memory_space=pltpu.HBM)] * n_w,
-        scratch_shapes=[pltpu.VMEM((2 * x.shape[0], x.shape[1] // 2), F32) for x in shards]
-        + [pltpu.VMEM((2 * x.shape[0], x.shape[1] // 2), BF) for x in shards]
-        + [
-            pltpu.SemaphoreType.DMA((n_w, n_sem)),
-            pltpu.SemaphoreType.DMA((n_w, n_sem)),
-            pltpu.SemaphoreType.DMA((n_w,)),
-        ],
-        compiler_params=pltpu.CompilerParams(
-            collective_id=0, has_side_effects=True, vmem_limit_bytes=32 * 1024 * 1024
-        ),
-        name="gather_weights",
-    )(*shards)
-
-
-def scatter_kernel(line_size, n_w, *refs):
-    ins, outs = refs[:n_w], refs[n_w : 2 * n_w]
-    acc, buf0, buf1, buf2, buf3, fin = [refs[(2 + i) * n_w : (3 + i) * n_w] for i in range(6)]
-    send, recv, local = refs[8 * n_w :]
-    row, line, core, first, second, across = place()
-    own_spot, sibling = 2 * line + core, (row, 2 * line + 1 - core)
-    peers = [(row, 2 * ((line + k) % line_size) + core) for k in range(1, line_size)]
-    to_first, to_second = (first, own_spot), (second, own_spot)
-    greet(peers + [to_first, to_second, sibling])
-    rows = [x.shape[0] for x in outs]
-    half = [x.shape[1] // 2 for x in ins]
-    started = []
-    copies = {}
-
-    def go(w, k, src, dst, device):
-        copy = remote(src, dst, send.at[w, k], recv.at[w, k], device)
-        copy.start()
-        started.append(copy)
-        return copy
-
-    def cols(w, which):
-        return pl.ds(pl.multiple_of(which * half[w], 128), half[w])
-
-    def size(w):
-        return 2 * rows[w] * line_size
-
-    def slab(w, index):
-        return pl.ds(pl.multiple_of(index * size(w), size(w)), size(w))
-
-    def add(w, index, other, other_start):
+
+
+GATHER_SEMS = 7
+
+
+class Scatter:
+    def __init__(self, net, w, out, base, half, bufs):
+        self.net, self.w, self.out, self.base, self.half = net, w, out, base, half
+        self.acc, self.buf0, self.buf1, self.buf2, self.buf3, self.fin = bufs
+        self.rows = out.shape[0]
+        self.size = 2 * self.rows * net.line_size
+
+    def open(self, outbox, own=None):
+        self.sib = self.net.go(self.w, 0, outbox, self.buf0, self.net.sibling)
+        self.own = own
+        if own is not None:
+            own.start()
+
+    def slab(self, index):
+        return pl.ds(pl.multiple_of(index * self.size, self.size), self.size)
+
+    def add(self, index, other, start):
         step = 48
-        base = index * size(w)
+        acc = self.acc
 
         def one(i, carry):
-            at = pl.ds(pl.multiple_of(base + i * step, 16), step)
-            there = pl.ds(pl.multiple_of(other_start + i * step, 16), step)
-            acc[w][at, :] = acc[w][at, :] + other[there, :]
+            at = pl.ds(pl.multiple_of(index * self.size + i * step, 16), step)
+            there = pl.ds(pl.multiple_of(start + i * step, 16), step)
+            acc[at, :] = acc[at, :] + other[there, :]
             return carry
 
-        lax.fori_loop(0, size(w) // step, one, 0)
-
-    def open_up(w):
-        copies[w, 0] = go(w, 0, ins[w].at[:, cols(w, 1 - core)], buf0[w], sibling)
-        copies[w, "own"] = pltpu.make_async_copy(ins[w].at[:, cols(w, core)], acc[w], local.at[w])
-        copies[w, "own"].start()
-
-    def step_one(w):
-        copies[w, "own"].wait()
-        copies[w, 0].wait_recv()
-        add(w, across, buf0[w], across * size(w))
-        copies[w, 1] = go(w, 1, acc[w].at[slab(w, across), :], buf1[w].at[0], to_second)
-        add(w, second, buf0[w], second * size(w))
-        copies[w, 2] = go(w, 2, acc[w].at[slab(w, second), :], buf1[w].at[1], to_second)
-        add(w, first, buf0[w], first * size(w))
-        add(w, row, buf0[w], row * size(w))
-
-    def step_two(w):
-        copies[w, 1].wait_recv()
-        add(w, first, buf1[w].at[0], 0)
-        copies[w, 3] = go(w, 3, acc[w].at[slab(w, first), :], buf2[w], to_first)
-        copies[w, 2].wait_recv()
-        add(w, row, buf1[w].at[1], 0)
-
-    def step_three(w):
-        copies[w, 3].wait_recv()
-        add(w, row, buf2[w], 0)
-        block = 2 * rows[w]
-        for k in range(1, line_size):
-            there = (line + k) % line_size
-            at = pl.ds(pl.multiple_of((row * line_size + there) * block, block), block)
-            copies[w, 3 + k] = go(w, 3 + k, acc[w].at[at, :], buf3[w].at[line], peers[k - 1])
-        at = pl.ds(pl.multiple_of((row * line_size + line) * block, block), block)
-        buf3[w][line] = acc[w][at, :]
-
-    def step_four(w):
-        for k in range(1, line_size):
-            copies[w, 3 + k].wait_recv()
-        total = buf3[w][0].astype(F32)
-        for k in range(1, line_size):
-            total = total + buf3[w][k].astype(F32)
-        fin[w][...] = total
-        part = pl.ds(pl.multiple_of((1 - core) * rows[w], 8), rows[w])
-        copies[w, 9] = go(w, 3 + line_size, fin[w].at[part, :], outs[w].at[:, cols(w, core)], sibling)
-        part = pl.ds(pl.multiple_of(core * rows[w], 8), rows[w])
-        outs[w][:, cols(w, core)] = fin[w][part, :]
-
-    for w in range(n_w):
-        open_up(w)
-    for t in range(n_w + 3):
-        if t < n_w:
-            step_one(t)
-        if 0 <= t - 1 < n_w:
-            step_two(t - 1)
-        if 0 <= t - 2 < n_w:
-            step_three(t - 2)
-        if 0 <= t - 3 < n_w:
-            step_four(t - 3)
-    for w in range(n_w):
-        copies[w, 9].wait_recv()
-    for copy in started:
-        copy.wait_send()
-
-
-def scatter_grads(grads, seq_size):
-    line_size, n_w = seq_size // 2, len(grads)
-    n_dev = 4 * seq_size
-    n_sem = line_size + 4
-    rows = [x.shape[0] // n_dev for x in grads]
-    half = [x.shape[1] // 2 for x in grads]
-    kinds = [x.dtype for x in grads]
-    vmem = pl.BlockSpec(memory_space=pltpu.VMEM)
-    every = range(n_w)
-    quarter = [2 * rows[w] * line_size for w in every]
-    return pl.pallas_call(
-        functools.partial(scatter_kernel, line_size, n_w),
-        out_shape=[jax.ShapeDtypeStruct((rows[w], 2 * half[w]), F32) for w in every],
-        in_specs=[pl.BlockSpec(memory_space=pltpu.HBM)] * n_w,
-        out_specs=[vmem] * n_w,
-        scratch_shapes=[pltpu.VMEM((4 * quarter[w], half[w]), kinds[w]) for w in every]
-        + [pltpu.VMEM((4 * quarter[w], half[w]), kinds[w]) for w in every]
-        + [pltpu.VMEM((2, quarter[w], half[w]), kinds[w]) for w in every]
-        + [pltpu.VMEM((quarter[w], half[w]), kinds[w]) for w in every]
-        + [pltpu.VMEM((line_size, 2 * rows[w], half[w]), kinds[w]) for w in every]
-        + [pltpu.VMEM((2 * rows[w], half[w]), F32) for w in every]
-        + [
-            pltpu.SemaphoreType.DMA((n_w, n_sem)),
-            pltpu.SemaphoreType.DMA((n_w, n_sem)),
-            pltpu.SemaphoreType.DMA((n_w,)),
-        ],
-        compiler_params=pltpu.CompilerParams(
-            collective_id=1, has_side_effects=True, vmem_limit_bytes=48 * 1024 * 1024
-        ),
-        name="scatter_grads",
-    )(*grads)
+        lax.fori_loop(0, self.size // step, one, 0)
+
+    def step_one(self):
+        net, w = self.net, self.w
+        if self.own is not None:
+            self.own.wait()
+        self.sib.wait_recv()
+        self.add(net.across, self.buf0, net.across * self.size)
+        acc = self.acc
+        self.one = net.go(w, 1, acc.at[self.slab(net.across), :], self.buf1.at[0], net.to_second)
+        self.add(net.second, self.buf0, net.second * self.size)
+        self.two = net.go(w, 2, acc.at[self.slab(net.second), :], self.buf1.at[1], net.to_second)
+        self.add(net.first, self.buf0, net.first * self.size)
+        self.add(net.row, self.buf0, net.row * self.size)
+
+    def step_two(self):
+        net = self.net
+        self.one.wait_recv()
+        self.add(net.first, self.buf1.at[0], 0)
+        src = self.acc.at[self.slab(net.first), :]
+        self.three = net.go(self.w, 3, src, self.buf2, net.to_first)
+        self.two.wait_recv()
+        self.add(net.row, self.buf1.at[1], 0)
+
+    def step_three(self):
+        net = self.net
+        self.three.wait_recv()
+        self.add(net.row, self.buf2, 0)
+        block, n = 2 * self.rows, net.line_size
+        self.z = []
+
+        def at(line):
+            return pl.ds(pl.multiple_of((net.row * n + line) * block, block), block)
+
+        for k, device in enumerate(net.peers):
+            src = self.acc.at[at((net.line + 1 + k) % n), :]
+            self.z.append(net.go(self.w, 4 + k, src, self.buf3.at[net.line], device))
+        self.buf3[net.line] = self.acc[at(net.line), :]
+
+    def step_four(self):
+        net = self.net
+        for copy in self.z:
+            copy.wait_recv()
+        total = self.buf3[0].astype(F32)
+        for k in range(1, net.line_size):
+            total = total + self.buf3[k].astype(F32)
+        self.fin[...] = total
+        part = pl.ds(pl.multiple_of((1 - net.core) * self.rows, 8), self.rows)
+        here = columns(self.base, net.core, self.half)
+        self.last = net.go(
+            self.w, 3 + net.line_size, self.fin.at[part, :], self.out.at[:, here], net.sibling
+        )
+        part = pl.ds(pl.multiple_of(net.core * self.rows, 8), self.rows)
+        self.out[:, here] = self.fin[part, :]
+
+    def close(self):
+        self.last.wait_recv()
+
+
+SCATTER_SEMS = 4
+
+
+def scatter_scratch(rows, half, dtype, line_size):
+    quarter = 2 * rows * line_size
+    return [
+        pltpu.VMEM((4 * quarter, half), dtype),
+        pltpu.VMEM((4 * quarter, half), dtype),
+        pltpu.VMEM((2, quarter, half), dtype),
+        pltpu.VMEM((quarter, half), dtype),
+        pltpu.VMEM((line_size, 2 * rows, half), dtype),
+        pltpu.VMEM((2 * rows, half), F32),
+    ]
 
 
 PAIR = 128
@@ -781,21 +729,39 @@
     return prod, term_one, term_two, term_three
 
 
-def attend_kernel(
-    reach, q, k, v, table,
-    attn, vpad, landq, landk, mix, p1, e, wt, p2o, zo, lvo,
-    lb, numer, nrecv, stat, srecv, mstat, conv, fcol, send, recv,
+def band(line, length, reach):
+    wide = jnp.broadcast_to(line, (length, line.shape[1]))
+    return pltpu.roll(wide, 0, 1, stride=1, stride_axis=0)[:, : length + 2 * reach]
+
+
+def fill_bands(lines, table, reach):
+    pairs, rows = table.shape[0], table.shape[1] // 4
+    for p in range(pairs):
+        for h in (0, 1):
+            high, low = split(band(lines[2 * p + h : 2 * p + h + 1, :], rows, reach))
+            table[p, h * rows : (h + 1) * rows, :] = high
+            table[p, (2 + h) * rows : (3 + h) * rows, :] = low
+
+
+def front_kernel(
+    reach,
+    tokens, qkv_w, out_w, up_w, down_w, vec_w, lines,
+    f_qkv, f_out, f_up, f_down, f_rows,
+    q, k, attn, vpad, landq, landk, mix, p1, e, wt, p2o, zo, lvo,
+    v, table, f_vec, lb, numer, nrecv, stat, srecv, mstat, conv, fcol, *rest,
 ):
-    group = Group(send, recv)
+    asm, stage = rest[:7], rest[7:14]
+    g_send, g_recv, g_local, send, recv = rest[14:]
+    net, group = Net(g_send, g_recv), Group(send, recv)
     me, size = group.me, group.size
     n_seq, length, width = q.shape
     pairs = width // PAIR
     own = n_seq * pairs // size
-    each = width // (pairs // own)
+    each = own * PAIR
     land_local = LAND // size
     seg = length // land_local
     scale = (PAIR // 2) ** -0.5
-    greet(group.peers())
+    greet(group.peers() + [net.to_first, net.to_second])
 
     def owner_seq(d):
         return d * own // pairs
@@ -803,7 +769,50 @@
     def owner_lanes(d):
         return pl.ds(pl.multiple_of((d * own % pairs) * PAIR, PAIR), each)
 
-    halo_in, halo_sent = group.halo(0, v, vpad, reach)
+    plan = [(vec_w, f_vec, 0), (qkv_w, f_qkv, width), (qkv_w, f_qkv, 0), (qkv_w, f_qkv, 2 * width)]
+    plan += [(out_w, f_out, 0), (up_w, f_up, 0), (down_w, f_down, 0)]
+    pieces = []
+    for w, (src, dst, base) in enumerate(plan):
+        half = asm[w].shape[1]
+        pieces.append(Gather(net, w, src, dst, base, half, asm[w], stage[w], g_local.at[w]))
+    g_vec, g_k, g_q, g_v, g_out, g_up, g_down = pieces
+    for piece in pieces[:4]:
+        piece.spread()
+    fill_bands(lines, table, reach)
+
+    def project(dst, base, bias):
+        step = 2 * PAIR
+        for at in range(0, width, step):
+            x = nn(tokens[...], f_qkv[:, base + at : base + at + step])
+            if bias is not None:
+                x = x + f_rows[bias : bias + 1, at : at + step]
+            dst[:, :, at : at + step] = x.astype(BF).reshape(n_seq, length, step)
+
+    g_vec.step_one()
+    g_k.step_one()
+    g_q.step_one()
+    g_vec.step_two()
+    g_k.step_two()
+    g_v.step_one()
+    g_out.spread()
+    g_up.spread()
+    g_vec.step_three()
+    g_q.step_two()
+    g_k.step_three()
+    g_down.spread()
+    g_vec.close()
+    f_rows[...] = f_vec[:, :PAIR].astype(F32).T[: f_rows.shape[0]]
+    g_v.step_two()
+    g_k.close()
+    project(k, width, None)
+    g_q.step_three()
+    g_q.close()
+    project(q, 0, 0)
+    g_v.step_three()
+    g_out.step_one()
+    g_up.step_one()
+    g_v.close()
+    project(v, 2 * width, 1)
 
     def own_landmarks(s, carry):
         both = [
@@ -815,6 +824,9 @@
 
     lax.fori_loop(0, n_seq, own_landmarks, 0)
     landed = group.push(1, lambda d: lb.at[me], lb.at[me])
+    halo_in, halo_sent = group.halo(0, v, vpad, reach)
+    g_out.step_two()
+    g_down.step_one()
     for copy in landed:
         copy.wait_recv()
 
@@ -847,6 +859,7 @@
         2, lambda d: numer.at[owner_seq(d), :, owner_lanes(d)], nrecv.at[me]
     )
     stats_in = group.push(3, lambda d: stat.at[d], srecv.at[me])
+    g_up.step_two()
     nrecv[me] = numer[owner_seq(me), :, owner_lanes(me)]
     srecv[me] = stat[me]
 
@@ -880,7 +893,10 @@
             over_landmarks(step * per_step + j)
         return carry
 
-    lax.fori_loop(0, PINV_ITERS, pinv_step, 0)
+    lax.fori_loop(0, PINV_ITERS // 2, pinv_step, 0)
+    g_out.step_three()
+    g_down.step_two()
+    lax.fori_loop(PINV_ITERS // 2, PINV_ITERS, pinv_step, 0)
 
     for copy in sums_in + stats_in:
         copy.wait_recv()
@@ -910,6 +926,7 @@
     mine = mix.at[my_seq, :, owner_lanes(me)]
     mix_in = group.push(4, lambda d: mine, mine)
     back_in = group.push(5, lambda d: mstat.at[me], mstat.at[me])
+    g_up.step_three()
     for copy in mix_in + back_in:
         copy.wait_recv()
 
@@ -930,29 +947,46 @@
         return carry
 
     lax.fori_loop(0, n_seq, result, 0)
+    g_down.step_three()
+    for piece in (g_out, g_up, g_down):
+        piece.close()
     halo_sent()
     group.finish()
-
-
-def attend(q, k, v, table, seq_size, reach):
-    n_seq, length, width = q.shape
+    net.finish()
+
+
+def front(tokens, matrices, table, lines, seq_size, reach):
+    n_seq, length, width = tokens.shape
     pairs = width // PAIR
     units = n_seq * pairs
     own = units // seq_size
-    vmem = pl.BlockSpec(memory_space=pltpu.VMEM)
+    n_dev = 4 * seq_size
+    line_size = seq_size // 2
+    vmem, hbm = pl.BlockSpec(memory_space=pltpu.VMEM), pl.BlockSpec(memory_space=pltpu.HBM)
     shape = jax.ShapeDtypeStruct
     land = shape((n_seq, LAND, width), BF)
+    qkv_w, out_w, up_w, down_w = matrices
+    whole = [shape((n_dev * x.shape[0], x.shape[1]), BF) for x in matrices]
+    asm = [(table.shape[0], table.shape[1] // 2)] + [(qkv_w.shape[0], width // 2)] * 3
+    asm += [(x.shape[0], x.shape[1] // 2) for x in (out_w, up_w, down_w)]
+    n_sem = line_size + GATHER_SEMS
     return pl.pallas_call(
-        functools.partial(attend_kernel, reach),
-        out_shape=[
-            shape(q.shape, BF), shape((n_seq, length + 2 * reach, width), BF), land, land, land,
+        functools.partial(front_kernel, reach),
+        out_shape=whole
+        + [
+            shape((16, width), F32),
+            shape(tokens.shape, BF), shape(tokens.shape, BF), shape(tokens.shape, BF),
+            shape((n_seq, length + 2 * reach, width), BF), land, land, land,
             shape((units, PAIR, length), F32), shape((units, PAIR, length), BF),
             shape((PAIR, PAIR), F32), shape((own, PAIR, PAIR), F32),
             shape((PINV_ITERS + 1, own, PAIR, PAIR), F32), shape((LAND, own * PAIR), F32),
         ],
-        in_specs=[vmem] * 4,
-        out_specs=[vmem] * 11,
+        in_specs=[vmem] * 7,
+        out_specs=[vmem, hbm, hbm, hbm] + [vmem] * 14,
         scratch_shapes=[
+            pltpu.VMEM(tokens.shape, BF),
+            pltpu.VMEM((pairs, 4 * length, length + 2 * reach), BF),
+            pltpu.VMEM((n_dev * table.shape[0], table.shape[1]), BF),
             pltpu.VMEM((seq_size, n_seq, 2 * LAND // seq_size, width), BF),
             pltpu.VMEM((n_seq, LAND, width), BF),
             pltpu.VMEM((seq_size, LAND, own * PAIR), BF),
@@ -961,35 +995,34 @@
             pltpu.VMEM((seq_size, 8, PAIR), F32),
             pltpu.VMEM((n_seq, length, width), F32),
             pltpu.VMEM((PAIR, PAIR), F32),
+        ]
+        + [pltpu.VMEM((2 * r, h), F32) for r, h in asm]
+        + [pltpu.VMEM((2 * r, h), BF) for r, h in asm]
+        + [
+            pltpu.SemaphoreType.DMA((7, n_sem)),
+            pltpu.SemaphoreType.DMA((7, n_sem)),
+            pltpu.SemaphoreType.DMA((7,)),
             pltpu.SemaphoreType.DMA((6, seq_size)),
             pltpu.SemaphoreType.DMA((6, seq_size)),
         ],
         compiler_params=pltpu.CompilerParams(
-            collective_id=2, has_side_effects=True, vmem_limit_bytes=48 * 1024 * 1024
+            collective_id=0, has_side_effects=True, vmem_limit_bytes=56 * 1024 * 1024
         ),
-        name="attend",
-    )(q, k, v, table)
-
-
-def bands(taps, length, reach, flip):
-    heads, count = taps.shape
-    width = length + 2 * reach
-    line = taps[:, ::-1] if flip else taps
-    line = jnp.pad(line, ((0, 0), (0, width + 1 - count)))
-    rows = jnp.tile(line, (1, length))[:, : length * width].reshape(heads, length, width)
-    high = rows.astype(BF)
-    low = (rows - high.astype(F32)).astype(BF)
-    both = jnp.stack([high, low], axis=1).reshape(heads // 2, 2, 2, length, width)
-    return jnp.swapaxes(both, 1, 2).reshape(heads // 2, 4 * length, width)
-
-
-def attend_back_kernel(
-    reach, n_taps, ga, q, k, vpad, table, landq, landk, mix, p1, e, wt, p2o, zo, lvo,
-    grad, tapg,
+        name="front",
+    )(tokens.reshape(n_seq * length, width), *matrices, table, lines)
+
+
+def back_kernel(
+    reach, n_taps,
+    ga, tokens, resid, f_qkv, vec_rows, lines, d_down, d_up, d_out,
+    q, k, vpad, landq, landk, mix, p1, e, wt, p2o, zo, lvo,
+    input_grad, s_qkv, s_out, s_up, s_down, s_small,
+    grad, tapg, table, tok_t, outbox, small_box,
     gpad, gmix, gmr, low, gfull, stat, mstat, gcol, gq, gv, lkp, lpart, lpr, two, twr, dz, dp,
-    skew, own_g, send, recv,
+    skew, own_g, *rest,
 ):
-    group = Group(send, recv)
+    bufs, (g_send, g_recv, g_local, send, recv) = rest[:-5], rest[-5:]
+    net, group = Net(g_send, g_recv), Group(send, recv)
     me, size = group.me, group.size
     n_seq, length, width = q.shape
     pairs = width // PAIR
@@ -999,7 +1032,7 @@
     seg = length // land_local
     half = PAIR // 2
     scale = half**-0.5
-    greet(group.peers())
+    greet(group.peers() + [net.to_first, net.to_second])
 
     def owner_seq(d):
         return d * own // pairs
@@ -1007,6 +1040,38 @@
     def owner_lanes(d):
         return pl.ds(pl.multiple_of((d * own % pairs) * PAIR, PAIR), each)
 
+    plan = [(s_down, 0), (s_up, 0), (s_out, 0)]
+    plan += [(s_qkv, 2 * width), (s_qkv, 0), (s_qkv, width), (s_small, 0)]
+    pieces = []
+    for w, (out, base) in enumerate(plan):
+        own_bufs = bufs[6 * w : 6 * w + 6]
+        pieces.append(Scatter(net, w, out, base, own_bufs[0].shape[1], own_bufs))
+    r_down, r_up, r_out, r_v, r_q, r_k, r_small = pieces
+
+    def open_whole(w, src):
+        piece = pieces[w]
+        other, here = [columns(0, c, piece.half) for c in (1 - net.core, net.core)]
+        own_part = pltpu.make_async_copy(src.at[:, here], piece.acc, g_local.at[w])
+        piece.open(src.at[:, other], own_part)
+
+    def open_weight(piece, box):
+        step = 2 * PAIR
+        rows = tok_t.shape[0]
+
+        def one(i, carry):
+            at = pl.ds(pl.multiple_of(i * step, step), step)
+            x = tok_t[at, :]
+            other, here = [columns(piece.base, c, piece.half) for c in (1 - net.core, net.core)]
+            outbox[box, at, :] = nn(x, grad[:, other]).astype(BF)
+            piece.acc[at, :] = nn(x, grad[:, here]).astype(BF)
+            return carry
+
+        lax.fori_loop(0, rows // step, one, 0)
+        piece.open(outbox.at[box])
+
+    open_whole(0, d_down)
+    open_whole(1, d_up)
+    open_whole(2, d_out)
     halo_in, halo_sent = group.halo(0, ga, gpad, reach)
 
     def first(s, carry):
@@ -1023,6 +1088,9 @@
     lax.fori_loop(0, n_seq, first, 0)
     gmix_in = group.push(1, lambda d: gmix.at[owner_seq(d), :, owner_lanes(d)], gmr.at[me])
     gmr[me] = gmix[owner_seq(me), :, owner_lanes(me)]
+    r_down.step_one()
+    r_up.step_one()
+    fill_bands(lines, table, reach)
     halo_in()
     skew[...] = jnp.zeros(skew.shape, F32)
 
@@ -1049,6 +1117,9 @@
         for row in range(8, length, 8):
             total = total + pltpu.roll(skew[h, row : row + 8, :], wide - row, 1)
         tapg[h] = total[:, :PAIR]
+    r_down.step_two()
+    r_out.step_one()
+    tok_t[...] = tokens[...].T
 
     for copy in gmix_in:
         copy.wait_recv()
@@ -1072,6 +1143,7 @@
     gfull[my_seq, :, owner_lanes(me)] = own_g[...]
     g_in = group.push(2, lambda d: own_g, gfull.at[my_seq, :, owner_lanes(me)])
     back_in = group.push(3, lambda d: stat, mstat.at[me])
+    r_up.step_two()
     for copy in g_in + back_in:
         copy.wait_recv()
     rows = jnp.concatenate(
@@ -1091,8 +1163,12 @@
         prob = e[unit].astype(F32) * weight
         back = nt(g, vpad[s, pl.ds(reach, length), at]) - offset
         gs = (prob * back).astype(BF)
-        gv[s, :, at] += tn(prob.astype(BF), g)
-        grad[s, :, pl.ds(pl.multiple_of(width + p * PAIR, PAIR), PAIR)] = (
+        values = gv[s, :, at] + tn(prob.astype(BF), g)
+        v_at = pl.ds(pl.multiple_of(2 * width + p * PAIR, PAIR), PAIR)
+        rows = pl.ds(pl.multiple_of(s * length, length), length)
+        grad[rows, v_at] = values.astype(BF)
+        rows = pl.ds(pl.multiple_of(s * length, length), length)
+        grad[rows, pl.ds(pl.multiple_of(width + p * PAIR, PAIR), PAIR)] = (
             tn(gs, apart(landq[s, :, at])) * scale
         ).astype(BF)
         lq = (together(nn(gs, k[s, :, at])) * scale).reshape(size, land_local, PAIR)
@@ -1119,7 +1195,11 @@
             third(step * per_step + j)
         return carry
 
-    lax.fori_loop(0, PINV_ITERS, pinv_back, 0)
+    lax.fori_loop(0, PINV_ITERS // 2, pinv_back, 0)
+    r_down.step_three()
+    r_out.step_two()
+    lax.fori_loop(PINV_ITERS // 2, PINV_ITERS, pinv_back, 0)
+    r_up.step_three()
 
     for i in range(own):
         at = pl.ds(i * PAIR, PAIR)
@@ -1140,6 +1220,8 @@
     twr[me] = two[me]
     part_in = group.push(4, lambda d: lpart.at[d], lpr.at[me])
     two_in = group.push(5, lambda d: two.at[d], twr.at[me])
+    open_weight(r_v, 0)
+    r_down.step_four()
     for copy in part_in + two_in:
         copy.wait_recv()
 
@@ -1158,31 +1240,109 @@
                 )
                 for x in (total[:land_local], total[land_local:])
             ]
-            grad[s, :, at] = (gq[s, :, at] + spread[0]).astype(BF)
+            rows = pl.ds(pl.multiple_of(s * length, length), length)
+            grad[rows, at] = (gq[s, :, at] + spread[0]).astype(BF)
             key_at = pl.ds(width + p * PAIR, PAIR)
-            grad[s, :, key_at] = (grad[s, :, key_at].astype(F32) + spread[1]).astype(BF)
-            grad[s, :, pl.ds(2 * width + p * PAIR, PAIR)] = gv[s, :, at].astype(BF)
+            grad[rows, key_at] = (grad[rows, key_at].astype(F32) + spread[1]).astype(BF)
         return carry
 
     lax.fori_loop(0, n_seq, close, 0)
+    open_weight(r_q, 1)
+    r_v.step_one()
+    open_weight(r_k, 2)
+    r_q.step_one()
+    r_out.step_three()
+
+    def column_sums(base):
+        total = jnp.zeros((1, width), F32)
+        for s in range(n_seq):
+            x = grad[s * length : (s + 1) * length, base : base + width].astype(F32)
+            total = total + jnp.sum(x, axis=0, keepdims=True)
+        return total
+
+    count = vec_rows.shape[0]
+    which = lax.broadcasted_iota(jnp.int32, (count, width), 0)
+    table_rows = vec_rows[...]
+    table_rows = jnp.where(which == 0, column_sums(0), table_rows)
+    table_rows = jnp.where(which == 1, column_sums(2 * width), table_rows)
+    table_rows = jnp.concatenate([table_rows, jnp.zeros((PAIR - count, width), F32)], axis=0)
+    left = table_rows.T
+    sums = tapg[:, 0, :]
+    for b in range(1, 8):
+        sums = sums + pltpu.roll(tapg[:, b, :], PAIR - b, 1)
+    shard = r_small.rows
+    sums = jnp.concatenate([sums, jnp.zeros((shard - sums.shape[0], PAIR), F32)], axis=0)
+    right = jnp.broadcast_to(sums[None], (width // shard, shard, PAIR)).reshape(width, PAIR)
+    zero = net.core == 0
+    r_small.acc[...] = jnp.where(zero, left, right)
+    small_box[...] = jnp.where(zero, right, left)
+    r_small.open(small_box)
+    r_v.step_two()
+    r_k.step_one()
+
+    def inputs(i, carry):
+        step = 2 * PAIR
+        rows = pl.ds(pl.multiple_of(i * step, step), step)
+        for at in range(0, width, step):
+            x = nt(grad[rows, :], f_qkv[at : at + step, :])
+            out = x + resid[rows, at : at + step]
+            input_grad[rows, at : at + step] = out.astype(BF)
+        return carry
+
+    lax.fori_loop(0, tokens.shape[0] // (2 * PAIR), inputs, 0)
+    r_small.step_one()
+    r_q.step_two()
+    r_up.step_four()
+    r_out.step_four()
+    r_k.step_two()
+    r_v.step_three()
+    r_small.step_two()
+    r_q.step_three()
+    r_k.step_three()
+    r_v.step_four()
+    r_small.step_three()
+    r_q.step_four()
+    r_k.step_four()
+    r_small.step_four()
+    for piece in pieces:
+        piece.close()
     halo_sent()
     group.finish()
-
-
-def attend_back(ga, q, k, vpad, table, landq, landk, mix, p1, e, wt, p2o, zo, lvo, seq_size, reach):
+    net.finish()
+
+
+def back(
+    ga, tokens, resid, f_qkv, vec_rows, lines, d_down, d_up, d_out, kept, shards, seq_size, reach
+):
+    q = kept[0]
     n_seq, length, width = q.shape
     pairs = width // PAIR
     units = n_seq * pairs
     own = units // seq_size
-    vmem = pl.BlockSpec(memory_space=pltpu.VMEM)
+    line_size = seq_size // 2
+    vmem, hbm = pl.BlockSpec(memory_space=pltpu.VMEM), pl.BlockSpec(memory_space=pltpu.HBM)
     shape = jax.ShapeDtypeStruct
     part = 2 * LAND // seq_size
+    s_qkv, s_out, s_up, s_down = [shape(x.shape, F32) for x in shards]
+    s_small = shape((s_qkv.shape[0], 2 * PAIR), F32)
+    bufs = []
+    for x in (s_down, s_up, s_out):
+        bufs += scatter_scratch(x.shape[0], x.shape[1] // 2, BF, line_size)
+    for _ in range(3):
+        bufs += scatter_scratch(s_qkv.shape[0], width // 2, BF, line_size)
+    bufs += scatter_scratch(s_qkv.shape[0], PAIR, F32, line_size)
     return pl.pallas_call(
-        functools.partial(attend_back_kernel, reach, 2 * reach + 1),
-        out_shape=[shape((n_seq, length, 3 * width), BF), shape((2 * pairs, 8, PAIR), F32)],
-        in_specs=[vmem] * 14,
-        out_specs=[vmem] * 2,
+        functools.partial(back_kernel, reach, 2 * reach + 1),
+        out_shape=[shape(tokens.shape, BF), s_qkv, s_out, s_up, s_down, s_small],
+        in_specs=[vmem] * 6 + [hbm] * 3 + [vmem] * 12,
+        out_specs=[vmem] * 6,
         scratch_shapes=[
+            pltpu.VMEM((n_seq * length, 3 * width), BF),
+            pltpu.VMEM((2 * pairs, 8, PAIR), F32),
+            pltpu.VMEM((pairs, 4 * length, length + 2 * reach), BF),
+            pltpu.VMEM((width, n_seq * length), BF),
+            pltpu.VMEM((3, width, width // 2), BF),
+            pltpu.VMEM((width, PAIR), F32),
             pltpu.VMEM((n_seq, length + 2 * reach, width), BF),
             pltpu.VMEM((n_seq, LAND, width), BF),
             pltpu.VMEM((seq_size, LAND, own * PAIR), BF),
@@ -1202,18 +1362,20 @@
             pltpu.VMEM((own, PAIR, PAIR), F32),
             pltpu.VMEM((2 * pairs, length, 2 * PAIR), F32),
             pltpu.VMEM((LAND, own * PAIR), BF),
+        ]
+        + bufs
+        + [
+            pltpu.SemaphoreType.DMA((7, line_size + SCATTER_SEMS)),
+            pltpu.SemaphoreType.DMA((7, line_size + SCATTER_SEMS)),
+            pltpu.SemaphoreType.DMA((7,)),
             pltpu.SemaphoreType.DMA((6, seq_size)),
             pltpu.SemaphoreType.DMA((6, seq_size)),
         ],
         compiler_params=pltpu.CompilerParams(
-            collective_id=3, has_side_effects=True, vmem_limit_bytes=56 * 1024 * 1024
+            collective_id=1, has_side_effects=True, vmem_limit_bytes=60 * 1024 * 1024
         ),
-        name="attend_back",
-    )(ga, q, k, vpad, table, landq, landk, mix, p1, e, wt, p2o, zo, lvo)
-
-
-def tap_sums(parts, count):
-    return sum(parts[:, b, b : b + count] for b in range(8))
+        name="back",
+    )(ga, tokens, resid, f_qkv, vec_rows, lines, d_down, d_up, d_out, *kept)
 
 
 def kernels_fit(args):
@@ -1239,24 +1401,6 @@
     )
 
 
-def all_weights(matrices, vectors):
-    count = vectors.shape[0]
-    table = jnp.pad(vectors.T, ((0, 0), (0, 256 - count)))
-    whole = gather_weights(matrices + (table,), lax.axis_size("seq"))
-    return (*whole[:4], whole[4][:, :count].T)
-
-
-def all_grads(matrices, grad_vec, grad_taps):
-    n_dev = lax.axis_size("rows") * lax.axis_size("seq")
-    count, width = grad_vec.shape
-    heads, taps = grad_taps.shape
-    each = jnp.pad(grad_taps, ((0, width // n_dev - heads), (0, 0)))
-    small = jnp.concatenate([grad_vec.T, jnp.tile(each, (n_dev, 1))], axis=1)
-    small = jnp.pad(small, ((0, 0), (0, 256 - count - taps)))
-    sums = scatter_grads([*matrices, small], lax.axis_size("seq"))
-    return (*sums[:4], sums[4][:, :count].T, sums[4][:heads, count : count + taps])
-
-
 def with_kernels(
     tokens, cotangent, qkv_weight, out_weight, up_weight, down_weight, vectors, taps,
     qkv_first, qkv_second, out_first, out_second, up_first, up_second, down_first, down_second,
@@ -1268,26 +1412,22 @@
     seq_size = lax.axis_size("seq")
     reach = tap_count // 2
     row_count = seq_count * local_len
-    full_qkv, full_out, full_up, full_down, full_vec = all_weights(
-        (qkv_weight, out_weight, up_weight, down_weight), vectors
-    )
-    vec_float = full_vec.astype(jnp.float32)
+    count = vectors.shape[0]
+    matrices = (qkv_weight, out_weight, up_weight, down_weight)
+    table = jnp.pad(vectors.T, ((0, 0), (0, 2 * PAIR - count)))
+    lines = jnp.pad(taps, ((0, 0), (0, 2 * PAIR - tap_count)))
     flat_in = tokens.reshape(row_count, model_width)
-    project = jnp.dot(flat_in, full_qkv, preferred_element_type=jnp.float32)
-    queries = (project[:, :model_width] + vec_float[0]).astype(BF).reshape(tokens.shape)
-    key_rows = project[:, model_width : 2 * model_width].astype(BF).reshape(tokens.shape)
-    values = (project[:, 2 * model_width :] + vec_float[1]).astype(BF).reshape(tokens.shape)
-    attn, *kept = attend(
-        queries, key_rows, values, bands(taps, local_len, reach, False), seq_size, reach
-    )
-    padded, land_q, land_k, mix, *rest = kept
-    attn_low = attn.reshape(row_count, model_width)
+    full_qkv, full_out, full_up, full_down, vec_float, *kept = front(
+        tokens, matrices, table, lines, seq_size, reach
+    )
+    attn_low = kept.pop(2).reshape(row_count, model_width)
+    queries, key_rows = kept[:2]
     branch = jnp.dot(attn_low, full_out, preferred_element_type=jnp.float32) + vec_float[2]
     resid_one = flat_in.astype(jnp.float32) + branch
     normed, norm_pull_one = jax.vjp(layer_norm, resid_one, vec_float[6], vec_float[3])
     normed_low = normed.astype(BF)
     hidden_pre = jnp.dot(normed_low, full_up, preferred_element_type=jnp.float32) + vec_float[
-        8:
+        8:count
     ].reshape(hidden_width)
     active, gelu_pull = jax.vjp(gelu_exact, hidden_pre)
     active_low = active.astype(BF)
@@ -1311,22 +1451,11 @@
     grad_attn = jnp.einsum(
         "ne,de->nd", grad_branch, full_out, preferred_element_type=jnp.float32
     ).astype(BF)
-    grad_proj, tap_parts = attend_back(
-        grad_attn.reshape(tokens.shape), queries, key_rows, padded,
-        bands(taps, local_len, reach, True), land_q, land_k, mix, *rest, seq_size, reach,
-    )
-    grad_proj = grad_proj.reshape(row_count, 3 * model_width)
-    grad_qkv = jnp.einsum("nd,ne->de", flat_in, grad_proj, preferred_element_type=jnp.float32)
-    input_grad = (
-        jnp.einsum("ne,de->nd", grad_proj, full_qkv, preferred_element_type=jnp.float32)
-        + grad_resid_one
-    )
-    input_grad = input_grad.astype(BF).reshape(tokens.shape)
-    bias_sums = jnp.sum(grad_proj.astype(jnp.float32), axis=0)
-    grad_vec = jnp.concatenate(
+    nothing = jnp.zeros((1, model_width), F32)
+    vec_rows = jnp.concatenate(
         [
-            bias_sums[None, :model_width],
-            bias_sums[None, 2 * model_width :],
+            nothing,
+            nothing,
             jnp.sum(grad_branch.astype(jnp.float32), axis=0)[None],
             grad_shift_one[None],
             jnp.sum(grad_ff.astype(jnp.float32), axis=0)[None],
@@ -1334,14 +1463,19 @@
             grad_gain_one[None],
             grad_gain_two[None],
             jnp.sum(grad_hidden.astype(jnp.float32), axis=0).reshape(-1, model_width),
+            jnp.zeros((16 - count, model_width), F32),
         ],
         axis=0,
     )
-    summed_qkv, summed_out, summed_up, summed_down, summed_vec, summed_taps = all_grads(
-        [x.astype(BF) for x in (grad_qkv, grad_out, grad_up, grad_down)],
-        grad_vec,
-        tap_sums(tap_parts, tap_count),
-    )
+    flipped = jnp.pad(taps[:, ::-1], ((0, 0), (0, 2 * PAIR - tap_count)))
+    input_grad, summed_qkv, summed_out, summed_up, summed_down, small = back(
+        grad_attn.reshape(tokens.shape), flat_in, grad_resid_one, full_qkv, vec_rows, flipped,
+        *[x.astype(BF) for x in (grad_down, grad_up, grad_out)],
+        kept, matrices, seq_size, reach,
+    )
+    input_grad = input_grad.reshape(tokens.shape)
+    summed_vec = small[:, :count].T
+    summed_taps = small[:head_count, PAIR : PAIR + tap_count]
     new_qkv = adam_step(qkv_weight, qkv_first, qkv_second, summed_qkv, rate_matrix, decay_rate)
     new_out = adam_step(out_weight, out_first, out_second, summed_out, rate_output, decay_rate)
     new_up = adam_step(up_weight, up_first, up_second, summed_up, rate_matrix, decay_rate)

time: 440 us -> 330 us (0.75)
  Pallas kernels: 316 us -> 248 us
  local copies, waits for them, and re-layouts: 40.6 us -> 10.1 us
  matrix products: 59.7 us -> 54 us
    pallas_call x4 -> x2, Pallas kernels: 316 us -> 248 us  [the longest x1 142 us: back(): pl.pallas_call(functools.partial(back_kernel, reach, 2 * reach + 1), out_...]
    dot_general x3 -> x0, matrix products: 11.8 us -> none  [the longest x1 4.72 us: with_kernels(): jnp.einsum('ne,de->nd', grad_proj, full_qkv, preferred_element_type=jnp.f...]
    unnamed x135 -> x67, local copies, waits for them, and re-layouts: 13.6 us -> 4.43 us
    another operation x6 -> x0, local copies, waits for them, and re-layouts: 7.2 us -> none  [the longest x4 6.85 us: bands(): jnp.tile(line, (1, length))[:, :length * width]]
    slice x6 -> x1, local copies, waits for them, and re-layouts: 7.82 us -> 0.74 us  [with_kernels(): vec_float[8:count].reshape(hidden_width)]
    reshape x2 -> x0, local copies, waits for them, and re-layouts: 5.44 us -> none  [bands(): jnp.tile(line, (1, length))[:, :length * width]]
where the time goes in v3:
time: 330 us; the launch traced here: 325 us
  Pallas kernels  248 us (75%)
  matrix products  54 us (16%)
  other arithmetic  11.5 us (3%)
  local copies, waits for them, and re-layouts  10.1 us (3%)
    pallas_call x1, Pallas kernels, back(): pl.pallas_call(functools.partial(back_kernel, reach, 2 * reach + 1), out_...  142 us
    pallas_call x1, Pallas kernels, front(): pl.pallas_call(functools.partial(front_kernel, reach), out_shape=whole +...  106 us
    dot_general x1, matrix products, with_kernels(): jnp.dot(normed_low, full_up, preferred_element_type=jnp.float32)  18.6 us
    dot_general x1, matrix products, with_kernels(): jnp.einsum('nd,fd->nf', grad_ff, full_down, preferred_element_type=jnp.fl...  9.26 us
    sub x6, other arithmetic, adam_step(): weight - step_rate * (update + decay_coef * weight)  7.31 us
    dot_general x1, matrix products, with_kernels(): jnp.einsum('nf,nd->fd', active_low, grad_ff, preferred_element_type=jnp.f...  7.01 us

profile of v3, /device:TPU:0, one launch (start us, length us, event | category | flops | bytes accessed | tf_op | source)
XLA Modules:
  0.0 325.0 jit_solution(2056427448696859634)
XLA Ops:
  0.7 0.8 copy.48
  2.0 1.3 pad.12.lines
  3.4 105.6 %front.1 = (bf16[768,2304]{1,0:T(8,128)(2,1)}, bf16[768,768]{1,0:T(8,128)(2,1)}, bf16[768,3072]{1,0:T(8,128)(2,1)}, bf16[3072,768]{1,0:T(8,128)(2,1)}, f32[16,76...) custom-call(bf16[512,768]{1,0:T(8,128)(2,1)} %bitcast.41, ...), custom_call_target="tpu_custom_call" | custom-call | tf_op jit(solution)/shard_map/front/pallas_call | solution.py:973
  109.0 1.0 slice_reduce_fusion.1
  110.0 0.7 slice.30
  110.8 2.8 fusion.35
  113.9 18.6 %multiply_convert_fusion = (bf16[512,3072]{1,0:T(8,128)(2,1)S(1)}, f32[512,3072]{1,0:T(8,128)}, f32[512,3072]{1,0:T(8,128)}) fusion(f32[3072]{0:T(1024)S(1)} %add.183, bf16[768,3072]{1,0:T(8,128)(2,1)S(1)} %copy-done.24, f32[512,768]{1,0:T(8,128)S(1)} %get-tuple-element.151, f32[768]{0:T(1024)S(1)} %get-tuple-element.116, f32[768]{0:T(1024)S(1)} %get-tuple-element.117, ...), kind=kOutput, calls=%fused_computation.4 | convolution fusion | flops 2521694208 | bytes 22042624 | tf_op jit(solution)/shard_map/dot_general | solution.py:1429
  132.6 2.8 fusion.36
  135.8 0.8 fusion.9
  136.5 1.6 fusion.33
  138.4 9.3 %convert_reduce_fusion = (f32[3072]{0:T(1024)S(1)}, bf16[512,3072]{1,0:T(8,128)(2,1)}) fusion(f32[512,3072]{1,0:T(8,128)} %get-tuple-element.148, f32[512,3072]{1,0:T(8,128)} %get-tuple-element.152, f32[3072]{0:T(1024)S(1)} %add.183, bf16[512,768]{1,0:T(8,128)(2,1)S(1)} %get-tuple-element.140, bf16[3072,768]{1,0:T(8,128)(2,1)S(1)} %bitcast.51), kind=kOutput, calls=%fused_computation.2 | convolution fusion | flops 2442654720 | bytes 21258240 | tf_op jit(solution)/shard_map/nd,fd->nf/dot_general | solution.py:1441
  147.6 5.0 %multiply_reduce_fusion = (f32[768]{0:T(1024)S(1)}, f32[512]{0:T(512)S(1)}, f32[768]{0:T(1024)S(1)}, f32[512,768]{1,0:T(8,128)S(1)}) fusion(f32[512,768]{1,0:T(8,128)S(1)} %get-tuple-element.151, f32[512]{0:T(512)S(1)} %fusion.18, f32[512]{0:T(512)S(1)} %broadcast_multiply_fusion.1, f32[768]{0:T(1024)S(1)} %get-tuple-element.117, ...), kind=kOutput, calls=%fused_computation.29 | convolution fusion | flops 2419849216 | bytes 12600320 | tf_op jit(solution)/shard_map/nf,df->nd/dot_general | solution.py:1445
  154.0 1.7 convolution_convert_fusion.3
  155.9 1.3 concatenate.7.vec_rows
  157.9 7.0 %convolution_convert_fusion.1.d_down = bf16[3072,768]{1,0:T(8,128)(2,1)} fusion(bf16[512,3072]{1,0:T(8,128)(2,1)} %copy-done.27, bf16[512,768]{1,0:T(8,128)(2,1)} %copy-done.7), kind=kOutput, calls=%fused_computation.19 | convolution fusion | flops 2418278400 | bytes 8650752 | tf_op jit(solution)/shard_map/nf,nd->fd/dot_general | solution.py:1440
  164.9 4.9 %convolution_convert_fusion.d_up = bf16[768,3072]{1,0:T(8,128)(2,1)} fusion(bf16[512,3072]{1,0:T(8,128)(2,1)S(1)} %copy-done.26, f32[512,768]{1,0:T(8,128)S(1)} %get-tuple-element.151, f32[768]{0:T(1024)S(1)} %get-tuple-element.116, f32[768]{0:T(1024)S(1)} %get-tuple-element.117, f32[512]{0:T(512)S(1)} %fusion.18, f32[512]{0:T(512)S(1)} %broadcast_multiply_fusion.1), kind=kOutput, calls=%fused_computation.18 | convolution fusion | flops 2420244480 | bytes 9447424 | tf_op jit(solution)/shard_map/nd,nf->df/dot_general | solution.py:1443
  169.8 1.9 convolution_convert_fusion.2.d_out
  171.7 142.4 %back.1 = (bf16[512,768]{1,0:T(8,128)(2,1)}, f32[24,2304]{1,0:T(8,128)}, f32[24,768]{1,0:T(8,128)}, f32[24,3072]{1,0:T(8,128)}, f32[96,768]{1,0:T(8,128)}, /*index=5*/f32[24,256]{1,0:T(8,128)}) custom-call(bf16[4,128,768]{2,1,0:T(8,128)(2,1)} %bitcast.44, bf16[512,768]{1,0:T(8,128)(2,1)} %bitcast.43, f32[512,768]{1,0:T(8,128)} %copy-done, ...), custom_call_target="tpu_custom_call" | custom-call | tf_op jit(solution)/shard_map/back/pallas_call | solution.py:1334
  314.3 2.0 multiply_subtract_fusion.2
  316.3 1.6 multiply_subtract_fusion.3
  317.9 2.0 multiply_subtract_fusion.1
  320.0 1.1 multiply_subtract_fusion
  321.2 0.7 copy.54
  323.9 0.9 copy.58
  (94 shorter events, 6.0 us)
Async XLA Ops:
  110.8 21.8 %slice-start = ((s8[4718592]{0:T(1024)(128)(4,1)}), s8[4194304]{0:T(1024)(128)(4,1)S(1)}, s32[]{:S(2)}) async-start(s8[4718592]{0:T(1024)(128)(4,1)} %bitcast.50), calls=%async_computation | async-start | bytes 8388608
  113.9 18.6 %slice-start.1 = ((s8[4718592]{0:T(1024)(128)(4,1)}), s8[524288]{0:T(1024)(128)(4,1)S(1)}, s32[]{:S(2)}) async-start(s8[4718592]{0:T(1024)(128)(4,1)} %bitcast.50), calls=%async_computation.1 | async-start | bytes 1048576
  138.4 9.3 %copy-start.7 = (bf16[512,768]{1,0:T(8,128)(2,1)}, bf16[512,768]{1,0:T(8,128)(2,1)S(1)}, u32[]{:S(2)}) copy-start(bf16[512,768]{1,0:T(8,128)(2,1)S(1)} %get-tuple-element.140) | copy-start | bytes 2359300
  153.6 16.3 %copy-start = (f32[512,768]{1,0:T(8,128)}, f32[512,768]{1,0:T(8,128)S(1)}, u32[]{:S(2)}) copy-start(f32[512,768]{1,0:T(8,128)S(1)} %get-tuple-element.142.resid) | copy-start | bytes 4718596
  157.9 7.0 %copy-start.26 = (bf16[512,3072]{1,0:T(8,128)(2,1)S(1)}, bf16[512,3072]{1,0:T(8,128)(2,1)}, u32[]{:S(2)}) copy-start(bf16[512,3072]{1,0:T(8,128)(2,1)} %get-tuple-element.138) | copy-start | bytes 9437188
  171.7 142.6 %copy-start.4 = (f32[24,2304]{1,0:T(8,128)S(1)}, f32[24,2304]{1,0:T(8,128)}, u32[]{:S(2)}) copy-start(f32[24,2304]{1,0:T(8,128)} %qkv_w.1) | copy-start | bytes 663556
  171.7 142.6 %copy-start.14 = (f32[24,2304]{1,0:T(8,128)S(1)}, f32[24,2304]{1,0:T(8,128)}, u32[]{:S(2)}) copy-start(f32[24,2304]{1,0:T(8,128)} %param.29) | copy-start | bytes 663556
  171.7 142.6 %copy-start.15 = (f32[24,2304]{1,0:T(8,128)S(1)}, f32[24,2304]{1,0:T(8,128)}, u32[]{:S(2)}) copy-start(f32[24,2304]{1,0:T(8,128)} %param.28) | copy-start | bytes 663556
  171.7 144.6 %copy-start.13 = (f32[24,768]{1,0:T(8,128)S(1)}, f32[24,768]{1,0:T(8,128)}, u32[]{:S(2)}) copy-start(f32[24,768]{1,0:T(8,128)} %out_w.1) | copy-start | bytes 221188
  171.7 144.6 %copy-start.17 = (f32[24,768]{1,0:T(8,128)S(1)}, f32[24,768]{1,0:T(8,128)}, u32[]{:S(2)}) copy-start(f32[24,768]{1,0:T(8,128)} %param.31) | copy-start | bytes 221188
  171.7 144.6 %copy-start.18 = (f32[24,768]{1,0:T(8,128)S(1)}, f32[24,768]{1,0:T(8,128)}, u32[]{:S(2)}) copy-start(f32[24,768]{1,0:T(8,128)} %param.30) | copy-start | bytes 221188
  171.7 146.2 %copy-start.2 = (f32[24,3072]{1,0:T(8,128)S(1)}, f32[24,3072]{1,0:T(8,128)}, u32[]{:S(2)}) copy-start(f32[24,3072]{1,0:T(8,128)} %up_w.1) | copy-start | bytes 884740
  171.7 146.2 %copy-start.8 = (f32[24,3072]{1,0:T(8,128)S(1)}, f32[24,3072]{1,0:T(8,128)}, u32[]{:S(2)}) copy-start(f32[24,3072]{1,0:T(8,128)} %param.33) | copy-start | bytes 884740
  171.7 146.2 %copy-start.9 = (f32[24,3072]{1,0:T(8,128)S(1)}, f32[24,3072]{1,0:T(8,128)}, u32[]{:S(2)}) copy-start(f32[24,3072]{1,0:T(8,128)} %param.32) | copy-start | bytes 884740
  314.2 5.8 %copy-start.3 = (f32[96,768]{1,0:T(8,128)S(1)}, f32[96,768]{1,0:T(8,128)}, u32[]{:S(2)}) copy-start(f32[96,768]{1,0:T(8,128)} %down_w.1) | copy-start | bytes 884740
  314.2 5.8 %copy-start.10 = (f32[96,768]{1,0:T(8,128)S(1)}, f32[96,768]{1,0:T(8,128)}, u32[]{:S(2)}) copy-start(f32[96,768]{1,0:T(8,128)} %param.35) | copy-start | bytes 884740
  314.2 5.8 %copy-start.11 = (f32[96,768]{1,0:T(8,128)S(1)}, f32[96,768]{1,0:T(8,128)}, u32[]{:S(2)}) copy-start(f32[96,768]{1,0:T(8,128)} %param.34) | copy-start | bytes 884740
  314.2 5.8 %copy-start.12 = (f32[96,768]{1,0:T(8,128)S(1)}, f32[96,768]{1,0:T(8,128)}, u32[]{:S(2)}) copy-start(f32[96,768]{1,0:T(8,128)} %get-tuple-element.66) | copy-start | bytes 884740
  314.2 6.8 %copy-start.22 = (f32[12,24]{1,0:T(8,128)S(1)}, f32[12,24]{1,0:T(8,128)}, u32[]{:S(2)}) copy-start(f32[12,24]{1,0:T(8,128)} %param.37) | copy-start | bytes 3460
  314.2 6.9 %copy-start.23 = (f32[12,24]{1,0:T(8,128)S(1)}, f32[12,24]{1,0:T(8,128)}, u32[]{:S(2)}) copy-start(f32[12,24]{1,0:T(8,128)} %param.36) | copy-start | bytes 3460
  314.3 7.0 %copy-start.19 = (f32[24,256]{1,0:T(8,128)S(1)}, f32[24,256]{1,0:T(8,128)}, u32[]{:S(2)}) copy-start(f32[24,256]{1,0:T(8,128)} %get-tuple-element.67) | copy-start | bytes 73732
  314.3 9.0 %copy-start.20 = (f32[12,33]{1,0:T(8,128)S(1)}, f32[12,33]{1,0:T(8,128)}, u32[]{:S(2)}) copy-start(f32[12,33]{1,0:T(8,128)} %param.39) | copy-start | bytes 4756
  314.3 9.0 %copy-start.21 = (f32[12,33]{1,0:T(8,128)S(1)}, f32[12,33]{1,0:T(8,128)}, u32[]{:S(2)}) copy-start(f32[12,33]{1,0:T(8,128)} %param.38) | copy-start | bytes 4756
  314.3 9.6 %copy-start.6 = (bf16[512,768]{1,0:T(8,128)(2,1)S(1)}, bf16[512,768]{1,0:T(8,128)(2,1)}, u32[]{:S(2)}) copy-start(bf16[512,768]{1,0:T(8,128)(2,1)} %get-tuple-element.62) | copy-start | bytes 2359300
  (6 other events, 19.1 us)

commit v4 on v3

--- a/solution.py
+++ b/solution.py
@@ -676,6 +676,40 @@
         self.started += copies
         return copies
 
+    def line_peers(self):
+        n, line, core = self.size // 2, self.me // 2, self.me % 2
+        return [(self.row, 2 * ((line + k) % n) + core) for k in range(1, n)]
+
+    def go(self, channel, k, src, dst, device):
+        copy = remote(src, dst, self.send.at[channel, k], self.recv.at[channel, k], device)
+        copy.start()
+        self.started.append(copy)
+        return copy
+
+    def share(self, parts):
+        n, line, core = self.size // 2, self.me // 2, self.me % 2
+        sibling = (self.row, 2 * line + 1 - core)
+        there, here = [], []
+        for channel, block in parts:
+            mine = block(self.me)
+            there.append(
+                [self.go(channel, k, mine, mine, d) for k, d in enumerate(self.line_peers())]
+            )
+        for channel, block in parts:
+            here.append(self.go(channel, n - 1, block(self.me), block(self.me), sibling))
+
+        def arrive():
+            for k in range(1, n):
+                source = 2 * ((line - k + n) % n) + core
+                for (channel, block), copies in zip(parts, there):
+                    copies[k - 1].wait_recv()
+                    got = block(source)
+                    here.append(self.go(channel, n - 1 + k, got, got, sibling))
+            for copy in here:
+                copy.wait_recv()
+
+        return arrive
+
     def halo(self, channel, source, padded, reach):
         length = source.shape[1]
         copies = []
@@ -823,12 +857,11 @@
         return carry
 
     lax.fori_loop(0, n_seq, own_landmarks, 0)
-    landed = group.push(1, lambda d: lb.at[me], lb.at[me])
+    landed = group.share([(1, lambda d: lb.at[d])])
     halo_in, halo_sent = group.halo(0, v, vpad, reach)
     g_out.step_two()
     g_down.step_one()
-    for copy in landed:
-        copy.wait_recv()
+    landed()
 
     def whole_landmarks(s, carry):
         x = lb[:, s].astype(F32)
@@ -923,12 +956,14 @@
         lvo[:, at] = mean
         mixed = together(three(nn, split(zo[PINV_ITERS, i]), split(apart(mean))))
         mix[my_seq, :, lanes(my_pair + i)] = mixed.astype(BF)
-    mine = mix.at[my_seq, :, owner_lanes(me)]
-    mix_in = group.push(4, lambda d: mine, mine)
-    back_in = group.push(5, lambda d: mstat.at[me], mstat.at[me])
+    mixed_in = group.share(
+        [
+            (4, lambda d: mix.at[owner_seq(d), :, owner_lanes(d)]),
+            (5, lambda d: mstat.at[d]),
+        ]
+    )
     g_up.step_three()
-    for copy in mix_in + back_in:
-        copy.wait_recv()
+    mixed_in()
 
     rows = jnp.concatenate(
         [mstat[...].reshape(8 * size, PAIR), jnp.zeros((PAIR - 8 * size, PAIR), F32)], axis=0
@@ -1012,13 +1047,193 @@
     )(tokens.reshape(n_seq * length, width), *matrices, table, lines)
 
 
+def gelu_parts(x):
+    expo = jnp.exp(-0.5 * x * x)
+    t = 1.0 / (1.0 + (0.3275911 * 0.7071067811865476) * jnp.abs(x))
+    tail = -0.284496736 + t * (1.421413741 + t * (-1.453152027 + t * 1.061405429))
+    tail = 0.5 * expo * t * (0.254829592 + t * tail)
+    below = jnp.where(x >= 0.0, 1.0 - tail, tail)
+    return x * below, below + x * expo * 0.3989422804014327
+
+
+def norm_parts(resid):
+    center = resid - jnp.mean(resid, axis=-1, keepdims=True)
+    scale = lax.rsqrt(jnp.mean(center * center, axis=-1, keepdims=True) + norm_eps)
+    return center * scale, scale
+
+
+def norm_back(grad, gain, unit, scale):
+    inner = grad * gain
+    mean = jnp.mean(inner, axis=-1, keepdims=True)
+    along = jnp.mean(inner * unit, axis=-1, keepdims=True)
+    return scale * (inner - mean - unit * along)
+
+
+def row_sum(x):
+    return jnp.sum(x, axis=0, keepdims=True)
+
+
+def feed_kernel(
+    attn, tokens, cot, rows, h_out, h_up, h_down,
+    layer_out, grad_one, ga, sums, d_down, d_up, d_out,
+    w_out, w_up, w_down, g_down, g_up, g_out, active, slope, unit_one, scale_one, normed, low, low_t,
+    total, grad_two, ff, attn_t, w_sem, o_sem,
+):
+    count, width = attn.shape
+    hidden = w_up.shape[1]
+    loads = [
+        pltpu.make_async_copy(src, dst, w_sem.at[i])
+        for i, (src, dst) in enumerate(((h_out, w_out), (h_up, w_up), (h_down, w_down)))
+    ]
+    for load in loads:
+        load.start()
+    block = 2 * PAIR
+    n_rows, n_wide = count // block, width // block
+    row_groups = hidden // width
+    sums[...] = jnp.zeros(sums.shape, F32)
+
+    def row(i):
+        return rows[i : i + 1, :]
+
+    def at_rows(i):
+        return pl.ds(pl.multiple_of(i * block, block), block)
+
+    loads[0].wait()
+
+    def first(i, carry):
+        at = at_rows(i)
+        resid = tokens[at, :].astype(F32) + (nn(attn[at, :], w_out[...]) + row(2))
+        unit, scale = norm_parts(resid)
+        out = unit * row(6) + row(3)
+        unit_one[at, :] = unit
+        scale_one[at, :] = jnp.broadcast_to(scale, (block, PAIR))
+        normed[at, :] = out
+        low[at, :] = out.astype(BF)
+        total[at, :] = jnp.broadcast_to(row(4), (block, width))
+        return carry
+
+    lax.fori_loop(0, n_rows, first, 0)
+    low_t[...] = low[...].T
+    attn_t[...] = attn[...].T
+    loads[1].wait()
+    loads[2].wait()
+
+    def forward(r, carry):
+        for j in range(n_wide):
+            f = pl.ds(pl.multiple_of(r * width + j * block, block), block)
+            bias = rows[pl.ds(8 + r, 1), j * block : (j + 1) * block]
+            value, rate = gelu_parts(nn(low[...], w_up[:, f]) + bias)
+            value = value.astype(BF)
+            active[:, f] = value
+            slope[:, f] = rate.astype(BF)
+            total[...] += nn(value, w_down[f, :])
+        return carry
+
+    lax.fori_loop(0, row_groups, forward, 0)
+
+    def second(i, carry):
+        at = at_rows(i)
+        unit, scale = norm_parts(normed[at, :] + total[at, :])
+        layer_out[at, :] = (unit * row(7) + row(5)).astype(BF)
+        up = cot[at, :].astype(F32)
+        grad = norm_back(up, row(7), unit, scale)
+        grad_two[at, :] = grad
+        total[at, :] = grad
+        grad = grad.astype(BF)
+        ff[at, :] = grad
+        sums[4:5, :] += row_sum(grad.astype(F32))
+        sums[5:6, :] += row_sum(up)
+        sums[7:8, :] += row_sum(up * unit)
+        return carry
+
+    lax.fori_loop(0, n_rows, second, 0)
+
+    def backward(r, carry):
+        for j in range(n_wide):
+            f = pl.ds(pl.multiple_of(r * width + j * block, block), block)
+            lane = slice(j * block, (j + 1) * block)
+            grad = nt(ff[...], w_down[f, :]) * slope[:, f].astype(F32)
+            grad = grad.astype(BF)
+            sums[pl.ds(8 + r, 1), lane] = row_sum(grad.astype(F32))
+            g_up[:, f] = nn(low_t[...], grad).astype(BF)
+            g_down[f, :] = tn(active[:, f], ff[...]).astype(BF)
+            total[...] += nt(grad, w_up[:, f])
+        f = pl.ds(pl.multiple_of(r * width, width), width)
+        pltpu.make_async_copy(g_down.at[f, :], d_down.at[f, :], o_sem.at[0, r]).start()
+        pltpu.make_async_copy(g_up.at[:, f], d_up.at[:, f], o_sem.at[1, r]).start()
+        return carry
+
+    lax.fori_loop(0, row_groups, backward, 0)
+
+    def third(i, carry):
+        at = at_rows(i)
+        unit = unit_one[at, :]
+        up = total[at, :]
+        grad = norm_back(up, row(6), unit, scale_one[at, :1])
+        grad_one[at, :] = grad
+        grad = grad.astype(BF)
+        low[at, :] = grad
+        ga[at, :] = nt(grad, w_out[...]).astype(BF)
+        sums[2:3, :] += row_sum(grad.astype(F32))
+        sums[3:4, :] += row_sum(up)
+        sums[6:7, :] += row_sum(up * unit)
+        return carry
+
+    lax.fori_loop(0, n_rows, third, 0)
+    g_out[...] = nn(attn_t[...], low[...]).astype(BF)
+    last = pltpu.make_async_copy(g_out, d_out, o_sem.at[2, 0])
+    last.start()
+    for r in range(row_groups):
+        f = pl.ds(r * width, width)
+        pltpu.make_async_copy(g_down.at[f, :], d_down.at[f, :], o_sem.at[0, r]).wait()
+        pltpu.make_async_copy(g_up.at[:, f], d_up.at[:, f], o_sem.at[1, r]).wait()
+    last.wait()
+
+
+def feed(attn, tokens, cot, rows, weights):
+    count, width = attn.shape
+    hidden = weights[1].shape[1]
+    vmem, hbm = pl.BlockSpec(memory_space=pltpu.VMEM), pl.BlockSpec(memory_space=pltpu.HBM)
+    shape = jax.ShapeDtypeStruct
+    wide = [x.shape for x in weights]
+    return pl.pallas_call(
+        feed_kernel,
+        out_shape=[
+            shape(attn.shape, BF), shape(attn.shape, F32), shape(attn.shape, BF),
+            shape(rows.shape, F32),
+        ]
+        + [shape(wide[i], BF) for i in (2, 1, 0)],
+        in_specs=[vmem] * 4 + [hbm] * 3,
+        out_specs=[vmem] * 4 + [hbm] * 3,
+        scratch_shapes=[pltpu.VMEM(x, BF) for x in wide]
+        + [pltpu.VMEM(wide[i], BF) for i in (2, 1, 0)]
+        + [
+            pltpu.VMEM((count, hidden), BF),
+            pltpu.VMEM((count, hidden), BF),
+            pltpu.VMEM((count, width), F32),
+            pltpu.VMEM((count, PAIR), F32),
+            pltpu.VMEM((count, width), F32),
+            pltpu.VMEM((count, width), BF),
+            pltpu.VMEM((width, count), BF),
+            pltpu.VMEM((count, width), F32),
+            pltpu.VMEM((count, width), F32),
+            pltpu.VMEM((count, width), BF),
+            pltpu.VMEM((width, count), BF),
+            pltpu.SemaphoreType.DMA((3,)),
+            pltpu.SemaphoreType.DMA((3, hidden // width)),
+        ],
+        compiler_params=pltpu.CompilerParams(vmem_limit_bytes=56 * 1024 * 1024),
+        name="feed",
+    )(attn, tokens, cot, rows, *weights)
+
+
 def back_kernel(
     reach, n_taps,
     ga, tokens, resid, f_qkv, vec_rows, lines, d_down, d_up, d_out,
     q, k, vpad, landq, landk, mix, p1, e, wt, p2o, zo, lvo,
     input_grad, s_qkv, s_out, s_up, s_down, s_small,
     grad, tapg, table, tok_t, outbox, small_box,
-    gpad, gmix, gmr, low, gfull, stat, mstat, gcol, gq, gv, lkp, lpart, lpr, two, twr, dz, dp,
+    gpad, gmix, gmr, low, gfull, mstat, gcol, gq, gv, lkp, lpart, lpr, lsum, gsum, gpart, dz, dp,
     skew, own_g, *rest,
 ):
     bufs, (g_send, g_recv, g_local, send, recv) = rest[:-5], rest[-5:]
@@ -1086,9 +1301,18 @@
         return carry
 
     lax.fori_loop(0, n_seq, first, 0)
-    gmix_in = group.push(1, lambda d: gmix.at[owner_seq(d), :, owner_lanes(d)], gmr.at[me])
-    gmr[me] = gmix[owner_seq(me), :, owner_lanes(me)]
+    chips, my_line, my_core = size // 2, me // 2, me % 2
+    core_lanes = [pl.ds(pl.multiple_of(c * each, PAIR), each) for c in (my_core, 1 - my_core)]
+    sibling = (group.row, 2 * my_line + 1 - my_core)
+    gmix_sib = group.go(1, chips, gmix.at[:, :, core_lanes[1]], gsum, sibling)
     r_down.step_one()
+    gmix_sib.wait_recv()
+    gpart[...] = gmix[:, :, core_lanes[0]] + gsum[...]
+    gmix_in = []
+    for kk, device in enumerate(group.line_peers()):
+        other = device[1] // 2
+        gmix_in.append(group.go(1, kk, gpart.at[other], gmr.at[my_line], device))
+    gmr[my_line] = gpart[my_line]
     r_up.step_one()
     fill_bands(lines, table, reach)
     halo_in()
@@ -1128,7 +1352,7 @@
     for i in range(own):
         at = pl.ds(i * PAIR, PAIR)
         total = gmr[0, :, at].astype(F32)
-        for src in range(1, size):
+        for src in range(1, chips):
             total = total + gmr[src, :, at].astype(F32)
         total = split(apart(total))
         means = apart(lvo[:, at])
@@ -1138,14 +1362,16 @@
         tile = jnp.where(lane_at == i, column, tile)
         dz[i] = three(nt, total, split(means))
         dp[i] = jnp.zeros((PAIR, PAIR), F32)
-    stat[...] = tile.T[:8]
-    mstat[me] = stat[...]
+    mstat[me] = tile.T[:8]
     gfull[my_seq, :, owner_lanes(me)] = own_g[...]
-    g_in = group.push(2, lambda d: own_g, gfull.at[my_seq, :, owner_lanes(me)])
-    back_in = group.push(3, lambda d: stat, mstat.at[me])
+    g_in = group.share(
+        [
+            (2, lambda d: gfull.at[owner_seq(d), :, owner_lanes(d)]),
+            (3, lambda d: mstat.at[d]),
+        ]
+    )
     r_up.step_two()
-    for copy in g_in + back_in:
-        copy.wait_recv()
+    g_in()
     rows = jnp.concatenate(
         [mstat[...].reshape(8 * size, PAIR), jnp.zeros((PAIR - 8 * size, PAIR), F32)], axis=0
     )
@@ -1173,7 +1399,8 @@
         ).astype(BF)
         lq = (together(nn(gs, k[s, :, at])) * scale).reshape(size, land_local, PAIR)
         lk = lkp[s, :, at].reshape(size, land_local, PAIR)
-        lpart[:, s, :, at] = jnp.concatenate([lq, lk], axis=1).astype(BF)
+        both = jnp.concatenate([lq, lk], axis=1).astype(BF)
+        lpart[:, :, s, :, at] = both.reshape(chips, 2, 2 * land_local, PAIR)
 
     per_step = n_seq * pairs // PINV_ITERS
 
@@ -1215,25 +1442,32 @@
         query = together(nn(gs[0], lk) + nn(gs[1], lk)) * scale
         key = together(tn(gs[0], lq) + tn(gs[1], lq)) * scale
         both = [x.reshape(size, land_local, PAIR) for x in (query, key)]
-        two[:, :, at] = jnp.concatenate(both, axis=1).astype(BF)
-    lpr[me] = lpart[me]
-    twr[me] = two[me]
-    part_in = group.push(4, lambda d: lpart.at[d], lpr.at[me])
-    two_in = group.push(5, lambda d: two.at[d], twr.at[me])
+        both = jnp.concatenate(both, axis=1).reshape(chips, 2, 2 * land_local, PAIR)
+        lpart[:, :, my_seq, :, here] = (lpart[:, :, my_seq, :, here].astype(F32) + both).astype(BF)
+    land_sib = group.go(4, chips, lpart.at[:, 1 - my_core], lsum, sibling)
+    land_sib.wait_recv()
+
+    def add_lands(i, carry):
+        lsum[i] = lsum[i] + lpart[i, my_core]
+        return carry
+
+    lax.fori_loop(0, chips, add_lands, 0)
+    lpr[my_line] = lsum[my_line]
+    land_in = []
+    for kk, device in enumerate(group.line_peers()):
+        land_in.append(group.go(4, kk, lsum.at[device[1] // 2], lpr.at[my_line], device))
     open_weight(r_v, 0)
     r_down.step_four()
-    for copy in part_in + two_in:
+    for copy in land_in:
         copy.wait_recv()
 
     def close(s, carry):
         for p in range(pairs):
             at = lanes(p)
             total = lpr[0, s, :, at].astype(F32)
-            for src in range(1, size):
+            for src in range(1, chips):
                 total = total + lpr[src, s, :, at].astype(F32)
-            owner = s * pairs + p
-            spot = pl.ds(pl.multiple_of((owner % own) * PAIR, PAIR), PAIR)
-            total = (total + twr[owner // own, :, spot].astype(F32)) * (1.0 / seg)
+            total = total * (1.0 / seg)
             spread = [
                 jnp.concatenate(
                     [jnp.broadcast_to(x[i : i + 1], (seg, PAIR)) for i in range(land_local)], axis=0
@@ -1345,19 +1579,19 @@
             pltpu.VMEM((width, PAIR), F32),
             pltpu.VMEM((n_seq, length + 2 * reach, width), BF),
             pltpu.VMEM((n_seq, LAND, width), BF),
-            pltpu.VMEM((seq_size, LAND, own * PAIR), BF),
+            pltpu.VMEM((seq_size // 2, LAND, own * PAIR), BF),
             pltpu.VMEM((units, PAIR, length), BF),
             pltpu.VMEM((n_seq, LAND, width), BF),
-            pltpu.VMEM((8, PAIR), F32),
             pltpu.VMEM((seq_size, 8, PAIR), F32),
             pltpu.VMEM((PAIR, PAIR), F32),
             pltpu.VMEM((n_seq, length, width), F32),
             pltpu.VMEM((n_seq, length, width), F32),
             pltpu.VMEM((n_seq, LAND, width), F32),
-            pltpu.VMEM((seq_size, n_seq, part, width), BF),
-            pltpu.VMEM((seq_size, n_seq, part, width), BF),
-            pltpu.VMEM((seq_size, part, own * PAIR), BF),
-            pltpu.VMEM((seq_size, part, own * PAIR), BF),
+            pltpu.VMEM((seq_size // 2, 2, n_seq, part, width), BF),
+            pltpu.VMEM((seq_size // 2, n_seq, part, width), BF),
+            pltpu.VMEM((seq_size // 2, n_seq, part, width), BF),
+            pltpu.VMEM((n_seq, LAND, own * PAIR), BF),
+            pltpu.VMEM((n_seq, LAND, own * PAIR), BF),
             pltpu.VMEM((own, PAIR, PAIR), F32),
             pltpu.VMEM((own, PAIR, PAIR), F32),
             pltpu.VMEM((2 * pairs, length, 2 * PAIR), F32),
@@ -1394,10 +1628,14 @@
         and taps.shape[1] == 33
         and taps.shape[0] <= matrices[0].shape[0]
         and units == own * seq_size
+        and seq_size == 2 * n_seq
+        and width == 2 * own * PAIR
         and 2 * own <= 8
         and (width // PAIR) % own == 0
         and units % PINV_ITERS == 0
         and LAND == 8 * seq_size
+        and matrices[2].shape[1] == 4 * width
+        and args[6].shape[0] == 12
     )
 
 
@@ -1408,7 +1646,6 @@
 ):
     seq_count, local_len, model_width = tokens.shape
     head_count, tap_count = taps.shape
-    hidden_width = up_weight.shape[1]
     seq_size = lax.axis_size("seq")
     reach = tap_count // 2
     row_count = seq_count * local_len
@@ -1422,55 +1659,14 @@
     )
     attn_low = kept.pop(2).reshape(row_count, model_width)
     queries, key_rows = kept[:2]
-    branch = jnp.dot(attn_low, full_out, preferred_element_type=jnp.float32) + vec_float[2]
-    resid_one = flat_in.astype(jnp.float32) + branch
-    normed, norm_pull_one = jax.vjp(layer_norm, resid_one, vec_float[6], vec_float[3])
-    normed_low = normed.astype(BF)
-    hidden_pre = jnp.dot(normed_low, full_up, preferred_element_type=jnp.float32) + vec_float[
-        8:count
-    ].reshape(hidden_width)
-    active, gelu_pull = jax.vjp(gelu_exact, hidden_pre)
-    active_low = active.astype(BF)
-    ff_out = jnp.dot(active_low, full_down, preferred_element_type=jnp.float32) + vec_float[4]
-    layer_out, norm_pull_two = jax.vjp(layer_norm, normed + ff_out, vec_float[7], vec_float[5])
-    grad_resid_two, grad_gain_two, grad_shift_two = norm_pull_two(
-        cotangent.reshape(row_count, model_width).astype(jnp.float32)
-    )
-    grad_ff = grad_resid_two.astype(BF)
-    grad_down = jnp.einsum("nf,nd->fd", active_low, grad_ff, preferred_element_type=jnp.float32)
-    grad_active = jnp.einsum("nd,fd->nf", grad_ff, full_down, preferred_element_type=jnp.float32)
-    grad_hidden = gelu_pull(grad_active)[0].astype(BF)
-    grad_up = jnp.einsum("nd,nf->df", normed_low, grad_hidden, preferred_element_type=jnp.float32)
-    grad_normed = (
-        jnp.einsum("nf,df->nd", grad_hidden, full_up, preferred_element_type=jnp.float32)
-        + grad_resid_two
-    )
-    grad_resid_one, grad_gain_one, grad_shift_one = norm_pull_one(grad_normed)
-    grad_branch = grad_resid_one.astype(BF)
-    grad_out = jnp.einsum("nd,ne->de", attn_low, grad_branch, preferred_element_type=jnp.float32)
-    grad_attn = jnp.einsum(
-        "ne,de->nd", grad_branch, full_out, preferred_element_type=jnp.float32
-    ).astype(BF)
-    nothing = jnp.zeros((1, model_width), F32)
-    vec_rows = jnp.concatenate(
-        [
-            nothing,
-            nothing,
-            jnp.sum(grad_branch.astype(jnp.float32), axis=0)[None],
-            grad_shift_one[None],
-            jnp.sum(grad_ff.astype(jnp.float32), axis=0)[None],
-            grad_shift_two[None],
-            grad_gain_one[None],
-            grad_gain_two[None],
-            jnp.sum(grad_hidden.astype(jnp.float32), axis=0).reshape(-1, model_width),
-            jnp.zeros((16 - count, model_width), F32),
-        ],
-        axis=0,
+    layer_out, grad_resid_one, grad_attn, vec_rows, grad_down, grad_up, grad_out = feed(
+        attn_low, flat_in, cotangent.reshape(row_count, model_width), vec_float,
+        (full_out, full_up, full_down),
     )
     flipped = jnp.pad(taps[:, ::-1], ((0, 0), (0, 2 * PAIR - tap_count)))
     input_grad, summed_qkv, summed_out, summed_up, summed_down, small = back(
         grad_attn.reshape(tokens.shape), flat_in, grad_resid_one, full_qkv, vec_rows, flipped,
-        *[x.astype(BF) for x in (grad_down, grad_up, grad_out)],
+        grad_down, grad_up, grad_out,
         kept, matrices, seq_size, reach,
     )
     input_grad = input_grad.reshape(tokens.shape)
@@ -1482,7 +1678,7 @@
     new_down = adam_step(down_weight, down_first, down_second, summed_down, rate_matrix, decay_rate)
     new_vec = adam_step(vectors, vec_first, vec_second, summed_vec, rate_vector, 0.0)
     new_taps = adam_step(taps, tap_first, tap_second, summed_taps, rate_taps, 0.0)
-    out_tokens = layer_out.astype(BF).reshape(tokens.shape)
+    out_tokens = layer_out.reshape(tokens.shape)
     return (out_tokens, input_grad) + new_qkv + new_out + new_up + new_down + new_vec + new_taps
 
 

time: 330 us -> 283 us (0.86)
  matrix products: 54 us -> 0 us
  Pallas kernels: 248 us -> 267 us
  other arithmetic: 11.5 us -> 6.51 us
  local copies, waits for them, and re-layouts: 10.1 us -> 6.56 us
    dot_general x9 -> x0, matrix products: 54 us -> none  [the longest x1 18.6 us: with_kernels(): jnp.dot(normed_low, full_up, preferred_element_type=jnp.float32)]
    pallas_call x0 -> x1, Pallas kernels: none -> 37.9 us  [feed(): pl.pallas_call(feed_kernel, out_shape=[shape(attn.shape, BF), shape(attn....]
    pallas_call x1, Pallas kernels: 142 us -> 133 us  [back(): pl.pallas_call(functools.partial(back_kernel, reach, 2 * reach + 1), out_...]
    pallas_call x1, Pallas kernels: 106 us -> 96.2 us  [front(): pl.pallas_call(functools.partial(front_kernel, reach), out_shape=whole +...]
    reduce_sum x8 -> x0, other arithmetic: 4.17 us -> none  [the longest x2 2.25 us: layer_norm(): center = residual - jnp.mean(residual, axis=-1, keepdims=True)]
where the time goes in v4:
time: 283 us; the launch traced here: 281 us
  Pallas kernels  267 us (94%)
  local copies, waits for them, and re-layouts  6.56 us (2%)
  other arithmetic  6.51 us (2%)
    pallas_call x1, Pallas kernels, back(): pl.pallas_call(functools.partial(back_kernel, reach, 2 * reach + 1), out_...  133 us
    pallas_call x1, Pallas kernels, front(): pl.pallas_call(functools.partial(front_kernel, reach), out_shape=whole +...  96.2 us
    pallas_call x1, Pallas kernels, feed(): pl.pallas_call(feed_kernel, out_shape=[shape(attn.shape, BF), shape(attn....  37.9 us
    sub x6, other arithmetic, adam_step(): weight - step_rate * (update + decay_coef * weight)  6.51 us

profile of v4, /device:TPU:0, one launch (start us, length us, event | category | flops | bytes accessed | tf_op | source)
XLA Modules:
  0.0 281.1 jit_solution(14242113868850602460)
XLA Ops:
  0.7 0.8 copy.48
  1.4 0.6 pad.11.vec_w
  2.0 1.3 pad.12.lines
  3.4 96.2 %front.1 = (bf16[768,2304]{1,0:T(8,128)(2,1)}, bf16[768,768]{1,0:T(8,128)(2,1)}, bf16[768,3072]{1,0:T(8,128)(2,1)}, bf16[3072,768]{1,0:T(8,128)(2,1)}, f32[16,76...) custom-call(bf16[512,768]{1,0:T(8,128)(2,1)} %bitcast.14, ...), custom_call_target="tpu_custom_call" | custom-call | tf_op jit(solution)/shard_map/front/pallas_call | solution.py:1008
  99.6 0.0 copy-start.12
  99.6 37.9 %feed.1 = (bf16[512,768]{1,0:T(8,128)(2,1)}, f32[512,768]{1,0:T(8,128)}, bf16[512,768]{1,0:T(8,128)(2,1)}, f32[16,768]{1,0:T(8,128)}, bf16[3072,768]{1,0:T(8,128...) custom-call(bf16[512,768]{1,0:T(8,128)(2,1)} %bitcast.19, bf16[512,768]{1,0:T(8,128)(2,1)} %bitcast.15, ...), custom_call_target="tpu_custom_call" | custom-call | tf_op jit(solution)/shard_map/feed/pallas_call | solution.py:1199
  137.5 0.1 rev.3
  137.6 0.6 pad.13.lines
  138.2 0.0 copy-start.6
  138.2 133.0 %back.1 = (bf16[512,768]{1,0:T(8,128)(2,1)}, f32[24,2304]{1,0:T(8,128)}, f32[24,768]{1,0:T(8,128)}, f32[24,3072]{1,0:T(8,128)}, f32[96,768]{1,0:T(8,128)}, /*index=5*/f32[24,256]{1,0:T(8,128)}) custom-call(bf16[4,128,768]{2,1,0:T(8,128)(2,1)} %bitcast.17, bf16[512,768]{1,0:T(8,128)(2,1)} %bitcast.16, f32[512,768]{1,0:T(8,128)} %get-tuple-element.58.resid, ...), custom_call_target="tpu_custom_call" | custom-call | tf_op jit(solution)/shard_map/back/pallas_call | solution.py:1568
  271.2 0.0 copy-start.2
  271.3 0.0 copy-start.8
  271.3 0.0 copy-start.13
  271.4 2.2 multiply_subtract_fusion.1
  273.7 2.0 multiply_subtract_fusion
  275.7 0.9 multiply_subtract_fusion.2
  276.6 0.7 multiply_subtract_fusion.3
  277.3 0.1 copy.49
  277.4 0.1 copy.51
  277.6 0.7 copy.54
  278.2 0.7 copy.55
  278.9 0.7 copy.56
  279.6 0.6 multiply_subtract_fusion.5
  280.2 0.9 copy.58
  (38 shorter events, 0.1 us)
Async XLA Ops:
  99.6 37.9 %copy-start.12 = (f32[12,33]{1,0:T(8,128)S(1)}, f32[12,33]{1,0:T(8,128)}, u32[]{:S(2)}) copy-start(f32[12,33]{1,0:T(8,128)} %param.27) | copy-start | bytes 4756
  138.2 133.2 %copy-start = (f32[24,3072]{1,0:T(8,128)S(1)}, f32[24,3072]{1,0:T(8,128)}, u32[]{:S(2)}) copy-start(f32[24,3072]{1,0:T(8,128)} %up_w.1) | copy-start | bytes 884740
  138.2 133.2 %copy-start.4 = (f32[24,3072]{1,0:T(8,128)S(1)}, f32[24,3072]{1,0:T(8,128)}, u32[]{:S(2)}) copy-start(f32[24,3072]{1,0:T(8,128)} %param.33) | copy-start | bytes 884740
  138.2 133.2 %copy-start.5 = (f32[24,3072]{1,0:T(8,128)S(1)}, f32[24,3072]{1,0:T(8,128)}, u32[]{:S(2)}) copy-start(f32[24,3072]{1,0:T(8,128)} %param.32) | copy-start | bytes 884740
  138.2 135.5 %copy-start.1 = (f32[96,768]{1,0:T(8,128)S(1)}, f32[96,768]{1,0:T(8,128)}, u32[]{:S(2)}) copy-start(f32[96,768]{1,0:T(8,128)} %down_w.1) | copy-start | bytes 884740
  138.2 135.5 %copy-start.6 = (f32[96,768]{1,0:T(8,128)S(1)}, f32[96,768]{1,0:T(8,128)}, u32[]{:S(2)}) copy-start(f32[96,768]{1,0:T(8,128)} %param.35) | copy-start | bytes 884740
  138.2 135.5 %copy-start.7 = (f32[96,768]{1,0:T(8,128)S(1)}, f32[96,768]{1,0:T(8,128)}, u32[]{:S(2)}) copy-start(f32[96,768]{1,0:T(8,128)} %param.34) | copy-start | bytes 884740
  271.2 4.4 %copy-start.2 = (f32[24,2304]{1,0:T(8,128)S(1)}, f32[24,2304]{1,0:T(8,128)}, u32[]{:S(2)}) copy-start(f32[24,2304]{1,0:T(8,128)} %qkv_w.1) | copy-start | bytes 663556
  271.3 4.4 %copy-start.9 = (f32[24,2304]{1,0:T(8,128)S(1)}, f32[24,2304]{1,0:T(8,128)}, u32[]{:S(2)}) copy-start(f32[24,2304]{1,0:T(8,128)} %param.29) | copy-start | bytes 663556
  271.3 4.4 %copy-start.10 = (f32[24,2304]{1,0:T(8,128)S(1)}, f32[24,2304]{1,0:T(8,128)}, u32[]{:S(2)}) copy-start(f32[24,2304]{1,0:T(8,128)} %param.28) | copy-start | bytes 663556
  271.3 4.4 %copy-start.11 = (f32[24,2304]{1,0:T(8,128)S(1)}, f32[24,2304]{1,0:T(8,128)}, u32[]{:S(2)}) copy-start(f32[24,2304]{1,0:T(8,128)} %get-tuple-element.77) | copy-start | bytes 663556
  271.3 5.3 %copy-start.8 = (f32[24,768]{1,0:T(8,128)S(1)}, f32[24,768]{1,0:T(8,128)}, u32[]{:S(2)}) copy-start(f32[24,768]{1,0:T(8,128)} %out_w.1) | copy-start | bytes 221188
  271.3 5.3 %copy-start.13 = (f32[24,768]{1,0:T(8,128)S(1)}, f32[24,768]{1,0:T(8,128)}, u32[]{:S(2)}) copy-start(f32[24,768]{1,0:T(8,128)} %param.31) | copy-start | bytes 221188
  271.3 5.3 %copy-start.14 = (f32[24,768]{1,0:T(8,128)S(1)}, f32[24,768]{1,0:T(8,128)}, u32[]{:S(2)}) copy-start(f32[24,768]{1,0:T(8,128)} %param.30) | copy-start | bytes 221188
  271.3 5.3 %copy-start.15 = (f32[24,768]{1,0:T(8,128)S(1)}, f32[24,768]{1,0:T(8,128)}, u32[]{:S(2)}) copy-start(f32[24,768]{1,0:T(8,128)} %get-tuple-element.78) | copy-start | bytes 221188
  271.3 6.0 %copy-start.19 = (f32[12,24]{1,0:T(8,128)S(1)}, f32[12,24]{1,0:T(8,128)}, u32[]{:S(2)}) copy-start(f32[12,24]{1,0:T(8,128)} %param.36) | copy-start | bytes 3460
  271.3 6.1 %copy-start.20 = (f32[12,24]{1,0:T(8,128)S(1)}, f32[12,24]{1,0:T(8,128)}, u32[]{:S(2)}) copy-start(f32[12,24]{1,0:T(8,128)} %param.37) | copy-start | bytes 3460
  271.4 6.2 %copy-start.16 = (f32[24,256]{1,0:T(8,128)S(1)}, f32[24,256]{1,0:T(8,128)}, u32[]{:S(2)}) copy-start(f32[24,256]{1,0:T(8,128)} %get-tuple-element.81) | copy-start | bytes 73732
  271.4 8.2 %copy-start.17 = (f32[12,33]{1,0:T(8,128)S(1)}, f32[12,33]{1,0:T(8,128)}, u32[]{:S(2)}) copy-start(f32[12,33]{1,0:T(8,128)} %param.39) | copy-start | bytes 4756
  271.4 8.2 %copy-start.18 = (f32[12,33]{1,0:T(8,128)S(1)}, f32[12,33]{1,0:T(8,128)}, u32[]{:S(2)}) copy-start(f32[12,33]{1,0:T(8,128)} %param.38) | copy-start | bytes 4756
  271.4 8.8 %copy-start.3 = (bf16[512,768]{1,0:T(8,128)(2,1)S(1)}, bf16[512,768]{1,0:T(8,128)(2,1)}, u32[]{:S(2)}) copy-start(bf16[512,768]{1,0:T(8,128)(2,1)} %get-tuple-element.76) | copy-start | bytes 2359300

commit v5 on v4

--- a/solution.py
+++ b/solution.py
@@ -812,6 +812,8 @@
     g_vec, g_k, g_q, g_v, g_out, g_up, g_down = pieces
     for piece in pieces[:4]:
         piece.spread()
+    g_out.spread()
+    g_up.spread()
     fill_bands(lines, table, reach)
 
     def project(dst, base, bias):
@@ -828,12 +830,10 @@
     g_vec.step_two()
     g_k.step_two()
     g_v.step_one()
-    g_out.spread()
-    g_up.spread()
+    g_down.spread()
     g_vec.step_three()
     g_q.step_two()
     g_k.step_three()
-    g_down.spread()
     g_vec.close()
     f_rows[...] = f_vec[:, :PAIR].astype(F32).T[: f_rows.shape[0]]
     g_v.step_two()
@@ -1285,8 +1285,6 @@
         piece.open(outbox.at[box])
 
     open_whole(0, d_down)
-    open_whole(1, d_up)
-    open_whole(2, d_out)
     halo_in, halo_sent = group.halo(0, ga, gpad, reach)
 
     def first(s, carry):
@@ -1313,7 +1311,8 @@
         other = device[1] // 2
         gmix_in.append(group.go(1, kk, gpart.at[other], gmr.at[my_line], device))
     gmr[my_line] = gpart[my_line]
-    r_up.step_one()
+    open_whole(1, d_up)
+    open_whole(2, d_out)
     fill_bands(lines, table, reach)
     halo_in()
     skew[...] = jnp.zeros(skew.shape, F32)
@@ -1341,8 +1340,7 @@
         for row in range(8, length, 8):
             total = total + pltpu.roll(skew[h, row : row + 8, :], wide - row, 1)
         tapg[h] = total[:, :PAIR]
-    r_down.step_two()
-    r_out.step_one()
+    r_up.step_one()
     tok_t[...] = tokens[...].T
 
     for copy in gmix_in:
@@ -1370,7 +1368,6 @@
             (3, lambda d: mstat.at[d]),
         ]
     )
-    r_up.step_two()
     g_in()
     rows = jnp.concatenate(
         [mstat[...].reshape(8 * size, PAIR), jnp.zeros((PAIR - 8 * size, PAIR), F32)], axis=0
@@ -1422,11 +1419,14 @@
             third(step * per_step + j)
         return carry
 
-    lax.fori_loop(0, PINV_ITERS // 2, pinv_back, 0)
-    r_down.step_three()
+    third_of = PINV_ITERS // 3
+    lax.fori_loop(0, third_of, pinv_back, 0)
+    r_down.step_two()
+    r_out.step_one()
+    lax.fori_loop(third_of, 2 * third_of, pinv_back, 0)
+    lax.fori_loop(2 * third_of, PINV_ITERS, pinv_back, 0)
+    r_up.step_two()
     r_out.step_two()
-    lax.fori_loop(PINV_ITERS // 2, PINV_ITERS, pinv_back, 0)
-    r_up.step_three()
 
     for i in range(own):
         at = pl.ds(i * PAIR, PAIR)
@@ -1457,7 +1457,6 @@
     for kk, device in enumerate(group.line_peers()):
         land_in.append(group.go(4, kk, lsum.at[device[1] // 2], lpr.at[my_line], device))
     open_weight(r_v, 0)
-    r_down.step_four()
     for copy in land_in:
         copy.wait_recv()
 
@@ -1481,11 +1480,12 @@
         return carry
 
     lax.fori_loop(0, n_seq, close, 0)
+    r_down.step_three()
     open_weight(r_q, 1)
     r_v.step_one()
     open_weight(r_k, 2)
     r_q.step_one()
-    r_out.step_three()
+    r_up.step_three()
 
     def column_sums(base):
         total = jnp.zeros((1, width), F32)
@@ -1513,6 +1513,8 @@
     r_small.open(small_box)
     r_v.step_two()
     r_k.step_one()
+    r_out.step_three()
+    r_down.step_four()
 
     def inputs(i, carry):
         step = 2 * PAIR
@@ -1526,13 +1528,13 @@
     lax.fori_loop(0, tokens.shape[0] // (2 * PAIR), inputs, 0)
     r_small.step_one()
     r_q.step_two()
-    r_up.step_four()
-    r_out.step_four()
     r_k.step_two()
     r_v.step_three()
     r_small.step_two()
+    r_up.step_four()
     r_q.step_three()
     r_k.step_three()
+    r_out.step_four()
     r_v.step_four()
     r_small.step_three()
     r_q.step_four()

time: 283 us -> 256 us (0.905)
  Pallas kernels: 267 us -> 242 us
    pallas_call x1, Pallas kernels: 133 us -> 108 us  [back(): pl.pallas_call(functools.partial(back_kernel, reach, 2 * reach + 1), out_...]
where the time goes in v5:
time: 256 us
  Pallas kernels  242 us (95%)
  local copies, waits for them, and re-layouts  6.56 us (3%)
  other arithmetic  6.51 us (3%)
    pallas_call x1, Pallas kernels, back(): pl.pallas_call(functools.partial(back_kernel, reach, 2 * reach + 1), out_...  108 us
    pallas_call x1, Pallas kernels, front(): pl.pallas_call(functools.partial(front_kernel, reach), out_shape=whole +...  96.2 us
    pallas_call x1, Pallas kernels, feed(): pl.pallas_call(feed_kernel, out_shape=[shape(attn.shape, BF), shape(attn....  37.9 us
    sub x6, other arithmetic, adam_step(): weight - step_rate * (update + decay_coef * weight)  6.51 us

profile of v5, /device:TPU:0, one launch (start us, length us, event | category | flops | bytes accessed | tf_op | source)
XLA Modules:
  0.0 255.6 jit_solution(15612366168210823237)
XLA Ops:
  0.7 0.8 copy.48
  1.4 0.6 pad.11.vec_w
  2.0 1.3 pad.12.lines
  3.4 96.2 %front.1 = (bf16[768,2304]{1,0:T(8,128)(2,1)}, bf16[768,768]{1,0:T(8,128)(2,1)}, bf16[768,3072]{1,0:T(8,128)(2,1)}, bf16[3072,768]{1,0:T(8,128)(2,1)}, f32[16,76...) custom-call(bf16[512,768]{1,0:T(8,128)(2,1)} %bitcast.14, ...), custom_call_target="tpu_custom_call" | custom-call | tf_op jit(solution)/shard_map/front/pallas_call | solution.py:1008
  99.6 0.0 copy-start.12
  99.6 37.9 %feed.1 = (bf16[512,768]{1,0:T(8,128)(2,1)}, f32[512,768]{1,0:T(8,128)}, bf16[512,768]{1,0:T(8,128)(2,1)}, f32[16,768]{1,0:T(8,128)}, bf16[3072,768]{1,0:T(8,128...) custom-call(bf16[512,768]{1,0:T(8,128)(2,1)} %bitcast.19, bf16[512,768]{1,0:T(8,128)(2,1)} %bitcast.15, ...), custom_call_target="tpu_custom_call" | custom-call | tf_op jit(solution)/shard_map/feed/pallas_call | solution.py:1199
  137.5 0.1 rev.3
  137.6 0.6 pad.13.lines
  138.2 0.0 copy-start.6
  138.2 0.0 copy-start.7
  138.2 107.5 %back.1 = (bf16[512,768]{1,0:T(8,128)(2,1)}, f32[24,2304]{1,0:T(8,128)}, f32[24,768]{1,0:T(8,128)}, f32[24,3072]{1,0:T(8,128)}, f32[96,768]{1,0:T(8,128)}, /*index=5*/f32[24,256]{1,0:T(8,128)}) custom-call(bf16[4,128,768]{2,1,0:T(8,128)(2,1)} %bitcast.17, bf16[512,768]{1,0:T(8,128)(2,1)} %bitcast.16, f32[512,768]{1,0:T(8,128)} %get-tuple-element.58.resid, ...), custom_call_target="tpu_custom_call" | custom-call | tf_op jit(solution)/shard_map/back/pallas_call | solution.py:1570
  245.8 0.0 copy-start.9
  245.8 0.0 copy-start.10
  246.0 2.2 multiply_subtract_fusion.1
  248.2 2.0 multiply_subtract_fusion
  250.2 0.9 multiply_subtract_fusion.2
  251.2 0.7 multiply_subtract_fusion.3
  251.9 0.1 copy.49
  252.0 0.1 copy.51
  252.1 0.7 copy.54
  252.8 0.7 copy.55
  253.4 0.7 copy.56
  254.1 0.6 multiply_subtract_fusion.5
  254.7 0.9 copy.58
  (38 shorter events, 0.1 us)
Async XLA Ops:
  99.6 37.9 %copy-start.12 = (f32[12,33]{1,0:T(8,128)S(1)}, f32[12,33]{1,0:T(8,128)}, u32[]{:S(2)}) copy-start(f32[12,33]{1,0:T(8,128)} %param.27) | copy-start | bytes 4756
  138.2 107.8 %copy-start = (f32[24,3072]{1,0:T(8,128)S(1)}, f32[24,3072]{1,0:T(8,128)}, u32[]{:S(2)}) copy-start(f32[24,3072]{1,0:T(8,128)} %up_w.1) | copy-start | bytes 884740
  138.2 107.8 %copy-start.4 = (f32[24,3072]{1,0:T(8,128)S(1)}, f32[24,3072]{1,0:T(8,128)}, u32[]{:S(2)}) copy-start(f32[24,3072]{1,0:T(8,128)} %param.33) | copy-start | bytes 884740
  138.2 107.8 %copy-start.5 = (f32[24,3072]{1,0:T(8,128)S(1)}, f32[24,3072]{1,0:T(8,128)}, u32[]{:S(2)}) copy-start(f32[24,3072]{1,0:T(8,128)} %param.32) | copy-start | bytes 884740
  138.2 110.0 %copy-start.1 = (f32[96,768]{1,0:T(8,128)S(1)}, f32[96,768]{1,0:T(8,128)}, u32[]{:S(2)}) copy-start(f32[96,768]{1,0:T(8,128)} %down_w.1) | copy-start | bytes 884740
  138.2 110.0 %copy-start.6 = (f32[96,768]{1,0:T(8,128)S(1)}, f32[96,768]{1,0:T(8,128)}, u32[]{:S(2)}) copy-start(f32[96,768]{1,0:T(8,128)} %param.35) | copy-start | bytes 884740
  138.2 110.0 %copy-start.7 = (f32[96,768]{1,0:T(8,128)S(1)}, f32[96,768]{1,0:T(8,128)}, u32[]{:S(2)}) copy-start(f32[96,768]{1,0:T(8,128)} %param.34) | copy-start | bytes 884740
  245.8 4.4 %copy-start.2 = (f32[24,2304]{1,0:T(8,128)S(1)}, f32[24,2304]{1,0:T(8,128)}, u32[]{:S(2)}) copy-start(f32[24,2304]{1,0:T(8,128)} %qkv_w.1) | copy-start | bytes 663556
  245.8 4.4 %copy-start.9 = (f32[24,2304]{1,0:T(8,128)S(1)}, f32[24,2304]{1,0:T(8,128)}, u32[]{:S(2)}) copy-start(f32[24,2304]{1,0:T(8,128)} %param.29) | copy-start | bytes 663556
  245.8 4.4 %copy-start.10 = (f32[24,2304]{1,0:T(8,128)S(1)}, f32[24,2304]{1,0:T(8,128)}, u32[]{:S(2)}) copy-start(f32[24,2304]{1,0:T(8,128)} %param.28) | copy-start | bytes 663556
  245.8 4.4 %copy-start.11 = (f32[24,2304]{1,0:T(8,128)S(1)}, f32[24,2304]{1,0:T(8,128)}, u32[]{:S(2)}) copy-start(f32[24,2304]{1,0:T(8,128)} %get-tuple-element.77) | copy-start | bytes 663556
  245.8 5.3 %copy-start.8 = (f32[24,768]{1,0:T(8,128)S(1)}, f32[24,768]{1,0:T(8,128)}, u32[]{:S(2)}) copy-start(f32[24,768]{1,0:T(8,128)} %out_w.1) | copy-start | bytes 221188
  245.8 5.3 %copy-start.13 = (f32[24,768]{1,0:T(8,128)S(1)}, f32[24,768]{1,0:T(8,128)}, u32[]{:S(2)}) copy-start(f32[24,768]{1,0:T(8,128)} %param.31) | copy-start | bytes 221188
  245.8 5.3 %copy-start.14 = (f32[24,768]{1,0:T(8,128)S(1)}, f32[24,768]{1,0:T(8,128)}, u32[]{:S(2)}) copy-start(f32[24,768]{1,0:T(8,128)} %param.30) | copy-start | bytes 221188
  245.9 5.3 %copy-start.15 = (f32[24,768]{1,0:T(8,128)S(1)}, f32[24,768]{1,0:T(8,128)}, u32[]{:S(2)}) copy-start(f32[24,768]{1,0:T(8,128)} %get-tuple-element.78) | copy-start | bytes 221188
  245.9 6.0 %copy-start.19 = (f32[12,24]{1,0:T(8,128)S(1)}, f32[12,24]{1,0:T(8,128)}, u32[]{:S(2)}) copy-start(f32[12,24]{1,0:T(8,128)} %param.36) | copy-start | bytes 3460
  245.9 6.1 %copy-start.20 = (f32[12,24]{1,0:T(8,128)S(1)}, f32[12,24]{1,0:T(8,128)}, u32[]{:S(2)}) copy-start(f32[12,24]{1,0:T(8,128)} %param.37) | copy-start | bytes 3460
  245.9 6.2 %copy-start.16 = (f32[24,256]{1,0:T(8,128)S(1)}, f32[24,256]{1,0:T(8,128)}, u32[]{:S(2)}) copy-start(f32[24,256]{1,0:T(8,128)} %get-tuple-element.81) | copy-start | bytes 73732
  245.9 8.2 %copy-start.17 = (f32[12,33]{1,0:T(8,128)S(1)}, f32[12,33]{1,0:T(8,128)}, u32[]{:S(2)}) copy-start(f32[12,33]{1,0:T(8,128)} %param.39) | copy-start | bytes 4756
  245.9 8.2 %copy-start.18 = (f32[12,33]{1,0:T(8,128)S(1)}, f32[12,33]{1,0:T(8,128)}, u32[]{:S(2)}) copy-start(f32[12,33]{1,0:T(8,128)} %param.38) | copy-start | bytes 4756
  245.9 8.8 %copy-start.3 = (bf16[512,768]{1,0:T(8,128)(2,1)S(1)}, bf16[512,768]{1,0:T(8,128)(2,1)}, u32[]{:S(2)}) copy-start(bf16[512,768]{1,0:T(8,128)(2,1)} %get-tuple-element.76) | copy-start | bytes 2359300
